TPU v7x, 32 devices: a whole 2x2x4 slice. The times are simulated.
32 devices in a mesh: gx: 8 (over z, y), gy: 4 (over x, core).
Axes of the slice: x: 2, y: 2, z: 4, core: 2. Of those that a mesh axis runs over, the one named last changes fastest.
Arguments:
- hamiltonian: bfloat16 [32, 16, 64, 576], P('gx', 'gy'), as said below
- density: bfloat16 [32, 16, 64, 576], P('gx', 'gy'), as said below
- block_pattern: int32 [32, 16, 9], P('gx', 'gy'), may hold values from 0 to 1, as said below
- filter_mask: int32 [32, 16, 9], P('gx', 'gy'), may hold values from 0 to 1, as said below
Outputs:
- gradient: bfloat16 [32, 16, 64, 576], P('gx', 'gy')
Inputs may be any that keep to these rules, and one draw needn't show every extreme that they name: `block_pattern`: Symmetric: the value at block row i and slot k equals the value at block row i + s_k and slot 8 - k; the middle slot (k = 4) is always 1. `filter_mask`: Symmetric: the value at block row i and slot k equals the value at block row i + s_k and slot 8 - k; the middle slot (k = 4) is always 1. `hamiltonian`: A symmetric matrix: block (i, k) is the transpose of block (i + s_k, 8 - k), and every middle block (k = 4) is symmetric. `density`: A symmetric matrix: block (i, k) is the transpose of block (i + s_k, 8 - k), and every middle block (k = 4) is symmetric.
All inputs are finite; a program needn't handle non-finite values.
Results may differ from a plain program's by a relative error of at most 0.006.
Values may be sent and summed in bfloat16 or wider, within the bound.
No kernel may reach another device: no remote copies, remote signals or barrier semaphores. Data moves between devices by JAX's collectives and lax.ppermute only.
A program may use at most 192 MiB of HBM per device.

v0:
```python
import jax
import jax.numpy as jnp
import numpy as np
from jax import lax
from jax.sharding import PartitionSpec as P


def with_halo(block, sides, width):
    for axis, dim in sides:
        count = lax.axis_size(axis)
        forward = [(i, i + 1) for i in range(count - 1)]
        forward.append((count - 1, 0))
        backward = [(target, source) for source, target in forward]
        low = lax.ppermute(
            lax.slice_in_dim(block, block.shape[dim] - width, None, axis=dim), axis, forward
        )
        high = lax.ppermute(lax.slice_in_dim(block, 0, width, axis=dim), axis, backward)
        block = jnp.concatenate([low, block, high], axis=dim)
    return block


def slot_table():
    table = np.full((9, 9), 9, dtype=np.int32)
    for source in range(9):
        move_x = source // 3 - 1
        move_y = source % 3 - 1
        for target in range(9):
            rest_x = target // 3 - 1 - move_x
            rest_y = target % 3 - 1 - move_y
            if abs(rest_x) <= 1 and abs(rest_y) <= 1:
                table[source, target] = (rest_x + 1) * 3 + rest_y + 1
    return table


def block_mask(strips, mask, width):
    shape = strips.shape
    split = strips.reshape(shape[0], shape[1], width, 9, width)
    split = split * mask[:, :, None, :, None].astype(strips.dtype)
    return split.reshape(shape)


def stencil_product(left, right, margin, width):
    rows_x = left.shape[0]
    rows_y = left.shape[1]
    table = slot_table()
    stacked = []
    for source in range(9):
        move_x = source // 3 - 1
        move_y = source % 3 - 1
        moved = right[
            margin + move_x : margin + move_x + rows_x, margin + move_y : margin + move_y + rows_y
        ]
        split = moved.reshape(rows_x, rows_y, width, 9, width)
        padded = jnp.concatenate(
            [split, jnp.zeros((rows_x, rows_y, width, 1, width), split.dtype)], axis=3
        )
        stacked.append(jnp.take(padded, jnp.asarray(table[source]), axis=3))
    operand = jnp.stack(stacked, axis=2).reshape(rows_x, rows_y, 9 * width, 9 * width)
    return jnp.einsum("xyak,xykf->xyaf", left, operand, preferred_element_type=jnp.float32)


def transposed(padded, rows_x, rows_y, width):
    blocks = []
    for target in range(9):
        move_x = target // 3 - 1
        move_y = target % 3 - 1
        moved = padded[1 + move_x : 1 + move_x + rows_x, 1 + move_y : 1 + move_y + rows_y]
        blocks.append(moved[:, :, :, (8 - target) * width : (9 - target) * width])
    joined = jnp.stack(blocks, axis=3)
    return jnp.swapaxes(joined, 2, 4).reshape(rows_x, rows_y, width, 9 * width)


def per_device(hamiltonian, density, block_pattern, filter_mask):
    width = hamiltonian.shape[2]
    rows_x = hamiltonian.shape[0]
    rows_y = hamiltonian.shape[1]
    ham_masked = block_mask(hamiltonian, block_pattern, width)
    dens_masked = block_mask(density, block_pattern, width)
    depth = 1
    dens_pad = with_halo(dens_masked, (("gx", 0), ("gy", 1)), depth)
    hpp_pad = None
    hp = block_mask(stencil_product(ham_masked, dens_pad, 1, width), filter_mask, width).astype(
        jnp.bfloat16
    )
    hp_pad = with_halo(hp, (("gx", 0), ("gy", 1)), 1)
    hpp = block_mask(stencil_product(hp, dens_pad, 1, width), filter_mask, width).astype(
        jnp.bfloat16
    )
    php = block_mask(stencil_product(dens_masked, hp_pad, 1, width), filter_mask, width)
    hp_turned = transposed(hp_pad, rows_x, rows_y, width)
    hpp_pad = with_halo(hpp, (("gx", 0), ("gy", 1)), 1)
    hpp_turned = transposed(hpp_pad, rows_x, rows_y, width)
    linear = hp.astype(jnp.float32) + hp_turned.astype(jnp.float32)
    cubic = hpp.astype(jnp.float32) + php + hpp_turned.astype(jnp.float32)
    total = block_mask(3.0 * linear - 2.0 * cubic, filter_mask, width)
    return total.astype(jnp.bfloat16)


def solution(mesh):
    return jax.shard_map(
        per_device,
        mesh=mesh,
        in_specs=(
            P("gx", "gy", None, None),
            P("gx", "gy", None, None),
            P("gx", "gy", None),
            P("gx", "gy", None),
        ),
        out_specs=P("gx", "gy", None, None),
        check_vma=False,
    )
```

profile of v0, /device:TPU:0, one launch (start us, length us, event | category | flops | bytes accessed | tf_op | source)
XLA Modules:
  0.0 556.1 jit_solution(8246593637913454433)
XLA Ops:
  9.8 6.0 %collective-permute-start.1 = (bf16[1,4,64,576]{3,2,1,0:T(8,128)(2,1)}, bf16[1,4,64,576]{3,2,1,0:T(8,128)(2,1)S(1)}, u32[]{:S(2)}, u32[]{:S(2)}) collective-permute-start(bf16[1,4,64,576]{3,2,1,0:T(8,128)(2,1)} %copy.129), channel_id=1, source_target_pairs={{4,0},{8,4},{12,8},{16,12},{20,16},{24,20},{28,24},{0,28},{5,1},{9... | collective-permute-start | bytes 884744 | tf_op jit(solution)/shard_map/ppermute | solution.py:17
  17.5 5.6 collective-permute-done.1
  23.1 6.1 %collective-permute-done = bf16[1,4,64,576]{3,2,1,0:T(8,128)(2,1)S(1)} collective-permute-done((bf16[1,4,64,576]{3,2,1,0:T(8,128)(2,1)}, bf16[1,4,64,576]{3,2,1,0:T(8,128)(2,1)S(1)}, u32[]{:S(2)}, u32[]{:S(2)}) %collective-permute-start) | collective-permute-done | bytes 294944 | tf_op jit(solution)/shard_map/ppermute | solution.py:14
  42.7 4.3 copy.133
  53.6 4.3 copy.143
  66.1 4.2 gather_fusion.7
  144.8 4.3 gather_fusion.5
  164.8 25.1 %copy.146 = bf16[4,4,9,64,9,64]{5,4,3,2,1,0:T(8,128)(2,1)} copy(bf16[4,4,9,64,9,64]{5,3,1,0,4,2:T(8,128)(2,1)} %bitcast_dynamic-update-slice_fusion.9) | data formatting | bytes 21233664 | tf_op jit(solution)/shard_map/stack | solution.py:58
  189.9 42.4 %reshape.114 = bf16[4,4,576,576]{3,2,1,0:T(8,128)(2,1)} reshape(bf16[4,4,9,64,9,64]{5,4,3,2,1,0:T(8,128)(2,1)} %copy.146) | data formatting | bytes 21233664 | tf_op jit(solution)/shard_map/reshape | solution.py:58
  232.3 6.4 %multiply_convert_fusion.2 = (bf16[4,4,64,576]{3,2,1,0:T(8,128)(2,1)S(1)}, f32[4,4,64,576]{3,2,1,0:T(8,128)S(1)}) fusion(f32[4,4,576]{2,1,0:T(4,128)S(1)} %mul.78, bf16[4,4,576,576]{3,2,1,0:T(8,128)(2,1)} %reshape.114, bf16[4,4,64,576]{3,2,1,0:T(8,128)(2,1)S(1)} %copy-done.24, bf16[4,4,576]{2,1,0:T(4,128)(2,1)S(1)} %mul.71), kind=kOutput, calls=%fused_computation.22 | convolution fusion | flops 681246720 | bytes 15390720 | tf_op jit(solution)/shard_map/xyak,xykf->xyaf/dot_general | solution.py:59
  243.2 4.9 collective-permute-start.9
  249.0 4.7 collective-permute-start.5
  256.1 11.7 %collective-permute-done.8 = bf16[1,4,64,576]{3,2,1,0:T(8,128)(2,1)S(1)} collective-permute-done((bf16[1,4,64,576]{3,2,1,0:T(8,128)(2,1)S(1)}, bf16[1,4,64,576]{3,2,1,0:T(8,128)(2,1)S(1)}, u32[]{:S(2)}, u32[]{:S(2)}) %collective-permute-start.8) | collective-permute-done | bytes 294944 | tf_op jit(solution)/shard_map/ppermute | solution.py:14
  271.5 4.3 copy.158
  279.9 4.2 gather_fusion.13
  294.2 4.3 copy.152
  302.5 4.2 gather_fusion.10
  310.4 4.3 copy.164
  318.7 4.2 gather_fusion.16
  332.9 5.1 copy.169
  347.8 5.0 copy.148
  361.7 4.3 copy.150
  383.9 4.5 copy.154
  400.2 4.3 copy.156
  416.3 4.3 copy.160
  431.3 4.3 copy.162
  439.6 4.3 gather_fusion.15
  446.4 4.5 copy.166
  454.9 4.2 gather_fusion.17
  478.1 25.1 %copy.167 = bf16[4,4,9,64,9,64]{5,4,3,2,1,0:T(8,128)(2,1)} copy(bf16[4,4,9,64,9,64]{5,3,1,0,4,2:T(8,128)(2,1)} %bitcast_dynamic-update-slice_fusion) | data formatting | bytes 21233664 | tf_op jit(solution)/shard_map/stack | solution.py:58
  503.3 42.4 %reshape.125 = bf16[4,4,576,576]{3,2,1,0:T(8,128)(2,1)} reshape(bf16[4,4,9,64,9,64]{5,4,3,2,1,0:T(8,128)(2,1)} %copy.167) | data formatting | bytes 21233664 | tf_op jit(solution)/shard_map/reshape | solution.py:58
  545.6 10.2 %multiply_convert_fusion = bf16[4,4,64,576]{3,2,1,0:T(8,128)(2,1)} fusion(f32[4,4,64,576]{3,2,1,0:T(8,128)} %copy.169, bf16[4,4,64,576]{3,2,1,0:T(8,128)(2,1)S(1)} %multiply_convert_fusion.1, f32[4,4,64,576]{3,2,1,0:T(8,128)} %copy.148, f32[4,4,64,576]{3,2,1,0:T(8,128)} %copy-done.3, bf16[4,4,64,576]{3,2,1,0:T(8,128)(2,1)S(1)} %copy-done.2, ...), kind=kOutput, calls=%fused_computation.20 | convolution fusion | flops 687144960 | bytes 21270528 | tf_op jit(solution)/shard_map/xyak,xykf->xyaf/dot_general | solution.py:59
  (215 shorter events, 277.1 us)
Async XLA Ops:
  8.5 8.6 %copy-start.32 = (s32[9]{0:T(128)S(1)}, s32[9]{0:T(128)}, u32[]{:S(2)}) copy-start(s32[9]{0:T(128)} %constant.228) | copy-start | bytes 112
  8.5 8.6 %copy-start.34 = (s32[9]{0:T(128)S(1)}, s32[9]{0:T(128)}, u32[]{:S(2)}) copy-start(s32[9]{0:T(128)} %constant.227) | copy-start | bytes 112
  8.5 8.6 %copy-start.33 = (s32[9]{0:T(128)S(1)}, s32[9]{0:T(128)}, u32[]{:S(2)}) copy-start(s32[9]{0:T(128)} %constant.229) | copy-start | bytes 112
  8.5 8.6 %copy-start.31 = (s32[9]{0:T(128)S(1)}, s32[9]{0:T(128)}, u32[]{:S(2)}) copy-start(s32[9]{0:T(128)} %constant.226) | copy-start | bytes 112
  8.5 8.8 %copy-start.22 = (bf16[4,4,64,576]{3,2,1,0:T(8,128)(2,1)S(1)}, bf16[4,4,64,576]{3,2,1,0:T(8,128)(2,1)}, u32[]{:S(2)}) copy-start(bf16[4,4,64,576]{3,2,1,0:T(8,128)(2,1)} %param.34) | copy-start | bytes 3538948
  9.8 13.3 %collective-permute-start.1 = (bf16[1,4,64,576]{3,2,1,0:T(8,128)(2,1)}, bf16[1,4,64,576]{3,2,1,0:T(8,128)(2,1)S(1)}, u32[]{:S(2)}, u32[]{:S(2)}) collective-permute-start(bf16[1,4,64,576]{3,2,1,0:T(8,128)(2,1)} %copy.129), channel_id=1, source_target_pairs={{4,0},{8,4},{12,8},{16,12},{20,16},{24,20},{28,24},{0,28},{5,1},{9... | collective-permute-start | bytes 884744 | tf_op jit(solution)/shard_map/ppermute | solution.py:17
  17.1 12.1 %collective-permute-start = (bf16[1,4,64,576]{3,2,1,0:T(8,128)(2,1)}, bf16[1,4,64,576]{3,2,1,0:T(8,128)(2,1)S(1)}, u32[]{:S(2)}, u32[]{:S(2)}) collective-permute-start(bf16[1,4,64,576]{3,2,1,0:T(8,128)(2,1)} %copy.127), channel_id=1, source_target_pairs={{0,4},{4,8},{8,12},{12,16},{16,20},{20,24},{24,28},{28,0},{1,5},{5... | collective-permute-start | bytes 884744 | tf_op jit(solution)/shard_map/ppermute | solution.py:14
  17.4 13.5 %copy-start.21 = (bf16[4,4,64,9,64]{4,2,3,1,0:T(8,128)(2,1)S(1)}, bf16[4,4,64,9,64]{4,2,3,1,0:T(8,128)(2,1)}, u32[]{:S(2)}) copy-start(bf16[4,4,64,9,64]{4,2,3,1,0:T(8,128)(2,1)} %copy-done.20) | copy-start | bytes 3538948
  17.5 52.8 %copy-start.1 = (bf16[4,4,64,576]{3,2,1,0:T(8,128)(2,1)}, bf16[4,4,64,576]{3,2,1,0:T(8,128)(2,1)S(1)}, u32[]{:S(2)}) copy-start(bf16[4,4,64,576]{3,2,1,0:T(8,128)(2,1)S(1)} %broadcast_multiply_fusion.1) | copy-start | bytes 3538948
  30.3 40.0 %collective-permute-start.3 = (bf16[6,1,64,576]{3,2,1,0:T(8,128)(2,1)}, bf16[6,1,64,576]{3,2,1,0:T(8,128)(2,1)}, u32[]{:S(2)}, u32[]{:S(2)}) collective-permute-start(bf16[6,1,64,576]{3,2,1,0:T(8,128)(2,1)} %get-tuple-element.28), channel_id=1, source_target_pairs={{1,0},{2,1},{3,2},{0,3},{5,4},{6,5},{7,6},{4,7},{9,8},{10,9},{11,1... | collective-permute-start | bytes 1327112 | tf_op jit(solution)/shard_map/ppermute | solution.py:17
  30.3 40.0 %collective-permute-start.2 = (bf16[6,1,64,576]{3,2,1,0:T(8,128)(2,1)}, bf16[6,1,64,576]{3,2,1,0:T(8,128)(2,1)}, u32[]{:S(2)}, u32[]{:S(2)}) collective-permute-start(bf16[6,1,64,576]{3,2,1,0:T(8,128)(2,1)} %get-tuple-element.29), channel_id=1, source_target_pairs={{0,1},{1,2},{2,3},{3,0},{4,5},{5,6},{6,7},{7,4},{8,9},{9,10},{10,1... | collective-permute-start | bytes 1327112 | tf_op jit(solution)/shard_map/ppermute | solution.py:14
  33.2 4.2 copy-start.29
  33.2 4.2 copy-start.30
  33.3 4.2 copy-start.27
  33.3 4.2 copy-start.28
  144.8 4.4 copy-start.10
  189.9 42.4 %copy-start.24 = (bf16[4,4,64,576]{3,2,1,0:T(8,128)(2,1)S(1)}, bf16[4,4,64,576]{3,2,1,0:T(8,128)(2,1)}, u32[]{:S(2)}) copy-start(bf16[4,4,64,576]{3,2,1,0:T(8,128)(2,1)} %param.33) | copy-start | bytes 3538948
  232.3 8.7 %copy-start = (bf16[4,4,576,576]{3,2,1,0:T(8,128)(2,1)S(1)}, bf16[4,4,576,576]{3,2,1,0:T(8,128)(2,1)}, u32[]{:S(2)}) copy-start(bf16[4,4,576,576]{3,2,1,0:T(8,128)(2,1)} %reshape.114) | copy-start | bytes 31850500
  238.6 4.5 copy-start.3
  243.2 12.8 %collective-permute-start.9 = (bf16[1,4,64,576]{3,2,1,0:T(8,128)(2,1)S(1)}, bf16[1,4,64,576]{3,2,1,0:T(8,128)(2,1)S(1)}, u32[]{:S(2)}, u32[]{:S(2)}) collective-permute-start(bf16[1,4,64,576]{3,2,1,0:T(8,128)(2,1)S(1)} %get-tuple-element.35), channel_id=1, source_target_pairs={{4,0},{8,4},{12,8},{16,12},{20,16},{24,20},{28,24},{0,28},{5,1},{9... | collective-permute-start | bytes 884744 | tf_op jit(solution)/shard_map/ppermute | solution.py:17
  248.1 19.7 %collective-permute-start.8 = (bf16[1,4,64,576]{3,2,1,0:T(8,128)(2,1)S(1)}, bf16[1,4,64,576]{3,2,1,0:T(8,128)(2,1)S(1)}, u32[]{:S(2)}, u32[]{:S(2)}) collective-permute-start(bf16[1,4,64,576]{3,2,1,0:T(8,128)(2,1)S(1)} %get-tuple-element.34), channel_id=1, source_target_pairs={{0,4},{4,8},{8,12},{12,16},{16,20},{20,24},{24,28},{28,0},{1,5},{5... | collective-permute-start | bytes 884744 | tf_op jit(solution)/shard_map/ppermute | solution.py:14
  249.0 36.7 %collective-permute-start.5 = (bf16[1,4,64,576]{3,2,1,0:T(8,128)(2,1)}, bf16[1,4,64,576]{3,2,1,0:T(8,128)(2,1)S(1)}, u32[]{:S(2)}, u32[]{:S(2)}) collective-permute-start(bf16[1,4,64,576]{3,2,1,0:T(8,128)(2,1)} %get-tuple-element.33), channel_id=1, source_target_pairs={{4,0},{8,4},{12,8},{16,12},{20,16},{24,20},{28,24},{0,28},{5,1},{9... | collective-permute-start | bytes 884744 | tf_op jit(solution)/shard_map/ppermute | solution.py:17
  253.7 32.0 %collective-permute-start.4 = (bf16[1,4,64,576]{3,2,1,0:T(8,128)(2,1)}, bf16[1,4,64,576]{3,2,1,0:T(8,128)(2,1)S(1)}, u32[]{:S(2)}, u32[]{:S(2)}) collective-permute-start(bf16[1,4,64,576]{3,2,1,0:T(8,128)(2,1)} %get-tuple-element.32), channel_id=1, source_target_pairs={{0,4},{4,8},{8,12},{12,16},{16,20},{20,24},{24,28},{28,0},{1,5},{5... | collective-permute-start | bytes 884744 | tf_op jit(solution)/shard_map/ppermute | solution.py:14
  256.0 11.7 %copy-start.4 = (bf16[1,4,64,576]{3,2,1,0:T(8,128)(2,1)}, bf16[1,4,64,576]{3,2,1,0:T(8,128)(2,1)S(1)}, u32[]{:S(2)}) copy-start(bf16[1,4,64,576]{3,2,1,0:T(8,128)(2,1)S(1)} %collective-permute-done.9) | copy-start | bytes 884740
  268.9 54.0 %collective-permute-start.10 = (bf16[6,1,64,576]{3,2,1,0:T(8,128)(2,1)}, bf16[6,1,64,576]{3,2,1,0:T(8,128)(2,1)}, u32[]{:S(2)}, u32[]{:S(2)}) collective-permute-start(bf16[6,1,64,576]{3,2,1,0:T(8,128)(2,1)} %get-tuple-element.25), channel_id=1, source_target_pairs={{0,1},{1,2},{2,3},{3,0},{4,5},{5,6},{6,7},{7,4},{8,9},{9,10},{10,1... | collective-permute-start | bytes 1327112 | tf_op jit(solution)/shard_map/ppermute | solution.py:14
  284.0 40.1 %collective-permute-start.11 = (bf16[6,1,64,576]{3,2,1,0:T(8,128)(2,1)}, bf16[6,1,64,576]{3,2,1,0:T(8,128)(2,1)}, u32[]{:S(2)}, u32[]{:S(2)}) collective-permute-start(bf16[6,1,64,576]{3,2,1,0:T(8,128)(2,1)} %get-tuple-element.24), channel_id=1, source_target_pairs={{1,0},{2,1},{3,2},{0,3},{5,4},{6,5},{7,6},{4,7},{9,8},{10,9},{11,1... | collective-permute-start | bytes 1327112 | tf_op jit(solution)/shard_map/ppermute | solution.py:17
  286.8 51.2 %collective-permute-start.6 = (bf16[6,1,64,576]{3,2,1,0:T(8,128)(2,1)}, bf16[6,1,64,576]{3,2,1,0:T(8,128)(2,1)}, u32[]{:S(2)}, u32[]{:S(2)}) collective-permute-start(bf16[6,1,64,576]{3,2,1,0:T(8,128)(2,1)} %get-tuple-element.23), channel_id=1, source_target_pairs={{0,1},{1,2},{2,3},{3,0},{4,5},{5,6},{6,7},{7,4},{8,9},{9,10},{10,1... | collective-permute-start | bytes 1327112 | tf_op jit(solution)/shard_map/ppermute | solution.py:14
  287.5 51.6 %collective-permute-start.7 = (bf16[6,1,64,576]{3,2,1,0:T(8,128)(2,1)}, bf16[6,1,64,576]{3,2,1,0:T(8,128)(2,1)}, u32[]{:S(2)}, u32[]{:S(2)}) collective-permute-start(bf16[6,1,64,576]{3,2,1,0:T(8,128)(2,1)} %get-tuple-element.22), channel_id=1, source_target_pairs={{1,0},{2,1},{3,2},{0,3},{5,4},{6,5},{7,6},{4,7},{9,8},{10,9},{11,1... | collective-permute-start | bytes 1327112 | tf_op jit(solution)/shard_map/ppermute | solution.py:17
  374.2 4.0 copy-start.19
  439.6 4.3 copy-start.23
  459.2 4.0 copy-start.13
  503.3 42.4 %copy-start.2 = (bf16[4,4,64,576]{3,2,1,0:T(8,128)(2,1)S(1)}, bf16[4,4,64,576]{3,2,1,0:T(8,128)(2,1)}, u32[]{:S(2)}) copy-start(bf16[4,4,64,576]{3,2,1,0:T(8,128)(2,1)} %copy-done.1) | copy-start | bytes 3538948
  (15 other events, 29.7 us)
where the time goes:
time: 566 us; the launch traced here: 556 us
  local copies, waits for them, and re-layouts  461 us (81%)
  other arithmetic  30.4 us (5%)
  waiting for transfers between devices  25.7 us (5%)
  starting transfers between devices  19.6 us (3%)
  matrix products  18.7 us (3%)
    reshape x2, local copies, waits for them, and re-layouts, stencil_product(): jnp.stack(stacked, axis=2).reshape(rows_x, rows_y, 9 * width, 9 * width)  84.7 us
    gather x18, local copies, waits for them, and re-layouts, stencil_product(): stacked.append(jnp.take(padded, jnp.asarray(table[source]), axis=3))  68.3 us
    reshape x17, local copies, waits for them, and re-layouts, stencil_product(): split = moved.reshape(rows_x, rows_y, width, 9, width)  65.9 us
    concatenate x18, local copies, waits for them, and re-layouts, stencil_product(): jnp.concatenate([split, jnp.zeros((rows_x, rows_y, width, 1, width), spli...  60.3 us
    another operation x4, local copies, waits for them, and re-layouts, stencil_product(): jnp.stack(stacked, axis=2).reshape(rows_x, rows_y, 9 * width, 9 * width)  54.3 us
    unnamed x87, local copies, waits for them, and re-layouts  40.3 us
    slice x10, local copies, waits for them, and re-layouts, transposed(): padded[1 + move_x:1 + move_x + rows_x, 1 + move_y:1 + move_y + rows_y]  31.2 us
    slice x9, local copies, waits for them, and re-layouts, stencil_product(): right[margin + move_x:margin + move_x + rows_x, margin + move_y:margin +...  30.3 us
  transfers between devices with their start and end apart: 12, of which 4 were waited for; matrix products, arithmetic and copies ran while one was open for 20% of the time, Pallas kernels for 0%

commit v1 on v0

v1 whole, which is shorter than its diff:
```python
import functools

import jax
import jax.numpy as jnp
from jax import lax
from jax.experimental import pallas as pl
from jax.experimental.pallas import tpu as pltpu
from jax.sharding import PartitionSpec as P

W = 64
BF = jnp.bfloat16
F32 = jnp.float32
VMEM = pl.BlockSpec(memory_space=pltpu.VMEM)


def strip_mask(mask_ref, x):
    slot = lax.broadcasted_iota(jnp.int32, (9, 9 * W), 0)
    lane = lax.broadcasted_iota(jnp.int32, (9, 9 * W), 1)
    spread = (lane // W == slot).astype(BF)
    flags = mask_ref[x].astype(F32).astype(BF)
    return jnp.dot(flags, spread, preferred_element_type=F32)


def window_mask(mask_ref, x):
    slot = lax.broadcasted_iota(jnp.int32, (9, 12 * W), 0)
    lane = lax.broadcasted_iota(jnp.int32, (9, 12 * W), 1)
    flags = mask_ref[x].astype(F32).astype(BF)
    out = []
    for r in range(2):
        dy = (lane % 256) // W - r
        inside = (dy >= 0) & (dy <= 2) & (lane // 256 * 3 + dy == slot)
        out.append(jnp.dot(flags, inside.astype(BF), preferred_element_type=F32))
    return out


def put_strip(dst, x, y, strip):
    p, r = y // 2, y % 2
    for d in range(3):
        piece = strip[:, 192 * d : 192 * d + 192]
        zero = jnp.zeros((W, W), BF)
        parts = [piece, zero] if r == 0 else [zero, piece]
        dst[p, x + 1, W + W * r : 2 * W + W * r, 256 * d : 256 * d + 256] = jnp.concatenate(
            parts, axis=1
        )


def put_shared(dst, x):
    zero = jnp.zeros((W, 128), BF)
    for d in range(3):
        c = 256 * d
        dst[1, x + 1, 0:64, c : c + 128] = dst[0, x + 1, 128:192, c + 128 : c + 256]
        dst[1, x + 1, 0:64, c + 128 : c + 256] = zero
        dst[0, x + 1, 192:256, c + 128 : c + 256] = dst[1, x + 1, 64:128, c : c + 128]
        dst[0, x + 1, 192:256, c : c + 128] = zero


def put_y(dst, x, low, high):
    zero = jnp.zeros((W, 128), BF)
    for d in range(3):
        c = 256 * d
        dst[0, x + 1, 0:64, c : c + 128] = low[:, 128 * d : 128 * d + 128]
        dst[0, x + 1, 0:64, c + 128 : c + 256] = zero
        dst[1, x + 1, 192:256, c + 128 : c + 256] = high[:, 128 * d : 128 * d + 128]
        dst[1, x + 1, 192:256, c : c + 128] = zero


def put_x(dst, at, row, corner):
    z1 = jnp.zeros((W, W), BF)
    z2 = jnp.zeros((W, 128), BF)
    cell = []
    for y in range(4):
        first = row[y]
        last = row[4 + y // 2][:, W * (y % 2) : W * (y % 2) + W]
        cell.append(jnp.concatenate([first, last], axis=1))
    for p in range(2):
        a = corner[0] if p == 0 else cell[1][:, W:]
        d = corner[1] if p == 1 else cell[2][:, :128]
        tile = jnp.concatenate(
            [
                jnp.concatenate([a, z2], axis=1),
                jnp.concatenate([cell[2 * p], z1], axis=1),
                jnp.concatenate([z1, cell[2 * p + 1]], axis=1),
                jnp.concatenate([z2, d], axis=1),
            ],
            axis=0,
        )
        dst[p, at, :, 256:512] = tile
        if at == 0:
            dst[p, 0, :, 512:768] = dst[p, 1, :, 0:256].T
        else:
            dst[p, at, :, 0:256] = dst[p, at - 1, :, 512:768].T


def x_message(cells):
    out = [c[:, :128] for c in cells]
    out.append(jnp.concatenate([cells[0][:, 128:], cells[1][:, 128:]], axis=1))
    out.append(jnp.concatenate([cells[2][:, 128:], cells[3][:, 128:]], axis=1))
    return jnp.stack(out)


def pack_kernel(ham, dens, pattern, y_up, y_down, x_up, x_down):
    for x in range(4):
        mask = strip_mask(pattern, x).astype(BF)
        for n, ref in enumerate((ham, dens)):
            low = ref[x, 0] * mask[0:1]
            high = ref[x, 3] * mask[3:4]
            y_down[n, x] = jnp.concatenate([low[:, 192 * d : 192 * d + 128] for d in range(3)], axis=1)
            y_up[n, x] = jnp.concatenate(
                [high[:, 192 * d + 64 : 192 * d + 192] for d in range(3)], axis=1
            )
            if x in (0, 3):
                cells = [(ref[x, y] * mask[y : y + 1])[:, 192:384] for y in range(4)]
                out = x_down if x == 0 else x_up
                out[n] = x_message(cells)


def dense_product(left, right, p, x, e):
    total = None
    for d in range(max(-1, e - 1), min(1, e + 1) + 1):
        term = jnp.dot(
            left[:, 256 * (d + 1) : 256 * (d + 2)],
            right[p, x + 1 + d, :, 256 * (e - d + 1) : 256 * (e - d + 2)],
            preferred_element_type=F32,
        )
        total = term if total is None else total + term
    return total


def both_rows(masks, p):
    first, second = masks
    return jnp.concatenate(
        [
            jnp.broadcast_to(first[2 * p : 2 * p + 1], (W, 768)),
            jnp.broadcast_to(second[2 * p + 1 : 2 * p + 2], (W, 768)),
        ],
        axis=0,
    )


def first_kernel(
    ham, dens, pattern, kept, y_low, y_high, x_low, x_high, c_low, c_high,
    a_out, s_out, xd, sy_up, sy_down, sx_up, sx_down, xh,
):
    for n, (ref, dst) in enumerate(((ham, xh), (dens, xd))):
        for x in range(4):
            mask = strip_mask(pattern, x).astype(BF)
            for y in range(4):
                put_strip(dst, x, y, ref[x, y] * mask[y : y + 1])
            put_shared(dst, x)
            put_y(dst, x, y_low[n, x], y_high[n, x])
        put_x(dst, 0, x_low[n], c_low[n])
        put_x(dst, 5, x_high[n], c_high[n])
    for x in range(4):
        masks = window_mask(kept, x)
        for p in range(2):
            keep = both_rows(masks, p)
            lh = xh[p, x + 1, 64:192, :]
            ld = xd[p, x + 1, 64:192, :]
            for e in range(-1, 2):
                cols = slice(256 * (e + 1), 256 * (e + 2))
                a = (dense_product(lh, xd, p, x, e) * keep[:, cols]).astype(BF)
                b = (dense_product(ld, xh, p, x, e) * keep[:, cols]).astype(BF)
                a_out[p, x, :, cols] = a
                s_out[p, x, :, cols] = (a.astype(F32) + b.astype(F32)).astype(BF)
        for d in range(3):
            sy_up[x, :, 128 * d : 128 * d + 128] = s_out[1, x, 64:128, 256 * d + 128 : 256 * d + 256]
            sy_down[x, :, 128 * d : 128 * d + 128] = s_out[0, x, 0:64, 256 * d : 256 * d + 128]
    for x, out in ((0, sx_down), (3, sx_up)):
        out[...] = x_message(
            [
                s_out[y // 2, x, W * (y % 2) : W * (y % 2) + W, 256 + W * (y % 2) : 448 + W * (y % 2)]
                for y in range(4)
            ]
        )


def last_kernel(
    a_in, s_in, xd, kept, y_low, y_high, x_low, x_high, c_low, c_high, out, xs
):
    for x in range(4):
        for p in range(2):
            xs[p, x + 1, 64:192, :] = s_in[p, x]
        put_shared(xs, x)
        put_y(xs, x, y_low[x], y_high[x])
    put_x(xs, 0, x_low, c_low)
    put_x(xs, 5, x_high, c_high)
    for x in range(4):
        masks = window_mask(kept, x)
        for p in range(2):
            keep = both_rows(masks, p)
            la = a_in[p, x]
            ld = xd[p, x + 1, 64:192, :]
            for e in range(-1, 2):
                cols = slice(256 * (e + 1), 256 * (e + 2))
                cubic = dense_product(la, xd, p, x, e) + dense_product(ld, xs, p, x, e)
                linear = s_in[p, x, :, cols].astype(F32)
                total = ((3.0 * linear - 2.0 * cubic) * keep[:, cols]).astype(BF)
                first = slice(192 * (e + 1), 192 * (e + 2))
                out[x, 2 * p, :, first] = total[0:64, 0:192]
                out[x, 2 * p + 1, :, first] = total[64:128, 64:256]


def call(kernel, outs, scratch=()):
    return pl.pallas_call(
        kernel,
        out_shape=[jax.ShapeDtypeStruct(s, BF) for s in outs],
        out_specs=[VMEM] * len(outs),
        scratch_shapes=[pltpu.VMEM(s, BF) for s in scratch],
        compiler_params=pltpu.CompilerParams(vmem_limit_bytes=48 * 1024 * 1024),
    )


def shift(value, axis, step):
    count = lax.axis_size(axis)
    return lax.ppermute(value, axis, [(i, (i + step) % count) for i in range(count)])


def corners(low, high, x):
    return jnp.stack([low[:, x, :, 128:256], high[:, x, :, 128:256]], axis=1)


def exchange(y_up, y_down, x_up, x_down):
    y_low = shift(y_up, "gy", 1)
    y_high = shift(y_down, "gy", -1)
    x_low = shift(x_up, "gx", 1)
    x_high = shift(x_down, "gx", -1)
    c_low = shift(corners(y_low, y_high, 3), "gx", 1)
    c_high = shift(corners(y_low, y_high, 0), "gx", -1)
    return y_low, y_high, x_low, x_high, c_low, c_high


def per_device(ham, dens, pattern, kept):
    ym, xm = (4, W, 384), (6, W, 128)
    msg = call(pack_kernel, [(2,) + ym, (2,) + ym, (2,) + xm, (2,) + xm])(ham, dens, pattern)
    halo = exchange(*msg)
    dense = (2, 6, 256, 768)
    rows = (2, 4, 128, 768)
    a, s, xd, *msg = call(first_kernel, [rows, rows, dense, ym, ym, xm, xm], [dense])(
        ham, dens, pattern, kept, *halo
    )
    halo = exchange(*[m[None] for m in msg])
    return call(last_kernel, [ham.shape], [dense])(a, s, xd, kept, *[h[0] for h in halo])[0]


def solution(mesh):
    return jax.shard_map(
        per_device,
        mesh=mesh,
        in_specs=(
            P("gx", "gy", None, None),
            P("gx", "gy", None, None),
            P("gx", "gy", None),
            P("gx", "gy", None),
        ),
        out_specs=P("gx", "gy", None, None),
        check_vma=False,
    )
```

time: 566 us -> 53.6 us (0.09); the launches traced: 556 us -> 53 us
  local copies, waits for them, and re-layouts: 461 us -> 4.77 us
  other arithmetic: 30.4 us -> 0.03 us
  matrix products: 18.7 us -> 0 us
  waiting for transfers between devices: 25.7 us -> 12.2 us
  Pallas kernels: 0 us -> 12.4 us
    reshape x20 -> x0, local copies, waits for them, and re-layouts: 154 us -> none  [the longest x2 84.7 us: stencil_product(): jnp.stack(stacked, axis=2).reshape(rows_x, rows_y, 9 * width, 9 * width)]
    gather x18 -> x0, local copies, waits for them, and re-layouts: 68.3 us -> none  [stencil_product(): stacked.append(jnp.take(padded, jnp.asarray(table[source]), axis=3))]
    slice x26 -> x4, local copies, waits for them, and re-layouts: 65.1 us -> 0.03 us  [corners(): return jnp.stack([low[:, x, :, 128:256], high[:, x, :, 128:256]], axis=1)]
    concatenate x18 -> x0, local copies, waits for them, and re-layouts: 60.3 us -> none  [stencil_product(): jnp.concatenate([split, jnp.zeros((rows_x, rows_y, width, 1, width), spli...]
    another operation x5 -> x0, local copies, waits for them, and re-layouts: 54.3 us -> none  [the longest x4 54.3 us: stencil_product(): jnp.stack(stacked, axis=2).reshape(rows_x, rows_y, 9 * width, 9 * width)]
    unnamed x87 -> x10, local copies, waits for them, and re-layouts: 40.3 us -> 4.74 us
    dot_general x3 -> x0, matrix products: 18.7 us -> none  [stencil_product(): jnp.einsum('xyak,xykf->xyaf', left, operand, preferred_element_type=jnp.f...]
    convert_element_type x5 -> x0, local copies, waits for them, and re-layouts: 18.4 us -> none  [the longest x2 7.98 us: per_device(): cubic = hpp.astype(jnp.float32) + php + hpp_turned.astype(jnp.float32)]
  transfers between devices with their start and end apart: 12 -> 12, of which waited for: 4 -> 6; matrix products, arithmetic and copies ran while one was open for 20% -> 0% of each run, Pallas kernels for 0% -> 0%
where the time goes in v1:
time: 53.6 us; the launch traced here: 53 us
  starting transfers between devices  23.5 us (44%)
  Pallas kernels  12.4 us (23%)
  waiting for transfers between devices  12.2 us (23%)
  local copies, waits for them, and re-layouts  4.77 us (9%)
    ppermute x12, starting transfers between devices, shift(): lax.ppermute(value, axis, [(i, (i + step) % count) for i in range(count)])  23.5 us
    ppermute x12, waiting for transfers between devices, shift(): lax.ppermute(value, axis, [(i, (i + step) % count) for i in range(count)])  12.2 us
    pallas_call x1, Pallas kernels, per_device(): call(last_kernel, [ham.shape], [dense])  6.12 us
    pallas_call x1, Pallas kernels, per_device(): call(first_kernel, [rows, rows, dense, ym, ym, xm, xm], [dense])  5.57 us
    unnamed x10, local copies, waits for them, and re-layouts  4.74 us
  transfers between devices with their start and end apart: 12, of which 6 were waited for; matrix products, arithmetic and copies ran while one was open for 0% of the time, Pallas kernels for 0%

profile of v1, /device:TPU:0, one launch (start us, length us, event | category | flops | bytes accessed | tf_op | source)
XLA Modules:
  0.0 53.0 jit_solution(14884967543019578917)
XLA Ops:
  0.0 1.3 %copy-done = bf16[4,4,64,576]{3,2,1,0:T(8,128)(2,1)S(1)} copy-done((bf16[4,4,64,576]{3,2,1,0:T(8,128)(2,1)S(1)}, bf16[4,4,64,576]{3,2,1,0:T(8,128)(2,1)}, u32[]{:S(2)}) %copy-start) | copy-done | bytes 1179672
  1.3 1.3 %copy-done.1 = bf16[4,4,64,576]{3,2,1,0:T(8,128)(2,1)S(1)} copy-done((bf16[4,4,64,576]{3,2,1,0:T(8,128)(2,1)S(1)}, bf16[4,4,64,576]{3,2,1,0:T(8,128)(2,1)}, u32[]{:S(2)}) %copy-start.1) | copy-done | bytes 1179672
  2.6 0.7 %copy-done.3 = s32[4,4,9]{2,1,0:T(4,128)S(1)} copy-done((s32[4,4,9]{2,1,0:T(4,128)S(1)}, s32[4,4,9]{2,1,0:T(4,128)}, u32[]{:S(2)}) %copy-start.3) | copy-done | bytes 600
  3.3 0.7 %shard_map.46 = (bf16[2,4,64,384]{3,2,1,0:T(8,128)(2,1)S(1)}, bf16[2,4,64,384]{3,2,1,0:T(8,128)(2,1)S(1)}, bf16[2,6,64,128]{3,2,1,0:T(8,128)(2,1)S(1)}, bf16[2,6,64,128]{3,2,1,0:T(8,128)(2,1)S(1)}) custom-call(bf16[4,4,64,576]{3,2,1,0:T(8,128)(2,1)S(1)} %copy-done, bf16[4,4,64,576]{3,2,1,0:T(8,128)(2,1)S(1)} %copy-done.1, s32[4,4,9]{2,1,0:T(4,128)S(1)} %copy-done.3), custom_call_target="tpu_custom_call" | custom-call | tf_op jit(solution)/shard_map/pallas_call | solution.py:234
  4.0 0.5 collective-permute-start
  4.5 2.0 %collective-permute-start.1 = (bf16[2,4,64,384]{3,2,1,0:T(8,128)(2,1)S(1)}, bf16[2,4,64,384]{3,2,1,0:T(8,128)(2,1)S(1)}, u32[]{:S(2)}, u32[]{:S(2)}) collective-permute-start(bf16[2,4,64,384]{3,2,1,0:T(8,128)(2,1)S(1)} %get-tuple-element.17), channel_id=1, source_target_pairs={{0,3},{1,0},{2,1},{3,2},{4,7},{5,4},{6,5},{7,6},{8,11},{9,8},{10,9... | collective-permute-start | bytes 1179656 | tf_op jit(solution)/shard_map/ppermute | solution.py:215
  6.5 2.3 %collective-permute-start.2 = (bf16[2,6,64,128]{3,2,1,0:T(8,128)(2,1)S(1)}, bf16[2,6,64,128]{3,2,1,0:T(8,128)(2,1)S(1)}, u32[]{:S(2)}, u32[]{:S(2)}) collective-permute-start(bf16[2,6,64,128]{3,2,1,0:T(8,128)(2,1)S(1)} %get-tuple-element.18), channel_id=1, source_target_pairs={{0,4},{4,8},{8,12},{12,16},{16,20},{20,24},{24,28},{28,0},{1,5},{5... | collective-permute-start | bytes 589832 | tf_op jit(solution)/shard_map/ppermute | solution.py:215
  8.8 3.0 %collective-permute-start.3 = (bf16[2,6,64,128]{3,2,1,0:T(8,128)(2,1)S(1)}, bf16[2,6,64,128]{3,2,1,0:T(8,128)(2,1)S(1)}, u32[]{:S(2)}, u32[]{:S(2)}) collective-permute-start(bf16[2,6,64,128]{3,2,1,0:T(8,128)(2,1)S(1)} %get-tuple-element.19), channel_id=1, source_target_pairs={{0,28},{4,0},{8,4},{12,8},{16,12},{20,16},{24,20},{28,24},{1,29},{... | collective-permute-start | bytes 589832 | tf_op jit(solution)/shard_map/ppermute | solution.py:215
  11.8 1.6 %collective-permute-done.y_low = bf16[2,4,64,384]{3,2,1,0:T(8,128)(2,1)S(1)} collective-permute-done((bf16[2,4,64,384]{3,2,1,0:T(8,128)(2,1)S(1)}, bf16[2,4,64,384]{3,2,1,0:T(8,128)(2,1)S(1)}, u32[]{:S(2)}, u32[]{:S(2)}) %collective-permute-start) | collective-permute-done | bytes 393248 | tf_op jit(solution)/shard_map/ppermute | solution.py:215
  13.5 2.5 %collective-permute-done.1.y_high = bf16[2,4,64,384]{3,2,1,0:T(8,128)(2,1)S(1)} collective-permute-done((bf16[2,4,64,384]{3,2,1,0:T(8,128)(2,1)S(1)}, bf16[2,4,64,384]{3,2,1,0:T(8,128)(2,1)S(1)}, u32[]{:S(2)}, u32[]{:S(2)}) %collective-permute-start.1) | collective-permute-done | bytes 393248 | tf_op jit(solution)/shard_map/ppermute | solution.py:215
  16.0 1.6 %collective-permute-start.4 = (bf16[2,2,64,128]{3,2,1,0:T(8,128)(2,1)S(1)}, bf16[2,2,64,128]{3,2,1,0:T(8,128)(2,1)S(1)}, u32[]{:S(2)}, u32[]{:S(2)}) collective-permute-start(bf16[2,2,64,128]{3,2,1,0:T(8,128)(2,1)S(1)} %pad_maximum_fusion), channel_id=1, source_target_pairs={{0,4},{4,8},{8,12},{12,16},{16,20},{20,24},{24,28},{28,0},{1,5},{5... | collective-permute-start | bytes 196616 | tf_op jit(solution)/shard_map/ppermute | solution.py:215
  17.6 3.3 %collective-permute-start.5 = (bf16[2,2,64,128]{3,2,1,0:T(8,128)(2,1)S(1)}, bf16[2,2,64,128]{3,2,1,0:T(8,128)(2,1)S(1)}, u32[]{:S(2)}, u32[]{:S(2)}) collective-permute-start(bf16[2,2,64,128]{3,2,1,0:T(8,128)(2,1)S(1)} %pad_maximum_fusion.1), channel_id=1, source_target_pairs={{0,28},{4,0},{8,4},{12,8},{16,12},{20,16},{24,20},{28,24},{1,29},{... | collective-permute-start | bytes 196616 | tf_op jit(solution)/shard_map/ppermute | solution.py:215
  20.8 0.0 collective-permute-done.2.x_low
  20.8 0.0 collective-permute-done.3.x_high
  20.8 2.7 %collective-permute-done.4.c_low = bf16[2,2,64,128]{3,2,1,0:T(8,128)(2,1)S(1)} collective-permute-done((bf16[2,2,64,128]{3,2,1,0:T(8,128)(2,1)S(1)}, bf16[2,2,64,128]{3,2,1,0:T(8,128)(2,1)S(1)}, u32[]{:S(2)}, u32[]{:S(2)}) %collective-permute-start.4) | collective-permute-done | bytes 65568 | tf_op jit(solution)/shard_map/ppermute | solution.py:215
  23.6 0.3 collective-permute-done.5.c_high
  23.9 0.0 copy-done.4
  23.9 5.6 %shard_map.47 = (bf16[2,4,128,768]{3,2,1,0:T(8,128)(2,1)S(1)}, bf16[2,4,128,768]{3,2,1,0:T(8,128)(2,1)}, bf16[2,6,256,768]{3,2,1,0:T(8,128)(2,1)}, bf16[4,64,384...) custom-call(bf16[4,4,64,576]{3,2,1,0:T(8,128)(2,1)S(1)} %copy-done, ...), custom_call_target="tpu_custom_call" | custom-call | tf_op jit(solution)/shard_map/pallas_call | solution.py:238
  29.4 0.0 collective-permute-start.6
  29.4 1.0 %collective-permute-start.8 = (bf16[1,6,64,128]{3,2,1,0:T(8,128)(2,1)S(1)}, bf16[1,6,64,128]{3,2,1,0:T(8,128)(2,1)S(1)}, u32[]{:S(2)}, u32[]{:S(2)}) collective-permute-start(bf16[1,6,64,128]{3,2,1,0:T(8,128)(2,1)S(1)} %bitcast.19), channel_id=1, source_target_pairs={{0,4},{4,8},{8,12},{12,16},{16,20},{20,24},{24,28},{28,0},{1,5},{5... | collective-permute-start | bytes 294920 | tf_op jit(solution)/shard_map/ppermute | solution.py:215
  30.5 3.7 %collective-permute-start.9 = (bf16[1,6,64,128]{3,2,1,0:T(8,128)(2,1)S(1)}, bf16[1,6,64,128]{3,2,1,0:T(8,128)(2,1)S(1)}, u32[]{:S(2)}, u32[]{:S(2)}) collective-permute-start(bf16[1,6,64,128]{3,2,1,0:T(8,128)(2,1)S(1)} %bitcast.18), channel_id=1, source_target_pairs={{0,28},{4,0},{8,4},{12,8},{16,12},{20,16},{24,20},{28,24},{1,29},{... | collective-permute-start | bytes 294920 | tf_op jit(solution)/shard_map/ppermute | solution.py:215
  34.2 1.4 %collective-permute-start.7 = (bf16[1,4,64,384]{3,2,1,0:T(8,128)(2,1)S(1)}, bf16[1,4,64,384]{3,2,1,0:T(8,128)(2,1)S(1)}, u32[]{:S(2)}, u32[]{:S(2)}) collective-permute-start(bf16[1,4,64,384]{3,2,1,0:T(8,128)(2,1)S(1)} %bitcast.16), channel_id=1, source_target_pairs={{0,3},{1,0},{2,1},{3,2},{4,7},{5,4},{6,5},{7,6},{8,11},{9,8},{10,9... | collective-permute-start | bytes 589832 | tf_op jit(solution)/shard_map/ppermute | solution.py:215
  35.5 0.0 collective-permute-done.6
  35.6 3.2 %collective-permute-done.7 = bf16[1,4,64,384]{3,2,1,0:T(8,128)(2,1)S(1)} collective-permute-done((bf16[1,4,64,384]{3,2,1,0:T(8,128)(2,1)S(1)}, bf16[1,4,64,384]{3,2,1,0:T(8,128)(2,1)S(1)}, u32[]{:S(2)}, u32[]{:S(2)}) %collective-permute-start.7) | collective-permute-done | bytes 196640 | tf_op jit(solution)/shard_map/ppermute | solution.py:215
  38.8 0.1 collective-permute-start.10
  38.8 4.7 %collective-permute-start.11 = (bf16[1,2,64,128]{3,2,1,0:T(8,128)(2,1)S(1)}, bf16[1,2,64,128]{3,2,1,0:T(8,128)(2,1)S(1)}, u32[]{:S(2)}, u32[]{:S(2)}) collective-permute-start(bf16[1,2,64,128]{3,2,1,0:T(8,128)(2,1)S(1)} %pad_maximum_fusion.3), channel_id=1, source_target_pairs={{0,28},{4,0},{8,4},{12,8},{16,12},{20,16},{24,20},{28,24},{1,29},{... | collective-permute-start | bytes 98312 | tf_op jit(solution)/shard_map/ppermute | solution.py:215
  43.5 0.0 collective-permute-done.8
  43.5 0.0 collective-permute-done.9
  43.5 1.9 %collective-permute-done.10 = bf16[1,2,64,128]{3,2,1,0:T(8,128)(2,1)S(1)} collective-permute-done((bf16[1,2,64,128]{3,2,1,0:T(8,128)(2,1)S(1)}, bf16[1,2,64,128]{3,2,1,0:T(8,128)(2,1)S(1)}, u32[]{:S(2)}, u32[]{:S(2)}) %collective-permute-start.10) | collective-permute-done | bytes 32800 | tf_op jit(solution)/shard_map/ppermute | solution.py:215
  45.4 0.0 collective-permute-done.11
  45.4 1.4 %copy-done.2 = bf16[2,4,128,768]{3,2,1,0:T(8,128)(2,1)S(1)} copy-done((bf16[2,4,128,768]{3,2,1,0:T(8,128)(2,1)S(1)}, bf16[2,4,128,768]{3,2,1,0:T(8,128)(2,1)}, u32[]{:S(2)}) %copy-start.2) | copy-done | bytes 1572888
  46.8 6.1 %shard_map.48 = bf16[4,4,64,576]{3,2,1,0:T(8,128)(2,1)} custom-call(bf16[2,4,128,768]{3,2,1,0:T(8,128)(2,1)S(1)} %get-tuple-element.20.a_in, bf16[2,4,128,768]{3,2,1,0:T(8,128)(2,1)S(1)} %copy-done.2, bf16[2,6,256,768]{3,2,1,0:T(8,128)(2,1)} %get-tuple-element.22.xd, s32[4,4,9]{2,1,0:T(4,128)S(1)} %copy-done.4, bf16[4,64,384]{2,1,0:T(8,128)(2,1)S(1)} %bitcast.10, ...), custom_call_target="tpu_custom_call" | custom-call | tf_op jit(solution)/shard_map/pallas_call | solution.py:242
  (13 shorter events, 0.1 us)
Async XLA Ops:
  0.0 1.3 %copy-start = (bf16[4,4,64,576]{3,2,1,0:T(8,128)(2,1)S(1)}, bf16[4,4,64,576]{3,2,1,0:T(8,128)(2,1)}, u32[]{:S(2)}) copy-start(bf16[4,4,64,576]{3,2,1,0:T(8,128)(2,1)} %ham.3) | copy-start | bytes 3538948
  1.3 1.3 %copy-start.1 = (bf16[4,4,64,576]{3,2,1,0:T(8,128)(2,1)S(1)}, bf16[4,4,64,576]{3,2,1,0:T(8,128)(2,1)}, u32[]{:S(2)}) copy-start(bf16[4,4,64,576]{3,2,1,0:T(8,128)(2,1)} %dens.3) | copy-start | bytes 3538948
  2.6 0.7 %copy-start.3 = (s32[4,4,9]{2,1,0:T(4,128)S(1)}, s32[4,4,9]{2,1,0:T(4,128)}, u32[]{:S(2)}) copy-start(s32[4,4,9]{2,1,0:T(4,128)} %pattern.3) | copy-start | bytes 1732
  3.3 20.5 %copy-start.4 = (s32[4,4,9]{2,1,0:T(4,128)S(1)}, s32[4,4,9]{2,1,0:T(4,128)}, u32[]{:S(2)}) copy-start(s32[4,4,9]{2,1,0:T(4,128)} %kept.3) | copy-start | bytes 1732
  4.0 9.4 %collective-permute-start = (bf16[2,4,64,384]{3,2,1,0:T(8,128)(2,1)S(1)}, bf16[2,4,64,384]{3,2,1,0:T(8,128)(2,1)S(1)}, u32[]{:S(2)}, u32[]{:S(2)}) collective-permute-start(bf16[2,4,64,384]{3,2,1,0:T(8,128)(2,1)S(1)} %get-tuple-element.16), channel_id=1, source_target_pairs={{0,1},{1,2},{2,3},{3,0},{4,5},{5,6},{6,7},{7,4},{8,9},{9,10},{10,1... | collective-permute-start | bytes 1179656 | tf_op jit(solution)/shard_map/ppermute | solution.py:215
  4.5 11.4 %collective-permute-start.1 = (bf16[2,4,64,384]{3,2,1,0:T(8,128)(2,1)S(1)}, bf16[2,4,64,384]{3,2,1,0:T(8,128)(2,1)S(1)}, u32[]{:S(2)}, u32[]{:S(2)}) collective-permute-start(bf16[2,4,64,384]{3,2,1,0:T(8,128)(2,1)S(1)} %get-tuple-element.17), channel_id=1, source_target_pairs={{0,3},{1,0},{2,1},{3,2},{4,7},{5,4},{6,5},{7,6},{8,11},{9,8},{10,9... | collective-permute-start | bytes 1179656 | tf_op jit(solution)/shard_map/ppermute | solution.py:215
  6.5 14.3 %collective-permute-start.2 = (bf16[2,6,64,128]{3,2,1,0:T(8,128)(2,1)S(1)}, bf16[2,6,64,128]{3,2,1,0:T(8,128)(2,1)S(1)}, u32[]{:S(2)}, u32[]{:S(2)}) collective-permute-start(bf16[2,6,64,128]{3,2,1,0:T(8,128)(2,1)S(1)} %get-tuple-element.18), channel_id=1, source_target_pairs={{0,4},{4,8},{8,12},{12,16},{16,20},{20,24},{24,28},{28,0},{1,5},{5... | collective-permute-start | bytes 589832 | tf_op jit(solution)/shard_map/ppermute | solution.py:215
  8.8 12.0 %collective-permute-start.3 = (bf16[2,6,64,128]{3,2,1,0:T(8,128)(2,1)S(1)}, bf16[2,6,64,128]{3,2,1,0:T(8,128)(2,1)S(1)}, u32[]{:S(2)}, u32[]{:S(2)}) collective-permute-start(bf16[2,6,64,128]{3,2,1,0:T(8,128)(2,1)S(1)} %get-tuple-element.19), channel_id=1, source_target_pairs={{0,28},{4,0},{8,4},{12,8},{16,12},{20,16},{24,20},{28,24},{1,29},{... | collective-permute-start | bytes 589832 | tf_op jit(solution)/shard_map/ppermute | solution.py:215
  16.0 7.6 %collective-permute-start.4 = (bf16[2,2,64,128]{3,2,1,0:T(8,128)(2,1)S(1)}, bf16[2,2,64,128]{3,2,1,0:T(8,128)(2,1)S(1)}, u32[]{:S(2)}, u32[]{:S(2)}) collective-permute-start(bf16[2,2,64,128]{3,2,1,0:T(8,128)(2,1)S(1)} %pad_maximum_fusion), channel_id=1, source_target_pairs={{0,4},{4,8},{8,12},{12,16},{16,20},{20,24},{24,28},{28,0},{1,5},{5... | collective-permute-start | bytes 196616 | tf_op jit(solution)/shard_map/ppermute | solution.py:215
  17.6 6.3 %collective-permute-start.5 = (bf16[2,2,64,128]{3,2,1,0:T(8,128)(2,1)S(1)}, bf16[2,2,64,128]{3,2,1,0:T(8,128)(2,1)S(1)}, u32[]{:S(2)}, u32[]{:S(2)}) collective-permute-start(bf16[2,2,64,128]{3,2,1,0:T(8,128)(2,1)S(1)} %pad_maximum_fusion.1), channel_id=1, source_target_pairs={{0,28},{4,0},{8,4},{12,8},{16,12},{20,16},{24,20},{28,24},{1,29},{... | collective-permute-start | bytes 196616 | tf_op jit(solution)/shard_map/ppermute | solution.py:215
  29.4 6.1 %collective-permute-start.6 = (bf16[1,4,64,384]{3,2,1,0:T(8,128)(2,1)S(1)}, bf16[1,4,64,384]{3,2,1,0:T(8,128)(2,1)S(1)}, u32[]{:S(2)}, u32[]{:S(2)}) collective-permute-start(bf16[1,4,64,384]{3,2,1,0:T(8,128)(2,1)S(1)} %bitcast.17), channel_id=1, source_target_pairs={{0,1},{1,2},{2,3},{3,0},{4,5},{5,6},{6,7},{7,4},{8,9},{9,10},{10,1... | collective-permute-start | bytes 589832 | tf_op jit(solution)/shard_map/ppermute | solution.py:215
  29.4 14.1 %collective-permute-start.8 = (bf16[1,6,64,128]{3,2,1,0:T(8,128)(2,1)S(1)}, bf16[1,6,64,128]{3,2,1,0:T(8,128)(2,1)S(1)}, u32[]{:S(2)}, u32[]{:S(2)}) collective-permute-start(bf16[1,6,64,128]{3,2,1,0:T(8,128)(2,1)S(1)} %bitcast.19), channel_id=1, source_target_pairs={{0,4},{4,8},{8,12},{12,16},{16,20},{20,24},{24,28},{28,0},{1,5},{5... | collective-permute-start | bytes 294920 | tf_op jit(solution)/shard_map/ppermute | solution.py:215
  30.5 13.1 %collective-permute-start.9 = (bf16[1,6,64,128]{3,2,1,0:T(8,128)(2,1)S(1)}, bf16[1,6,64,128]{3,2,1,0:T(8,128)(2,1)S(1)}, u32[]{:S(2)}, u32[]{:S(2)}) collective-permute-start(bf16[1,6,64,128]{3,2,1,0:T(8,128)(2,1)S(1)} %bitcast.18), channel_id=1, source_target_pairs={{0,28},{4,0},{8,4},{12,8},{16,12},{20,16},{24,20},{28,24},{1,29},{... | collective-permute-start | bytes 294920 | tf_op jit(solution)/shard_map/ppermute | solution.py:215
  34.2 4.6 %collective-permute-start.7 = (bf16[1,4,64,384]{3,2,1,0:T(8,128)(2,1)S(1)}, bf16[1,4,64,384]{3,2,1,0:T(8,128)(2,1)S(1)}, u32[]{:S(2)}, u32[]{:S(2)}) collective-permute-start(bf16[1,4,64,384]{3,2,1,0:T(8,128)(2,1)S(1)} %bitcast.16), channel_id=1, source_target_pairs={{0,3},{1,0},{2,1},{3,2},{4,7},{5,4},{6,5},{7,6},{8,11},{9,8},{10,9... | collective-permute-start | bytes 589832 | tf_op jit(solution)/shard_map/ppermute | solution.py:215
  38.8 6.7 %collective-permute-start.10 = (bf16[1,2,64,128]{3,2,1,0:T(8,128)(2,1)S(1)}, bf16[1,2,64,128]{3,2,1,0:T(8,128)(2,1)S(1)}, u32[]{:S(2)}, u32[]{:S(2)}) collective-permute-start(bf16[1,2,64,128]{3,2,1,0:T(8,128)(2,1)S(1)} %pad_maximum_fusion.2), channel_id=1, source_target_pairs={{0,4},{4,8},{8,12},{12,16},{16,20},{20,24},{24,28},{28,0},{1,5},{5... | collective-permute-start | bytes 98312 | tf_op jit(solution)/shard_map/ppermute | solution.py:215
  38.8 6.6 %collective-permute-start.11 = (bf16[1,2,64,128]{3,2,1,0:T(8,128)(2,1)S(1)}, bf16[1,2,64,128]{3,2,1,0:T(8,128)(2,1)S(1)}, u32[]{:S(2)}, u32[]{:S(2)}) collective-permute-start(bf16[1,2,64,128]{3,2,1,0:T(8,128)(2,1)S(1)} %pad_maximum_fusion.3), channel_id=1, source_target_pairs={{0,28},{4,0},{8,4},{12,8},{16,12},{20,16},{24,20},{28,24},{1,29},{... | collective-permute-start | bytes 98312 | tf_op jit(solution)/shard_map/ppermute | solution.py:215
  45.4 1.4 %copy-start.2 = (bf16[2,4,128,768]{3,2,1,0:T(8,128)(2,1)S(1)}, bf16[2,4,128,768]{3,2,1,0:T(8,128)(2,1)}, u32[]{:S(2)}) copy-start(bf16[2,4,128,768]{3,2,1,0:T(8,128)(2,1)} %get-tuple-element.21.s_in) | copy-start | bytes 4718596

commit v2 on v1

v2 whole, which is shorter than its diff:
```python
import jax
import jax.numpy as jnp
from jax import lax
from jax.experimental import pallas as pl
from jax.experimental.pallas import tpu as pltpu
from jax.sharding import PartitionSpec as P

W = 64
BF = jnp.bfloat16
F32 = jnp.float32
VMEM = pl.BlockSpec(memory_space=pltpu.VMEM)


def spot(x, y, x2, y2):
    p = y // 2
    return p, x + 1, W * (y - 2 * p + 1), 256 * (x2 - x + 1) + W * (y2 - 2 * p + 1)


def block(dense, x, y, x2, y2):
    p, i, r, c = spot(x, y, x2, y2)
    return dense[p, i, r : r + W, c : c + W]


def strip_mask(mask_ref, x):
    slot = lax.broadcasted_iota(jnp.int32, (9, 9 * W), 0)
    lane = lax.broadcasted_iota(jnp.int32, (9, 9 * W), 1)
    spread = (lane // W == slot).astype(BF)
    flags = mask_ref[x].astype(F32).astype(BF)
    return jnp.dot(flags, spread, preferred_element_type=F32)


def window_mask(mask_ref, x):
    slot = lax.broadcasted_iota(jnp.int32, (9, 12 * W), 0)
    lane = lax.broadcasted_iota(jnp.int32, (9, 12 * W), 1)
    flags = mask_ref[x].astype(F32).astype(BF)
    out = []
    for r in range(2):
        dy = (lane % 256) // W - r
        inside = (dy >= 0) & (dy <= 2) & (lane // 256 * 3 + dy == slot)
        out.append(jnp.dot(flags, inside.astype(BF), preferred_element_type=F32))
    return out


def both_rows(masks, p):
    first, second = masks
    return jnp.concatenate(
        [
            jnp.broadcast_to(first[2 * p : 2 * p + 1], (W, 768)),
            jnp.broadcast_to(second[2 * p + 1 : 2 * p + 2], (W, 768)),
        ],
        axis=0,
    )


def put_strips(dst, ref, pattern):
    zero = jnp.zeros((W, W), BF)
    for x in range(4):
        mask = strip_mask(pattern, x).astype(BF)
        for y in range(4):
            strip = ref[x, y] * mask[y : y + 1]
            p, r = y // 2, y % 2
            for d in range(3):
                piece = strip[:, 192 * d : 192 * d + 192]
                parts = [piece, zero] if r == 0 else [zero, piece]
                dst[p, x + 1, W + W * r : 2 * W + W * r, 256 * d : 256 * d + 256] = (
                    jnp.concatenate(parts, axis=1)
                )


def put_shared(dst):
    zero = jnp.zeros((W, 128), BF)
    for i in range(1, 5):
        for d in range(3):
            c = 256 * d
            dst[1, i, 0:64, c : c + 128] = dst[0, i, 128:192, c + 128 : c + 256]
            dst[1, i, 0:64, c + 128 : c + 256] = zero
            dst[0, i, 192:256, c + 128 : c + 256] = dst[1, i, 64:128, c : c + 128]
            dst[0, i, 192:256, c : c + 128] = zero


def put_y(dst, side, along=None, across=None):
    zero = jnp.zeros((W, W), BF)
    y, halo = (0, -1) if side == 0 else (3, 4)
    for x in range(4):
        for d in (-1, 0, 1):
            x2 = x + d
            same = zero if along is None else along(x, x2)
            if 0 <= x2 < 4:
                inner = block(dst, x2, y, x, halo).T
            else:
                inner = zero if across is None else across(x, x2)
            rest = jnp.zeros((W, 128), BF)
            parts = [same, inner, rest] if side == 0 else [rest, inner, same]
            c = 256 * (d + 1)
            dst[side, x + 1, 192 * side : 192 * side + W, c : c + 256] = jnp.concatenate(parts, axis=1)


def put_x(dst, side, within=None):
    zero = jnp.zeros((W, W), BF)
    at, edge, out, back = (0, 1, 0, 2) if side == 0 else (5, 4, 2, 0)
    for p in range(2):
        if within is not None:
            first = 2 * p - 1
            rows = [
                jnp.concatenate(
                    [
                        within(first + i, first + j) if abs(i - j) <= 1 else zero
                        for j in range(4)
                    ],
                    axis=1,
                )
                for i in range(4)
            ]
            dst[p, at, :, 256:512] = jnp.concatenate(rows, axis=0)
        else:
            dst[p, at, :, 256:512] = jnp.zeros((256, 256), BF)
        dst[p, at, :, 256 * back : 256 * back + 256] = dst[
            p, edge, :, 256 * out : 256 * out + 256
        ].T


def dense_product(left, right, p, x, e, cols=(0, 256)):
    total = None
    for d in range(max(-1, e - 1), min(1, e + 1) + 1):
        c = 256 * (e - d + 1)
        term = jnp.dot(
            left[:, 256 * (d + 1) : 256 * (d + 2)],
            right[p, x + 1 + d, :, c + cols[0] : c + cols[1]],
            preferred_element_type=F32,
        )
        total = term if total is None else total + term
    return total


def line_message(blocks, ends, flags):
    tiles = []
    for get in blocks:
        tiles += [jnp.concatenate([get(i, i), get(i, i + 1)], axis=1) for i in range(4)]
    tiles.append(jnp.concatenate([blocks[0](0, -1), blocks[1](0, -1)], axis=1))
    rows = [jnp.broadcast_to(f, (16, W)).astype(BF) for f in flags]
    tiles.append(jnp.concatenate([blocks[2](0, -1), jnp.concatenate(rows, axis=0)], axis=1))
    for pair in ends:
        tiles.append(jnp.concatenate(pair, axis=1))
    return tiles


def local_kernel(
    ham, dens, pattern, kept, cy_up, cy_down, y_up, y_down, x_up, x_down, xh, xd, xs
):
    for ref, dst in ((ham, xh), (dens, xd)):
        put_strips(dst, ref, pattern)
        put_shared(dst)
        for side in range(2):
            put_y(dst, side)
        for side in range(2):
            put_x(dst, side)
    flags = {}
    for x in range(4):
        masks = window_mask(kept, x)
        for p in range(2):
            keep = both_rows(masks, p)
            for e in range(-1 if x == 0 else 0, 2):
                cols = slice(256 * (e + 1), 256 * (e + 2))
                whole = x in (0, 3) and e == 0
                rows = slice(64, 192) if whole or x in (0, 3) else slice(64 + W * p, 128 + W * p)
                part = slice(rows.start - 64, rows.stop - 64)
                total = dense_product(xh[p, x + 1, rows, :], xd, p, x, e)
                total += dense_product(xd[p, x + 1, rows, :], xh, p, x, e)
                xs[p, x + 1, rows, cols] = (total * keep[part, cols]).astype(BF)
        flags[x] = strip_mask(kept, x)
    mats = (xh, xd, xs)
    order = (xs, xh, xd)

    def flag(x, y, dx, dy):
        k = 3 * (dx + 1) + dy + 1
        return flags[x][y : y + 1, W * k : W * k + W]

    for x, out, dx in ((3, x_up, 1), (0, x_down, -1)):
        get = [lambda i, j, m=m: block(m, x, i, x, j) for m in mats]
        marks = [flag(x, 0, 0, -1), flag(x, 0, dx, -1), flag(x, 3, 0, 1), flag(x, 3, dx, 1)]
        for n, tile in enumerate(line_message(get, [], marks)):
            out[n] = tile
    for y, out, corner, dy in ((3, y_up, cy_up, 1), (0, y_down, cy_down, -1)):
        get = [lambda i, j, m=m: block(m, i, y, j, y) for m in mats]
        marks = [flag(0, y, -1, 0), flag(0, y, -1, dy), flag(3, y, 1, 0), flag(3, y, 1, dy)]
        ends = [[block(m, x, y, x2, y + dy) for m in (xh, xd)] for x, x2 in ((0, -1), (3, 4))]
        for n, tile in enumerate(line_message(get, ends, marks)):
            out[n] = tile
        for n, (x, x2) in enumerate(((0, -1), (3, 4))):
            parts = [block(m, x, y, x, y) for m in order]
            parts += [block(xs, x, y, x2, y), block(xs, x, y, x, y + dy), jnp.zeros((W, W), BF)]
            corner[n] = jnp.concatenate(parts, axis=1)


def line_blocks(msg, n, corners, first=None, last=None):
    def right(i):
        if i == 3 and last is not None:
            return last
        return msg[4 * n + i][:, W:]

    def left():
        if first is not None:
            return first
        return msg[12][:, W * n : W * n + W]

    def get(i, j):
        if i == j:
            return corners[0 if i < 0 else 1] if i in (-1, 4) else msg[4 * n + i][:, :W]
        if (i, j) == (0, -1):
            return left()
        if (i, j) == (-1, 0):
            return left().T
        return right(i) if j > i else right(j).T

    return get


def last_kernel(
    ham, dens, pattern, kept, y_low, y_high, x_low, x_high, c_low, c_high, out, xh, xd, xs, a_rows
):
    ys, xm, cs = (y_low, y_high), (x_low, x_high), (c_low, c_high)
    def corner(sx, sy, k):
        return cs[sx][sy][:, W * k : W * k + W]

    for n, (ref, dst) in enumerate(((ham, xh), (dens, xd))):
        put_strips(dst, ref, pattern)
        put_shared(dst)
        for side in range(2):
            m = ys[side]
            line = line_blocks(m, n, None)
            put_y(
                dst,
                side,
                line,
                lambda x, x2, m=m, n=n: m[14 if x == 0 else 15][:, W * n : W * n + W],
            )
        for side in range(2):
            put_x(dst, side, line_blocks(xm[side], n, [corner(side, t, n + 1) for t in range(2)]))
    for x in range(4):
        masks = window_mask(kept, x)
        for p in range(2):
            keep = both_rows(masks, p)
            lh = xh[p, x + 1, 64:192, :]
            ld = xd[p, x + 1, 64:192, :]
            for e in range(-1, 2):
                cols = slice(256 * (e + 1), 256 * (e + 2))
                a = dense_product(lh, xd, p, x, e) * keep[:, cols]
                b = dense_product(ld, xh, p, x, e) * keep[:, cols]
                a_rows[p, x, :, cols] = a.astype(BF)
                xs[p, x + 1, 64:192, cols] = (a + b).astype(BF)
    put_shared(xs)
    firsts = {}
    for sx in range(2):
        hx, ex, go, back = (0, 1, 0, 2) if sx == 0 else (5, 4, 2, 0)
        for sy in range(2):
            hp, ep, base = (0, 1, 0) if sy == 0 else (3, 2, 128)

            def at(m, k, f):
                part = 256 * (f[0] - k[0] + 1)
                rows = slice(base, base + 128) if k[1] is None else slice(W * k[1], W * k[1] + W)
                start = part + (base if f[1] is None else W * f[1])
                return m[sy, k[0], rows, start : start + (128 if f[1] is None else W)]

            def through(k, m, f):
                return jnp.dot(
                    at(xh, k, m), at(xd, m, f), preferred_element_type=F32
                ) + jnp.dot(at(xd, k, m), at(xh, m, f), preferred_element_type=F32)

            a, b, c, d = (hx, hp), (hx, ep), (ex, hp), (ex, ep)
            halo, brick = (hx, None), (ex, None)
            xt, yt = xm[sx], ys[sy]
            ba = xt[13][:, :W] if sy == 0 else xt[11][:, W:]
            ca = yt[13][:, :W] if sx == 0 else yt[11][:, W:]
            keep_ba = xt[13][32 * sy : 32 * sy + 1, W:].astype(F32)
            keep_bc = xt[13][32 * sy + 16 : 32 * sy + 17, W:].astype(F32)
            keep_ca = yt[13][32 * sx : 32 * sx + 1, W:].astype(F32)
            s_ba = ba.astype(F32) + corner(sx, sy, 4).astype(F32).T + through(b, brick, a) * keep_ba
            s_ca = (
                ca.astype(F32)
                + corner(sx, sy, 3).astype(F32).T
                + (through(c, b, a) + through(c, d, a)) * keep_ca
            )
            s_bc = (through(b, halo, c) + through(b, brick, c)) * keep_bc
            firsts[sx, sy] = s_ba.astype(BF), s_ca.astype(BF), s_bc.astype(BF).T
    for sy in range(2):
        line = line_blocks(ys[sy], 2, None, firsts[0, sy][1], firsts[1, sy][1])
        put_y(xs, sy, line, lambda x, x2, sy=sy: firsts[0 if x == 0 else 1, sy][2])
    for sx in range(2):
        put_x(
            xs,
            sx,
            line_blocks(
                xm[sx], 2, [corner(sx, t, 0) for t in range(2)], firsts[sx, 0][0], firsts[sx, 1][0]
            ),
        )
    for x in range(4):
        masks = window_mask(kept, x)
        for p in range(2):
            keep = both_rows(masks, p)
            la = a_rows[p, x]
            ld = xd[p, x + 1, 64:192, :]
            for e in range(-1, 2):
                cols = slice(256 * (e + 1), 256 * (e + 2))
                cubic = dense_product(la, xd, p, x, e) + dense_product(ld, xs, p, x, e)
                linear = xs[p, x + 1, 64:192, cols].astype(F32)
                total = ((3.0 * linear - 2.0 * cubic) * keep[:, cols]).astype(BF)
                first = slice(192 * (e + 1), 192 * (e + 2))
                out[x, 2 * p, :, first] = total[0:64, 0:192]
                out[x, 2 * p + 1, :, first] = total[64:128, 64:256]


def call(kernel, outs, scratch=()):
    return pl.pallas_call(
        kernel,
        out_shape=[jax.ShapeDtypeStruct(s, BF) for s in outs],
        out_specs=[VMEM] * len(outs),
        scratch_shapes=[pltpu.VMEM(s, BF) for s in scratch],
        compiler_params=pltpu.CompilerParams(vmem_limit_bytes=48 * 1024 * 1024),
    )


def shift(value, axis, step):
    count = lax.axis_size(axis)
    return lax.ppermute(value, axis, [(i, (i + step) % count) for i in range(count)])


def per_device(ham, dens, pattern, kept):
    dense = (2, 6, 256, 768)
    corner, y_line, x_line = (2, W, 384), (16, W, 128), (14, W, 128)
    cy_up, cy_down, y_up, y_down, x_up, x_down = call(
        local_kernel, [corner, corner, y_line, y_line, x_line, x_line], [dense] * 3
    )(ham, dens, pattern, kept)
    cy_low = shift(cy_up, "gy", 1)
    cy_high = shift(cy_down, "gy", -1)
    x_low = shift(x_up, "gx", 1)
    y_low = shift(y_up, "gy", 1)
    y_high = shift(y_down, "gy", -1)
    x_high = shift(x_down, "gx", -1)
    c_low = shift(jnp.stack([cy_low[1], cy_high[1]]), "gx", 1)
    c_high = shift(jnp.stack([cy_low[0], cy_high[0]]), "gx", -1)
    return call(last_kernel, [ham.shape], [dense] * 3 + [(2, 4, 128, 768)])(
        ham, dens, pattern, kept, y_low, y_high, x_low, x_high, c_low, c_high
    )[0]


def solution(mesh):
    return jax.shard_map(
        per_device,
        mesh=mesh,
        in_specs=(
            P("gx", "gy", None, None),
            P("gx", "gy", None, None),
            P("gx", "gy", None),
            P("gx", "gy", None),
        ),
        out_specs=P("gx", "gy", None, None),
        check_vma=False,
    )
```

time: 53.6 us -> 40.8 us (0.76)
  starting transfers between devices: 23.5 us -> 14.6 us
  waiting for transfers between devices: 12.2 us -> 9.72 us
  local copies, waits for them, and re-layouts: 4.77 us -> 4.05 us
    ppermute x12 -> x8, starting transfers between devices: 23.5 us -> 14.6 us  [shift(): lax.ppermute(value, axis, [(i, (i + step) % count) for i in range(count)])]
    ppermute x12 -> x8, waiting for transfers between devices: 12.2 us -> 9.72 us  [shift(): lax.ppermute(value, axis, [(i, (i + step) % count) for i in range(count)])]
    unnamed x10 -> x8, local copies, waits for them, and re-layouts: 4.74 us -> 4.02 us
    pallas_call x3 -> x2, Pallas kernels: 12.4 us -> 12.1 us  [the longest x1 8.47 us: per_device(): call(last_kernel, [ham.shape], [dense] * 3 + [(2, 4, 128, 768)])]
  transfers between devices with their start and end apart: 12 -> 8, of which waited for: 6 -> 2; matrix products, arithmetic and copies ran while one was open for 0% -> 0% of each run, Pallas kernels for 0% -> 0%
where the time goes in v2:
time: 40.8 us; the launch traced here: 40.6 us
  starting transfers between devices  14.6 us (36%)
  Pallas kernels  12.1 us (30%)
  waiting for transfers between devices  9.72 us (24%)
  local copies, waits for them, and re-layouts  4.05 us (10%)
    ppermute x8, starting transfers between devices, shift(): lax.ppermute(value, axis, [(i, (i + step) % count) for i in range(count)])  14.6 us
    ppermute x8, waiting for transfers between devices, shift(): lax.ppermute(value, axis, [(i, (i + step) % count) for i in range(count)])  9.72 us
    pallas_call x1, Pallas kernels, per_device(): call(last_kernel, [ham.shape], [dense] * 3 + [(2, 4, 128, 768)])  8.47 us
    unnamed x8, local copies, waits for them, and re-layouts  4.02 us
    pallas_call x1, Pallas kernels, per_device(): call(local_kernel, [corner, corner, y_line, y_line, x_line, x_line], [den...  3.63 us
  transfers between devices with their start and end apart: 8, of which 2 were waited for; matrix products, arithmetic and copies ran while one was open for 0% of the time, Pallas kernels for 0%

profile of v2, /device:TPU:0, one launch (start us, length us, event | category | flops | bytes accessed | tf_op | source)
XLA Modules:
  0.0 40.6 jit_solution(1793758818870411437)
XLA Ops:
  0.0 0.0 copy-start
  0.0 1.3 %copy-done = bf16[4,4,64,576]{3,2,1,0:T(8,128)(2,1)S(1)} copy-done((bf16[4,4,64,576]{3,2,1,0:T(8,128)(2,1)S(1)}, bf16[4,4,64,576]{3,2,1,0:T(8,128)(2,1)}, u32[]{:S(2)}) %copy-start) | copy-done | bytes 1179672
  1.3 0.0 copy-start.1
  1.3 1.3 %copy-done.1 = bf16[4,4,64,576]{3,2,1,0:T(8,128)(2,1)S(1)} copy-done((bf16[4,4,64,576]{3,2,1,0:T(8,128)(2,1)S(1)}, bf16[4,4,64,576]{3,2,1,0:T(8,128)(2,1)}, u32[]{:S(2)}) %copy-start.1) | copy-done | bytes 1179672
  2.6 0.0 copy-start.2
  2.6 0.7 %copy-done.2 = s32[4,4,9]{2,1,0:T(4,128)S(1)} copy-done((s32[4,4,9]{2,1,0:T(4,128)S(1)}, s32[4,4,9]{2,1,0:T(4,128)}, u32[]{:S(2)}) %copy-start.2) | copy-done | bytes 600
  3.3 0.0 copy-start.3
  3.3 0.7 %copy-done.3 = s32[4,4,9]{2,1,0:T(4,128)S(1)} copy-done((s32[4,4,9]{2,1,0:T(4,128)S(1)}, s32[4,4,9]{2,1,0:T(4,128)}, u32[]{:S(2)}) %copy-start.3) | copy-done | bytes 600
  4.0 3.6 %shard_map.46 = (bf16[2,64,384]{2,1,0:T(8,128)(2,1)S(1)}, bf16[2,64,384]{2,1,0:T(8,128)(2,1)S(1)}, bf16[16,64,128]{2,1,0:T(8,128)(2,1)S(1)}, bf16[16,64,128]{2,1...) custom-call(bf16[4,4,64,576]{3,2,1,0:T(8,128)(2,1)S(1)} %copy-done, ...), custom_call_target="tpu_custom_call" | custom-call | tf_op jit(solution)/shard_map/pallas_call | solution.py:330
  7.7 0.5 %collective-permute-start.4 = (bf16[2,64,384]{2,1,0:T(8,128)(2,1)S(1)}, bf16[2,64,384]{2,1,0:T(8,128)(2,1)S(1)}, u32[]{:S(2)}, u32[]{:S(2)}) collective-permute-start(bf16[2,64,384]{2,1,0:T(8,128)(2,1)S(1)} %get-tuple-element.15), channel_id=1, source_target_pairs={{0,1},{1,2},{2,3},{3,0},{4,5},{5,6},{6,7},{7,4},{8,9},{9,10},{10,1... | collective-permute-start | bytes 294920 | tf_op jit(solution)/shard_map/ppermute | solution.py:324
  8.2 2.0 %collective-permute-start.5 = (bf16[2,64,384]{2,1,0:T(8,128)(2,1)S(1)}, bf16[2,64,384]{2,1,0:T(8,128)(2,1)S(1)}, u32[]{:S(2)}, u32[]{:S(2)}) collective-permute-start(bf16[2,64,384]{2,1,0:T(8,128)(2,1)S(1)} %get-tuple-element.16), channel_id=1, source_target_pairs={{0,3},{1,0},{2,1},{3,2},{4,7},{5,4},{6,5},{7,6},{8,11},{9,8},{10,9... | collective-permute-start | bytes 294920 | tf_op jit(solution)/shard_map/ppermute | solution.py:324
  10.2 2.3 %collective-permute-start.2 = (bf16[14,64,128]{2,1,0:T(8,128)(2,1)S(1)}, bf16[14,64,128]{2,1,0:T(8,128)(2,1)S(1)}, u32[]{:S(2)}, u32[]{:S(2)}) collective-permute-start(bf16[14,64,128]{2,1,0:T(8,128)(2,1)S(1)} %get-tuple-element.13), channel_id=1, source_target_pairs={{0,4},{4,8},{8,12},{12,16},{16,20},{20,24},{24,28},{28,0},{1,5},{5... | collective-permute-start | bytes 688136 | tf_op jit(solution)/shard_map/ppermute | solution.py:324
  12.4 3.0 %collective-permute-start.3 = (bf16[14,64,128]{2,1,0:T(8,128)(2,1)S(1)}, bf16[14,64,128]{2,1,0:T(8,128)(2,1)S(1)}, u32[]{:S(2)}, u32[]{:S(2)}) collective-permute-start(bf16[14,64,128]{2,1,0:T(8,128)(2,1)S(1)} %get-tuple-element.14), channel_id=1, source_target_pairs={{0,28},{4,0},{8,4},{12,8},{16,12},{20,16},{24,20},{28,24},{1,29},{... | collective-permute-start | bytes 688136 | tf_op jit(solution)/shard_map/ppermute | solution.py:324
  15.5 0.0 collective-permute-start
  15.5 0.0 collective-permute-done.4
  15.5 1.7 %collective-permute-start.1 = (bf16[16,64,128]{2,1,0:T(8,128)(2,1)S(1)}, bf16[16,64,128]{2,1,0:T(8,128)(2,1)S(1)}, u32[]{:S(2)}, u32[]{:S(2)}) collective-permute-start(bf16[16,64,128]{2,1,0:T(8,128)(2,1)S(1)} %get-tuple-element.12), channel_id=1, source_target_pairs={{0,3},{1,0},{2,1},{3,2},{4,7},{5,4},{6,5},{7,6},{8,11},{9,8},{10,9... | collective-permute-start | bytes 786440 | tf_op jit(solution)/shard_map/ppermute | solution.py:324
  17.2 0.0 collective-permute-done.5
  17.3 0.1 collective-permute-start.6
  17.4 7.5 %collective-permute-done.6.c_low = bf16[2,64,384]{2,1,0:T(8,128)(2,1)S(1)} collective-permute-done((bf16[2,64,384]{2,1,0:T(8,128)(2,1)S(1)}, bf16[2,64,384]{2,1,0:T(8,128)(2,1)S(1)}, u32[]{:S(2)}, u32[]{:S(2)}) %collective-permute-start.6) | collective-permute-done | bytes 98336 | tf_op jit(solution)/shard_map/ppermute | solution.py:324
  24.9 5.0 %collective-permute-start.7 = (bf16[2,64,384]{2,1,0:T(8,128)(2,1)S(1)}, bf16[2,64,384]{2,1,0:T(8,128)(2,1)S(1)}, u32[]{:S(2)}, u32[]{:S(2)}) collective-permute-start(bf16[2,64,384]{2,1,0:T(8,128)(2,1)S(1)} %pad_maximum_fusion.1), channel_id=1, source_target_pairs={{0,28},{4,0},{8,4},{12,8},{16,12},{20,16},{24,20},{28,24},{1,29},{... | collective-permute-start | bytes 294920 | tf_op jit(solution)/shard_map/ppermute | solution.py:324
  29.9 2.2 %collective-permute-done.7.c_high = bf16[2,64,384]{2,1,0:T(8,128)(2,1)S(1)} collective-permute-done((bf16[2,64,384]{2,1,0:T(8,128)(2,1)S(1)}, bf16[2,64,384]{2,1,0:T(8,128)(2,1)S(1)}, u32[]{:S(2)}, u32[]{:S(2)}) %collective-permute-start.7) | collective-permute-done | bytes 98336 | tf_op jit(solution)/shard_map/ppermute | solution.py:324
  32.1 0.0 collective-permute-done.2.x_low
  32.1 0.0 collective-permute-done.3.x_high
  32.1 0.0 collective-permute-done.y_low
  32.1 0.0 collective-permute-done.1.y_high
  32.1 8.5 %shard_map.47 = bf16[4,4,64,576]{3,2,1,0:T(8,128)(2,1)} custom-call(bf16[4,4,64,576]{3,2,1,0:T(8,128)(2,1)S(1)} %copy-done, bf16[4,4,64,576]{3,2,1,0:T(8,128)(2,1)S(1)} %copy-done.1, s32[4,4,9]{2,1,0:T(4,128)S(1)} %copy-done.2, s32[4,4,9]{2,1,0:T(4,128)S(1)} %copy-done.3, bf16[16,64,128]{2,1,0:T(8,128)(2,1)S(1)} %collective-permute-done.y_low, ...), custom_call_target="tpu_custom_call" | custom-call | tf_op jit(solution)/shard_map/pallas_call | solution.py:341
  (4 shorter events, 0.1 us)
Async XLA Ops:
  0.0 1.3 %copy-start = (bf16[4,4,64,576]{3,2,1,0:T(8,128)(2,1)S(1)}, bf16[4,4,64,576]{3,2,1,0:T(8,128)(2,1)}, u32[]{:S(2)}) copy-start(bf16[4,4,64,576]{3,2,1,0:T(8,128)(2,1)} %ham.3) | copy-start | bytes 3538948
  1.3 1.3 %copy-start.1 = (bf16[4,4,64,576]{3,2,1,0:T(8,128)(2,1)S(1)}, bf16[4,4,64,576]{3,2,1,0:T(8,128)(2,1)}, u32[]{:S(2)}) copy-start(bf16[4,4,64,576]{3,2,1,0:T(8,128)(2,1)} %dens.3) | copy-start | bytes 3538948
  2.6 0.7 %copy-start.2 = (s32[4,4,9]{2,1,0:T(4,128)S(1)}, s32[4,4,9]{2,1,0:T(4,128)}, u32[]{:S(2)}) copy-start(s32[4,4,9]{2,1,0:T(4,128)} %pattern.3) | copy-start | bytes 1732
  3.3 0.7 %copy-start.3 = (s32[4,4,9]{2,1,0:T(4,128)S(1)}, s32[4,4,9]{2,1,0:T(4,128)}, u32[]{:S(2)}) copy-start(s32[4,4,9]{2,1,0:T(4,128)} %kept.3) | copy-start | bytes 1732
  7.7 7.8 %collective-permute-start.4 = (bf16[2,64,384]{2,1,0:T(8,128)(2,1)S(1)}, bf16[2,64,384]{2,1,0:T(8,128)(2,1)S(1)}, u32[]{:S(2)}, u32[]{:S(2)}) collective-permute-start(bf16[2,64,384]{2,1,0:T(8,128)(2,1)S(1)} %get-tuple-element.15), channel_id=1, source_target_pairs={{0,1},{1,2},{2,3},{3,0},{4,5},{5,6},{6,7},{7,4},{8,9},{9,10},{10,1... | collective-permute-start | bytes 294920 | tf_op jit(solution)/shard_map/ppermute | solution.py:324
  8.2 9.1 %collective-permute-start.5 = (bf16[2,64,384]{2,1,0:T(8,128)(2,1)S(1)}, bf16[2,64,384]{2,1,0:T(8,128)(2,1)S(1)}, u32[]{:S(2)}, u32[]{:S(2)}) collective-permute-start(bf16[2,64,384]{2,1,0:T(8,128)(2,1)S(1)} %get-tuple-element.16), channel_id=1, source_target_pairs={{0,3},{1,0},{2,1},{3,2},{4,7},{5,4},{6,5},{7,6},{8,11},{9,8},{10,9... | collective-permute-start | bytes 294920 | tf_op jit(solution)/shard_map/ppermute | solution.py:324
  10.2 21.9 %collective-permute-start.2 = (bf16[14,64,128]{2,1,0:T(8,128)(2,1)S(1)}, bf16[14,64,128]{2,1,0:T(8,128)(2,1)S(1)}, u32[]{:S(2)}, u32[]{:S(2)}) collective-permute-start(bf16[14,64,128]{2,1,0:T(8,128)(2,1)S(1)} %get-tuple-element.13), channel_id=1, source_target_pairs={{0,4},{4,8},{8,12},{12,16},{16,20},{20,24},{24,28},{28,0},{1,5},{5... | collective-permute-start | bytes 688136 | tf_op jit(solution)/shard_map/ppermute | solution.py:324
  12.4 19.6 %collective-permute-start.3 = (bf16[14,64,128]{2,1,0:T(8,128)(2,1)S(1)}, bf16[14,64,128]{2,1,0:T(8,128)(2,1)S(1)}, u32[]{:S(2)}, u32[]{:S(2)}) collective-permute-start(bf16[14,64,128]{2,1,0:T(8,128)(2,1)S(1)} %get-tuple-element.14), channel_id=1, source_target_pairs={{0,28},{4,0},{8,4},{12,8},{16,12},{20,16},{24,20},{28,24},{1,29},{... | collective-permute-start | bytes 688136 | tf_op jit(solution)/shard_map/ppermute | solution.py:324
  15.5 16.6 %collective-permute-start = (bf16[16,64,128]{2,1,0:T(8,128)(2,1)S(1)}, bf16[16,64,128]{2,1,0:T(8,128)(2,1)S(1)}, u32[]{:S(2)}, u32[]{:S(2)}) collective-permute-start(bf16[16,64,128]{2,1,0:T(8,128)(2,1)S(1)} %get-tuple-element.11), channel_id=1, source_target_pairs={{0,1},{1,2},{2,3},{3,0},{4,5},{5,6},{6,7},{7,4},{8,9},{9,10},{10,1... | collective-permute-start | bytes 786440 | tf_op jit(solution)/shard_map/ppermute | solution.py:324
  15.5 16.6 %collective-permute-start.1 = (bf16[16,64,128]{2,1,0:T(8,128)(2,1)S(1)}, bf16[16,64,128]{2,1,0:T(8,128)(2,1)S(1)}, u32[]{:S(2)}, u32[]{:S(2)}) collective-permute-start(bf16[16,64,128]{2,1,0:T(8,128)(2,1)S(1)} %get-tuple-element.12), channel_id=1, source_target_pairs={{0,3},{1,0},{2,1},{3,2},{4,7},{5,4},{6,5},{7,6},{8,11},{9,8},{10,9... | collective-permute-start | bytes 786440 | tf_op jit(solution)/shard_map/ppermute | solution.py:324
  17.3 7.6 %collective-permute-start.6 = (bf16[2,64,384]{2,1,0:T(8,128)(2,1)S(1)}, bf16[2,64,384]{2,1,0:T(8,128)(2,1)S(1)}, u32[]{:S(2)}, u32[]{:S(2)}) collective-permute-start(bf16[2,64,384]{2,1,0:T(8,128)(2,1)S(1)} %pad_maximum_fusion), channel_id=1, source_target_pairs={{0,4},{4,8},{8,12},{12,16},{16,20},{20,24},{24,28},{28,0},{1,5},{5... | collective-permute-start | bytes 294920 | tf_op jit(solution)/shard_map/ppermute | solution.py:324
  24.9 7.2 %collective-permute-start.7 = (bf16[2,64,384]{2,1,0:T(8,128)(2,1)S(1)}, bf16[2,64,384]{2,1,0:T(8,128)(2,1)S(1)}, u32[]{:S(2)}, u32[]{:S(2)}) collective-permute-start(bf16[2,64,384]{2,1,0:T(8,128)(2,1)S(1)} %pad_maximum_fusion.1), channel_id=1, source_target_pairs={{0,28},{4,0},{8,4},{12,8},{16,12},{20,16},{24,20},{28,24},{1,29},{... | collective-permute-start | bytes 294920 | tf_op jit(solution)/shard_map/ppermute | solution.py:324

commit v3 on v2

--- a/solution.py
+++ b/solution.py
@@ -41,23 +41,21 @@
     return out
 
 
-def both_rows(masks, p):
-    first, second = masks
+def both_rows(wide, x, p):
     return jnp.concatenate(
         [
-            jnp.broadcast_to(first[2 * p : 2 * p + 1], (W, 768)),
-            jnp.broadcast_to(second[2 * p + 1 : 2 * p + 2], (W, 768)),
+            jnp.broadcast_to(wide[x, 0, 2 * p : 2 * p + 1, :], (W, 768)),
+            jnp.broadcast_to(wide[x, 1, 2 * p + 1 : 2 * p + 2, :], (W, 768)),
         ],
         axis=0,
     )
 
 
-def put_strips(dst, ref, pattern):
+def put_strips(dst, ref):
     zero = jnp.zeros((W, W), BF)
     for x in range(4):
-        mask = strip_mask(pattern, x).astype(BF)
         for y in range(4):
-            strip = ref[x, y] * mask[y : y + 1]
+            strip = ref[x, y]
             p, r = y // 2, y % 2
             for d in range(3):
                 piece = strip[:, 192 * d : 192 * d + 192]
@@ -144,68 +142,126 @@
     return tiles
 
 
-def local_kernel(
-    ham, dens, pattern, kept, cy_up, cy_down, y_up, y_down, x_up, x_down, xh, xd, xs
+def send_kernel(
+    ham, dens, pattern, kept, cy_up, cy_down, ends, y_up, y_down, x_up, x_down, hm, dm, wide,
+    hb, db, pb, kb, live, keep, sems, mask_sems,
 ):
-    for ref, dst in ((ham, xh), (dens, xd)):
-        put_strips(dst, ref, pattern)
-        put_shared(dst)
-        for side in range(2):
-            put_y(dst, side)
-        for side in range(2):
-            put_x(dst, side)
-    flags = {}
-    for x in range(4):
-        masks = window_mask(kept, x)
-        for p in range(2):
-            keep = both_rows(masks, p)
-            for e in range(-1 if x == 0 else 0, 2):
-                cols = slice(256 * (e + 1), 256 * (e + 2))
-                whole = x in (0, 3) and e == 0
-                rows = slice(64, 192) if whole or x in (0, 3) else slice(64 + W * p, 128 + W * p)
-                part = slice(rows.start - 64, rows.stop - 64)
-                total = dense_product(xh[p, x + 1, rows, :], xd, p, x, e)
-                total += dense_product(xd[p, x + 1, rows, :], xh, p, x, e)
-                xs[p, x + 1, rows, cols] = (total * keep[part, cols]).astype(BF)
-        flags[x] = strip_mask(kept, x)
-    mats = (xh, xd, xs)
-    order = (xs, xh, xd)
+    masks = [
+        pltpu.make_async_copy(pattern, pb, mask_sems.at[0]),
+        pltpu.make_async_copy(kept, kb, mask_sems.at[1]),
+    ]
+    copies = []
+    for x in (0, 3, 1, 2):
+        for n, (ref, buf) in enumerate(((ham, hb), (dens, db))):
+            copies.append(pltpu.make_async_copy(ref.at[x], buf.at[x], sems.at[n, x]))
+    for copy in masks + copies:
+        copy.start()
+    for copy in masks:
+        copy.wait()
+    for x in range(4):
+        live[x] = strip_mask(pb, x)
+        keep[x] = strip_mask(kb, x)
+        wide[x, 0], wide[x, 1] = window_mask(kb, x)
+    for copy in copies:
+        copy.wait()
+    for x in range(4):
+        for y in range(4):
+            mask = live[x, y : y + 1, :].astype(BF)
+            hm[x, y] = hb[x, y] * mask
+            dm[x, y] = db[x, y] * mask
+
+    def lanes(dx, dy):
+        k = 3 * (dx + 1) + dy + 1
+        return slice(W * k, W * k + W)
 
     def flag(x, y, dx, dy):
-        k = 3 * (dx + 1) + dy + 1
-        return flags[x][y : y + 1, W * k : W * k + W]
+        return keep[x, y : y + 1, lanes(dx, dy)]
+
+    def get(ref, x, y, dx, dy):
+        return ref[x, y, :, lanes(dx, dy)]
+
+    def through(x, y, cells, dx, dy):
+        left, right = [], []
+        for first, second in ((hm, dm), (dm, hm)):
+            for mx, my in cells:
+                left.append(get(first, x, y, mx - x, my - y))
+                right.append(get(second, mx, my, x + dx - mx, y + dy - my))
+        total = jnp.dot(
+            jnp.concatenate(left, axis=1), jnp.concatenate(right, axis=0), preferred_element_type=F32
+        )
+        return (total * flag(x, y, dx, dy)).astype(BF)
+
+    def rows(left, right):
+        return lax.dot_general(left, right, (((1,), (1,)), ((), ())), preferred_element_type=F32)
+
+    def own(x, y):
+        total = rows(hm[x, y], dm[x, y])
+        return ((total + total.T) * flag(x, y, 0, 0)).astype(BF)
+
+    def link(x, y, dx, dy):
+        if dx == 1:
+            parts = [(slice(192, 576), slice(0, 384))]
+        else:
+            parts = [(slice(192 * d + 64, 192 * d + 192), slice(192 * d, 192 * d + 128)) for d in range(3)]
+        left, right = [], []
+        for first, second in ((hm, dm), (dm, hm)):
+            left += [first[x, y, :, one] for one, _ in parts]
+            right += [second[x + dx, y + dy, :, other] for _, other in parts]
+        total = rows(jnp.concatenate(left, axis=1), jnp.concatenate(right, axis=1))
+        return (total * flag(x, y, dx, dy)).astype(BF)
+
+    def pair(one, two):
+        return jnp.concatenate([one, two], axis=1)
+
+    selfs = {(x, y): own(x, y) for x in range(4) for y in range(4) if x in (0, 3) or y in (0, 3)}
+    for y, out, dy in ((3, cy_up, 1), (0, cy_down, -1)):
+        for n, (x, dx) in enumerate(((0, -1), (3, 1))):
+            across = through(x, y, ((x, y), (x - dx, y)), 0, dy)
+            out[n, 0] = pair(selfs[x, y], get(hm, x, y, 0, 0))
+            out[n, 1] = pair(get(dm, x, y, 0, 0), through(x, y, ((x, y), (x, y - dy)), dx, 0))
+            out[n, 2] = pair(across, jnp.zeros((W, W), BF))
+            ends[0 if y == 0 else 1, n] = across.T
+
+    def line(out, cell, step, marks):
+        dx, dy = step
+        for i in range(4):
+            x, y = cell(i)
+            for n, ref in enumerate((hm, dm)):
+                out[4 * n + i] = pair(get(ref, x, y, 0, 0), get(ref, x, y, dx, dy))
+            if i < 3:
+                out[9 + i] = pair(selfs[x, y], link(x, y, dx, dy))
+            else:
+                rows = [jnp.broadcast_to(m, (16, W)).astype(BF) for m in marks]
+                out[12] = pair(selfs[x, y], jnp.concatenate(rows, axis=0))
+        x, y = cell(0)
+        out[8] = pair(get(hm, x, y, -dx, -dy), get(dm, x, y, -dx, -dy))
 
     for x, out, dx in ((3, x_up, 1), (0, x_down, -1)):
-        get = [lambda i, j, m=m: block(m, x, i, x, j) for m in mats]
         marks = [flag(x, 0, 0, -1), flag(x, 0, dx, -1), flag(x, 3, 0, 1), flag(x, 3, dx, 1)]
-        for n, tile in enumerate(line_message(get, [], marks)):
-            out[n] = tile
-    for y, out, corner, dy in ((3, y_up, cy_up, 1), (0, y_down, cy_down, -1)):
-        get = [lambda i, j, m=m: block(m, i, y, j, y) for m in mats]
+        line(out, lambda i: (x, i), (0, 1), marks)
+    for y, out, dy in ((3, y_up, 1), (0, y_down, -1)):
         marks = [flag(0, y, -1, 0), flag(0, y, -1, dy), flag(3, y, 1, 0), flag(3, y, 1, dy)]
-        ends = [[block(m, x, y, x2, y + dy) for m in (xh, xd)] for x, x2 in ((0, -1), (3, 4))]
-        for n, tile in enumerate(line_message(get, ends, marks)):
-            out[n] = tile
-        for n, (x, x2) in enumerate(((0, -1), (3, 4))):
-            parts = [block(m, x, y, x, y) for m in order]
-            parts += [block(xs, x, y, x2, y), block(xs, x, y, x, y + dy), jnp.zeros((W, W), BF)]
-            corner[n] = jnp.concatenate(parts, axis=1)
+        line(out, lambda i: (i, y), (1, 0), marks)
+        for n, (x, dx) in enumerate(((0, -1), (3, 1))):
+            out[13 + n] = pair(get(hm, x, y, dx, dy), get(dm, x, y, dx, dy))
 
 
 def line_blocks(msg, n, corners, first=None, last=None):
+    base = 4 * n if n < 2 else 9
+
     def right(i):
         if i == 3 and last is not None:
             return last
-        return msg[4 * n + i][:, W:]
+        return msg[base + i][:, W:]
 
     def left():
         if first is not None:
             return first
-        return msg[12][:, W * n : W * n + W]
+        return msg[8][:, W * n : W * n + W]
 
     def get(i, j):
         if i == j:
-            return corners[0 if i < 0 else 1] if i in (-1, 4) else msg[4 * n + i][:, :W]
+            return corners[0 if i < 0 else 1] if i in (-1, 4) else msg[base + i][:, :W]
         if (i, j) == (0, -1):
             return left()
         if (i, j) == (-1, 0):
@@ -216,14 +272,18 @@
 
 
 def last_kernel(
-    ham, dens, pattern, kept, y_low, y_high, x_low, x_high, c_low, c_high, out, xh, xd, xs, a_rows
+    ham, dens, wide, y_low, y_high, x_low, x_high, cy_low, cy_high, c_low, c_high,
+    out, xh, xd, xs, a_rows,
 ):
-    ys, xm, cs = (y_low, y_high), (x_low, x_high), (c_low, c_high)
+    ys, xm, cys, cs = (y_low, y_high), (x_low, x_high), (cy_low, cy_high), (c_low, c_high)
+
     def corner(sx, sy, k):
-        return cs[sx][sy][:, W * k : W * k + W]
+        if k == 4:
+            return cs[sx][4][:, W * sy : W * sy + W]
+        return cs[sx][2 * sy + k // 2][:, W * (k % 2) : W * (k % 2) + W]
 
     for n, (ref, dst) in enumerate(((ham, xh), (dens, xd))):
-        put_strips(dst, ref, pattern)
+        put_strips(dst, ref)
         put_shared(dst)
         for side in range(2):
             m = ys[side]
@@ -232,20 +292,19 @@
                 dst,
                 side,
                 line,
-                lambda x, x2, m=m, n=n: m[14 if x == 0 else 15][:, W * n : W * n + W],
+                lambda x, x2, m=m, n=n: m[13 if x == 0 else 14][:, W * n : W * n + W],
             )
         for side in range(2):
             put_x(dst, side, line_blocks(xm[side], n, [corner(side, t, n + 1) for t in range(2)]))
     for x in range(4):
-        masks = window_mask(kept, x)
         for p in range(2):
-            keep = both_rows(masks, p)
+            mask = both_rows(wide, x, p)
             lh = xh[p, x + 1, 64:192, :]
             ld = xd[p, x + 1, 64:192, :]
             for e in range(-1, 2):
                 cols = slice(256 * (e + 1), 256 * (e + 2))
-                a = dense_product(lh, xd, p, x, e) * keep[:, cols]
-                b = dense_product(ld, xh, p, x, e) * keep[:, cols]
+                a = dense_product(lh, xd, p, x, e) * mask[:, cols]
+                b = dense_product(ld, xh, p, x, e) * mask[:, cols]
                 a_rows[p, x, :, cols] = a.astype(BF)
                 xs[p, x + 1, 64:192, cols] = (a + b).astype(BF)
     put_shared(xs)
@@ -269,12 +328,11 @@
             a, b, c, d = (hx, hp), (hx, ep), (ex, hp), (ex, ep)
             halo, brick = (hx, None), (ex, None)
             xt, yt = xm[sx], ys[sy]
-            ba = xt[13][:, :W] if sy == 0 else xt[11][:, W:]
-            ca = yt[13][:, :W] if sx == 0 else yt[11][:, W:]
-            keep_ba = xt[13][32 * sy : 32 * sy + 1, W:].astype(F32)
-            keep_bc = xt[13][32 * sy + 16 : 32 * sy + 17, W:].astype(F32)
-            keep_ca = yt[13][32 * sx : 32 * sx + 1, W:].astype(F32)
-            s_ba = ba.astype(F32) + corner(sx, sy, 4).astype(F32).T + through(b, brick, a) * keep_ba
+            ca = cys[sy][sx, 1][:, W:]
+            keep_ba = xt[12][32 * sy : 32 * sy + 1, W:].astype(F32)
+            keep_bc = xt[12][32 * sy + 16 : 32 * sy + 17, W:].astype(F32)
+            keep_ca = yt[12][32 * sx : 32 * sx + 1, W:].astype(F32)
+            s_ba = corner(sx, sy, 4).astype(F32).T + through(b, brick, a) * keep_ba
             s_ca = (
                 ca.astype(F32)
                 + corner(sx, sy, 3).astype(F32).T
@@ -294,28 +352,31 @@
             ),
         )
     for x in range(4):
-        masks = window_mask(kept, x)
         for p in range(2):
-            keep = both_rows(masks, p)
+            mask = both_rows(wide, x, p)
             la = a_rows[p, x]
             ld = xd[p, x + 1, 64:192, :]
             for e in range(-1, 2):
                 cols = slice(256 * (e + 1), 256 * (e + 2))
                 cubic = dense_product(la, xd, p, x, e) + dense_product(ld, xs, p, x, e)
                 linear = xs[p, x + 1, 64:192, cols].astype(F32)
-                total = ((3.0 * linear - 2.0 * cubic) * keep[:, cols]).astype(BF)
+                total = ((3.0 * linear - 2.0 * cubic) * mask[:, cols]).astype(BF)
                 first = slice(192 * (e + 1), 192 * (e + 2))
                 out[x, 2 * p, :, first] = total[0:64, 0:192]
                 out[x, 2 * p + 1, :, first] = total[64:128, 64:256]
 
 
-def call(kernel, outs, scratch=()):
+def call(kernel, outs, scratch=(), inputs=pl.no_block_spec, limit=48):
+    def shape(s):
+        return s if isinstance(s, jax.ShapeDtypeStruct) else jax.ShapeDtypeStruct(s, BF)
+
     return pl.pallas_call(
         kernel,
-        out_shape=[jax.ShapeDtypeStruct(s, BF) for s in outs],
+        out_shape=[shape(s) for s in outs],
+        in_specs=inputs,
         out_specs=[VMEM] * len(outs),
-        scratch_shapes=[pltpu.VMEM(s, BF) for s in scratch],
-        compiler_params=pltpu.CompilerParams(vmem_limit_bytes=48 * 1024 * 1024),
+        scratch_shapes=[pltpu.VMEM(s, BF) if isinstance(s, tuple) else s for s in scratch],
+        compiler_params=pltpu.CompilerParams(vmem_limit_bytes=limit * 1024 * 1024),
     )
 
 
@@ -326,20 +387,35 @@
 
 def per_device(ham, dens, pattern, kept):
     dense = (2, 6, 256, 768)
-    corner, y_line, x_line = (2, W, 384), (16, W, 128), (14, W, 128)
-    cy_up, cy_down, y_up, y_down, x_up, x_down = call(
-        local_kernel, [corner, corner, y_line, y_line, x_line, x_line], [dense] * 3
-    )(ham, dens, pattern, kept)
+    corner, y_line, x_line = (2, 3, W, 128), (15, W, 128), (13, W, 128)
+    mask = pltpu.VMEM(pattern.shape, pattern.dtype)
+    flags = pltpu.VMEM((4, 4, 9 * W), F32)
+    inputs = [pltpu.with_memory_space_constraint(v, pltpu.HBM) for v in (ham, dens, pattern, kept)]
+    cy_up, cy_down, ends, y_up, y_down, x_up, x_down, ham, dens, wide = call(
+        send_kernel,
+        [corner, corner, (2, 2, W, W), y_line, y_line, x_line, x_line, ham.shape, dens.shape]
+        + [jax.ShapeDtypeStruct((4, 2, 4, 12 * W), F32)],
+        [ham.shape, dens.shape, mask, mask, flags, flags]
+        + [pltpu.SemaphoreType.DMA((2, 4)), pltpu.SemaphoreType.DMA((2,))],
+        [pl.BlockSpec(memory_space=pl.ANY)] * 4,
+        16,
+    )(*inputs)
     cy_low = shift(cy_up, "gy", 1)
     cy_high = shift(cy_down, "gy", -1)
+    x_high = shift(x_down, "gx", -1)
     x_low = shift(x_up, "gx", 1)
     y_low = shift(y_up, "gy", 1)
+    y_down, y_low = lax.optimization_barrier((y_down, y_low))
     y_high = shift(y_down, "gy", -1)
-    x_high = shift(x_down, "gx", -1)
-    c_low = shift(jnp.stack([cy_low[1], cy_high[1]]), "gx", 1)
-    c_high = shift(jnp.stack([cy_low[0], cy_high[0]]), "gx", -1)
+
+    def forward(n):
+        sums = [v[n, 2, :, :W] + ends[s, n] for s, v in enumerate((cy_low, cy_high))]
+        return jnp.concatenate([cy_low[n, :2], cy_high[n, :2], jnp.concatenate(sums, axis=1)[None]])
+
+    c_high = shift(forward(0), "gx", -1)
+    c_low = shift(forward(1), "gx", 1)
     return call(last_kernel, [ham.shape], [dense] * 3 + [(2, 4, 128, 768)])(
-        ham, dens, pattern, kept, y_low, y_high, x_low, x_high, c_low, c_high
+        ham, dens, wide, y_low, y_high, x_low, x_high, cy_low, cy_high, c_low, c_high
     )[0]
 
 

time: 40.8 us -> 31.3 us (0.77)
  starting transfers between devices: 14.6 us -> 9.94 us
  local copies, waits for them, and re-layouts: 4.05 us -> 0.01 us
  Pallas kernels: 12.1 us -> 11.5 us
    ppermute x8, starting transfers between devices: 14.6 us -> 9.94 us  [shift(): lax.ppermute(value, axis, [(i, (i + step) % count) for i in range(count)])]
    unnamed x8 -> x0, local copies, waits for them, and re-layouts: 4.02 us -> none
    pallas_call x1, Pallas kernels: 8.47 us -> 7.62 us  [per_device(): call(last_kernel, [ham.shape], [dense] * 3 + [(2, 4, 128, 768)])]
  transfers between devices with their start and end apart: 8 -> 8, of which waited for: 2 -> 3; matrix products, arithmetic and copies ran while one was open for 0% -> 1% of each run, Pallas kernels for 0% -> 0%
where the time goes in v3:
time: 31.3 us; the launch traced here: 31.1 us
  Pallas kernels  11.5 us (37%)
  starting transfers between devices  9.94 us (32%)
  waiting for transfers between devices  9.38 us (30%)
    ppermute x8, starting transfers between devices, shift(): lax.ppermute(value, axis, [(i, (i + step) % count) for i in range(count)])  9.94 us
    ppermute x8, waiting for transfers between devices, shift(): lax.ppermute(value, axis, [(i, (i + step) % count) for i in range(count)])  9.38 us
    pallas_call x1, Pallas kernels, per_device(): call(last_kernel, [ham.shape], [dense] * 3 + [(2, 4, 128, 768)])  7.62 us
    pallas_call x1, Pallas kernels, per_device(): call(send_kernel, [corner, corner, (2, 2, W, W), y_line, y_line, x_line,...  3.92 us
  transfers between devices with their start and end apart: 8, of which 3 were waited for; matrix products, arithmetic and copies ran while one was open for 1% of the time, Pallas kernels for 0%

profile of v3, /device:TPU:0, one launch (start us, length us, event | category | flops | bytes accessed | tf_op | source)
XLA Modules:
  0.0 31.1 jit_solution(16584559970335471000)
XLA Ops:
  0.0 3.9 %shard_map.46 = (bf16[2,3,64,128]{3,2,1,0:T(8,128)(2,1)S(1)}, bf16[2,3,64,128]{3,2,1,0:T(8,128)(2,1)S(1)}, bf16[2,2,64,64]{3,2,1,0:T(8,128)(2,1)S(1)}, bf16[15,6...) custom-call(bf16[4,4,64,576]{3,2,1,0:T(8,128)(2,1)} %ham.1, ...), custom_call_target="tpu_custom_call" | custom-call | tf_op jit(solution)/shard_map/pallas_call | solution.py:394
  3.9 0.5 %collective-permute-start.4 = (bf16[2,3,64,128]{3,2,1,0:T(8,128)(2,1)S(1)}, bf16[2,3,64,128]{3,2,1,0:T(8,128)(2,1)S(1)}, u32[]{:S(2)}, u32[]{:S(2)}) collective-permute-start(bf16[2,3,64,128]{3,2,1,0:T(8,128)(2,1)S(1)} %get-tuple-element.26), channel_id=1, source_target_pairs={{0,1},{1,2},{2,3},{3,0},{4,5},{5,6},{6,7},{7,4},{8,9},{9,10},{10,1... | collective-permute-start | bytes 294920 | tf_op jit(solution)/shard_map/ppermute | solution.py:385
  4.4 2.0 %collective-permute-start.5 = (bf16[2,3,64,128]{3,2,1,0:T(8,128)(2,1)S(1)}, bf16[2,3,64,128]{3,2,1,0:T(8,128)(2,1)S(1)}, u32[]{:S(2)}, u32[]{:S(2)}) collective-permute-start(bf16[2,3,64,128]{3,2,1,0:T(8,128)(2,1)S(1)} %get-tuple-element.27), channel_id=1, source_target_pairs={{0,3},{1,0},{2,1},{3,2},{4,7},{5,4},{6,5},{7,6},{8,11},{9,8},{10,9... | collective-permute-start | bytes 294920 | tf_op jit(solution)/shard_map/ppermute | solution.py:385
  6.4 2.3 %collective-permute-start.2 = (bf16[13,64,128]{2,1,0:T(8,128)(2,1)S(1)}, bf16[13,64,128]{2,1,0:T(8,128)(2,1)S(1)}, u32[]{:S(2)}, u32[]{:S(2)}) collective-permute-start(bf16[13,64,128]{2,1,0:T(8,128)(2,1)S(1)} %get-tuple-element.24), channel_id=1, source_target_pairs={{0,4},{4,8},{8,12},{12,16},{16,20},{20,24},{24,28},{28,0},{1,5},{5... | collective-permute-start | bytes 638984 | tf_op jit(solution)/shard_map/ppermute | solution.py:385
  8.7 3.0 %collective-permute-start.3 = (bf16[13,64,128]{2,1,0:T(8,128)(2,1)S(1)}, bf16[13,64,128]{2,1,0:T(8,128)(2,1)S(1)}, u32[]{:S(2)}, u32[]{:S(2)}) collective-permute-start(bf16[13,64,128]{2,1,0:T(8,128)(2,1)S(1)} %get-tuple-element.25), channel_id=1, source_target_pairs={{0,28},{4,0},{8,4},{12,8},{16,12},{20,16},{24,20},{28,24},{1,29},{... | collective-permute-start | bytes 638984 | tf_op jit(solution)/shard_map/ppermute | solution.py:385
  11.7 0.0 collective-permute-start
  11.7 0.0 collective-permute-done.4.cy_low
  11.8 0.0 collective-permute-done.5.cy_high
  11.8 0.1 maximum_bitcast_fusion
  11.9 0.1 collective-permute-start.6
  12.0 5.4 %collective-permute-done.y_low = bf16[15,64,128]{2,1,0:T(8,128)(2,1)S(1)} collective-permute-done((bf16[15,64,128]{2,1,0:T(8,128)(2,1)S(1)}, bf16[15,64,128]{2,1,0:T(8,128)(2,1)S(1)}, u32[]{:S(2)}, u32[]{:S(2)}) %collective-permute-start) | collective-permute-done | bytes 245792 | tf_op jit(solution)/shard_map/ppermute | solution.py:385
  17.4 0.0 collective-permute-start.1
  17.4 0.1 maximum_bitcast_fusion.1
  17.5 2.1 %collective-permute-start.7 = (bf16[5,64,128]{2,1,0:T(8,128)(2,1)S(1)}, bf16[5,64,128]{2,1,0:T(8,128)(2,1)S(1)}, u32[]{:S(2)}, u32[]{:S(2)}) collective-permute-start(bf16[5,64,128]{2,1,0:T(8,128)(2,1)S(1)} %pad_maximum_fusion.1), channel_id=1, source_target_pairs={{0,28},{4,0},{8,4},{12,8},{16,12},{20,16},{24,20},{28,24},{1,29},{... | collective-permute-start | bytes 245768 | tf_op jit(solution)/shard_map/ppermute | solution.py:385
  19.5 1.8 %collective-permute-done.6.c_low = bf16[5,64,128]{2,1,0:T(8,128)(2,1)S(1)} collective-permute-done((bf16[5,64,128]{2,1,0:T(8,128)(2,1)S(1)}, bf16[5,64,128]{2,1,0:T(8,128)(2,1)S(1)}, u32[]{:S(2)}, u32[]{:S(2)}) %collective-permute-start.6) | collective-permute-done | bytes 81952 | tf_op jit(solution)/shard_map/ppermute | solution.py:385
  21.3 2.2 %collective-permute-done.7.c_high = bf16[5,64,128]{2,1,0:T(8,128)(2,1)S(1)} collective-permute-done((bf16[5,64,128]{2,1,0:T(8,128)(2,1)S(1)}, bf16[5,64,128]{2,1,0:T(8,128)(2,1)S(1)}, u32[]{:S(2)}, u32[]{:S(2)}) %collective-permute-start.7) | collective-permute-done | bytes 81952 | tf_op jit(solution)/shard_map/ppermute | solution.py:385
  23.5 0.0 collective-permute-done.2.x_low
  23.5 0.0 collective-permute-done.3.x_high
  23.5 0.0 collective-permute-done.1.y_high
  23.5 7.6 %shard_map.47 = bf16[4,4,64,576]{3,2,1,0:T(8,128)(2,1)} custom-call(bf16[4,4,64,576]{3,2,1,0:T(8,128)(2,1)S(1)} %get-tuple-element.17.ham, bf16[4,4,64,576]{3,2,1,0:T(8,128)(2,1)S(1)} %get-tuple-element.18.dens, f32[4,2,4,768]{3,2,1,0:T(4,128)S(1)} %get-tuple-element.19.wide, bf16[15,64,128]{2,1,0:T(8,128)(2,1)S(1)} %collective-permute-done.y_low, ...), custom_call_target="tpu_custom_call" | custom-call | tf_op jit(solution)/shard_map/pallas_call | solution.py:417
  (5 shorter events, 0.0 us)
Async XLA Ops:
  3.9 7.8 %collective-permute-start.4 = (bf16[2,3,64,128]{3,2,1,0:T(8,128)(2,1)S(1)}, bf16[2,3,64,128]{3,2,1,0:T(8,128)(2,1)S(1)}, u32[]{:S(2)}, u32[]{:S(2)}) collective-permute-start(bf16[2,3,64,128]{3,2,1,0:T(8,128)(2,1)S(1)} %get-tuple-element.26), channel_id=1, source_target_pairs={{0,1},{1,2},{2,3},{3,0},{4,5},{5,6},{6,7},{7,4},{8,9},{9,10},{10,1... | collective-permute-start | bytes 294920 | tf_op jit(solution)/shard_map/ppermute | solution.py:385
  4.4 7.3 %collective-permute-start.5 = (bf16[2,3,64,128]{3,2,1,0:T(8,128)(2,1)S(1)}, bf16[2,3,64,128]{3,2,1,0:T(8,128)(2,1)S(1)}, u32[]{:S(2)}, u32[]{:S(2)}) collective-permute-start(bf16[2,3,64,128]{3,2,1,0:T(8,128)(2,1)S(1)} %get-tuple-element.27), channel_id=1, source_target_pairs={{0,3},{1,0},{2,1},{3,2},{4,7},{5,4},{6,5},{7,6},{8,11},{9,8},{10,9... | collective-permute-start | bytes 294920 | tf_op jit(solution)/shard_map/ppermute | solution.py:385
  6.4 17.1 %collective-permute-start.2 = (bf16[13,64,128]{2,1,0:T(8,128)(2,1)S(1)}, bf16[13,64,128]{2,1,0:T(8,128)(2,1)S(1)}, u32[]{:S(2)}, u32[]{:S(2)}) collective-permute-start(bf16[13,64,128]{2,1,0:T(8,128)(2,1)S(1)} %get-tuple-element.24), channel_id=1, source_target_pairs={{0,4},{4,8},{8,12},{12,16},{16,20},{20,24},{24,28},{28,0},{1,5},{5... | collective-permute-start | bytes 638984 | tf_op jit(solution)/shard_map/ppermute | solution.py:385
  8.7 14.8 %collective-permute-start.3 = (bf16[13,64,128]{2,1,0:T(8,128)(2,1)S(1)}, bf16[13,64,128]{2,1,0:T(8,128)(2,1)S(1)}, u32[]{:S(2)}, u32[]{:S(2)}) collective-permute-start(bf16[13,64,128]{2,1,0:T(8,128)(2,1)S(1)} %get-tuple-element.25), channel_id=1, source_target_pairs={{0,28},{4,0},{8,4},{12,8},{16,12},{20,16},{24,20},{28,24},{1,29},{... | collective-permute-start | bytes 638984 | tf_op jit(solution)/shard_map/ppermute | solution.py:385
  11.7 5.6 %collective-permute-start = (bf16[15,64,128]{2,1,0:T(8,128)(2,1)S(1)}, bf16[15,64,128]{2,1,0:T(8,128)(2,1)S(1)}, u32[]{:S(2)}, u32[]{:S(2)}) collective-permute-start(bf16[15,64,128]{2,1,0:T(8,128)(2,1)S(1)} %get-tuple-element.21), channel_id=1, source_target_pairs={{0,1},{1,2},{2,3},{3,0},{4,5},{5,6},{6,7},{7,4},{8,9},{9,10},{10,1... | collective-permute-start | bytes 737288 | tf_op jit(solution)/shard_map/ppermute | solution.py:385
  11.9 9.4 %collective-permute-start.6 = (bf16[5,64,128]{2,1,0:T(8,128)(2,1)S(1)}, bf16[5,64,128]{2,1,0:T(8,128)(2,1)S(1)}, u32[]{:S(2)}, u32[]{:S(2)}) collective-permute-start(bf16[5,64,128]{2,1,0:T(8,128)(2,1)S(1)} %pad_maximum_fusion), channel_id=1, source_target_pairs={{0,4},{4,8},{8,12},{12,16},{16,20},{20,24},{24,28},{28,0},{1,5},{5... | collective-permute-start | bytes 245768 | tf_op jit(solution)/shard_map/ppermute | solution.py:385
  17.4 6.2 %collective-permute-start.1 = (bf16[15,64,128]{2,1,0:T(8,128)(2,1)S(1)}, bf16[15,64,128]{2,1,0:T(8,128)(2,1)S(1)}, u32[]{:S(2)}, u32[]{:S(2)}) collective-permute-start(bf16[15,64,128]{2,1,0:T(8,128)(2,1)S(1)} %get-tuple-element.23), channel_id=1, source_target_pairs={{0,3},{1,0},{2,1},{3,2},{4,7},{5,4},{6,5},{7,6},{8,11},{9,8},{10,9... | collective-permute-start | bytes 737288 | tf_op jit(solution)/shard_map/ppermute | solution.py:385
  17.5 6.1 %collective-permute-start.7 = (bf16[5,64,128]{2,1,0:T(8,128)(2,1)S(1)}, bf16[5,64,128]{2,1,0:T(8,128)(2,1)S(1)}, u32[]{:S(2)}, u32[]{:S(2)}) collective-permute-start(bf16[5,64,128]{2,1,0:T(8,128)(2,1)S(1)} %pad_maximum_fusion.1), channel_id=1, source_target_pairs={{0,28},{4,0},{8,4},{12,8},{16,12},{20,16},{24,20},{28,24},{1,29},{... | collective-permute-start | bytes 245768 | tf_op jit(solution)/shard_map/ppermute | solution.py:385

commit v4 on v3

--- a/solution.py
+++ b/solution.py
@@ -76,54 +76,41 @@
             dst[0, i, 192:256, c : c + 128] = zero
 
 
-def put_y(dst, side, along=None, across=None):
+def put_y(dst, side, along, across=None):
     zero = jnp.zeros((W, W), BF)
     y, halo = (0, -1) if side == 0 else (3, 4)
     for x in range(4):
         for d in (-1, 0, 1):
             x2 = x + d
-            same = zero if along is None else along(x, x2)
-            if 0 <= x2 < 4:
-                inner = block(dst, x2, y, x, halo).T
-            else:
-                inner = zero if across is None else across(x, x2)
+            inside = 0 <= x2 < 4
+            if not inside and across is None:
+                continue
+            same = along(x, x2)
+            inner = block(dst, x2, y, x, halo).T if inside else across(x, x2)
             rest = jnp.zeros((W, 128), BF)
             parts = [same, inner, rest] if side == 0 else [rest, inner, same]
             c = 256 * (d + 1)
             dst[side, x + 1, 192 * side : 192 * side + W, c : c + 256] = jnp.concatenate(parts, axis=1)
 
 
-def put_x(dst, side, within=None):
-    zero = jnp.zeros((W, W), BF)
-    at, edge, out, back = (0, 1, 0, 2) if side == 0 else (5, 4, 2, 0)
-    for p in range(2):
-        if within is not None:
-            first = 2 * p - 1
-            rows = [
-                jnp.concatenate(
-                    [
-                        within(first + i, first + j) if abs(i - j) <= 1 else zero
-                        for j in range(4)
-                    ],
-                    axis=1,
-                )
-                for i in range(4)
-            ]
-            dst[p, at, :, 256:512] = jnp.concatenate(rows, axis=0)
-        else:
-            dst[p, at, :, 256:512] = jnp.zeros((256, 256), BF)
-        dst[p, at, :, 256 * back : 256 * back + 256] = dst[
-            p, edge, :, 256 * out : 256 * out + 256
-        ].T
-
-
-def dense_product(left, right, p, x, e, cols=(0, 256)):
+def lower_blocks(places):
+    row = lax.broadcasted_iota(jnp.int32, (256, 256), 0) // W
+    col = lax.broadcasted_iota(jnp.int32, (256, 256), 1) // W
+    hit = None
+    for i, j in places:
+        here = (row == i) & (col == j)
+        hit = here if hit is None else hit | here
+    return hit.astype(BF)
+
+
+def dense_product(left, right, p, x, e, brick=False):
     total = None
     for d in range(max(-1, e - 1), min(1, e + 1) + 1):
-        c = 256 * (e - d + 1)
+        if brick and not 0 <= x + d < 4:
+            continue
         term = jnp.dot(
             left[:, 256 * (d + 1) : 256 * (d + 2)],
-            right[p, x + 1 + d, :, c + cols[0] : c + cols[1]],
+            right[p, x + 1 + d, :, 256 * (e - d + 1) : 256 * (e - d + 2)],
             preferred_element_type=F32,
         )
         total = term if total is None else total + term
@@ -143,7 +130,7 @@
 
 
 def send_kernel(
-    ham, dens, pattern, kept, cy_up, cy_down, ends, y_up, y_down, x_up, x_down, hm, dm, wide,
+    ham, dens, pattern, kept, ends, cy_up, cy_down, y_up, y_down, x_up, x_down, hm, dm, wide,
     hb, db, pb, kb, live, keep, sems, mask_sems,
 ):
     masks = [
@@ -216,10 +203,11 @@
     selfs = {(x, y): own(x, y) for x in range(4) for y in range(4) if x in (0, 3) or y in (0, 3)}
     for y, out, dy in ((3, cy_up, 1), (0, cy_down, -1)):
         for n, (x, dx) in enumerate(((0, -1), (3, 1))):
-            across = through(x, y, ((x, y), (x - dx, y)), 0, dy)
-            out[n, 0] = pair(selfs[x, y], get(hm, x, y, 0, 0))
-            out[n, 1] = pair(get(dm, x, y, 0, 0), through(x, y, ((x, y), (x, y - dy)), dx, 0))
-            out[n, 2] = pair(across, jnp.zeros((W, W), BF))
+            across = through(x, y, ((x - dx, y),), 0, dy)
+            along = through(x, y, ((x, y - dy),), dx, 0)
+            out[3 * n] = pair(selfs[x, y], get(hm, x, y, 0, 0))
+            out[3 * n + 1] = pair(get(dm, x, y, 0, 0), along)
+            out[3 * n + 2] = pair(across, along.T)
             ends[0 if y == 0 else 1, n] = across.T
 
     def line(out, cell, step, marks):
@@ -271,102 +259,216 @@
     return get
 
 
-def last_kernel(
-    ham, dens, wide, y_low, y_high, x_low, x_high, cy_low, cy_high, c_low, c_high,
-    out, xh, xd, xs, a_rows,
+def edge(side):
+    return (0, 0, 1, 2) if side == 0 else (3, 2, 1, 0)
+
+
+def part(n):
+    return slice(256 * n, 256 * n + 256)
+
+
+def unpack_rows(total, p, x, e, out):
+    cols = slice(192 * (e + 1), 192 * (e + 2))
+    out[x, 2 * p, :, cols] = total[0:64, 0:192]
+    out[x, 2 * p + 1, :, cols] = total[64:128, 64:256]
+
+
+def middle_kernel(
+    ham, dens, wide, y_low, y_high, out, h_edge, d_edge, h_back, d_back, a_edge, g_edge, done_edge,
+    xh, xd, xs, a_rows, rows, sems,
 ):
-    ys, xm, cys, cs = (y_low, y_high), (x_low, x_high), (cy_low, cy_high), (c_low, c_high)
-
-    def corner(sx, sy, k):
-        if k == 4:
-            return cs[sx][4][:, W * sy : W * sy + W]
-        return cs[sx][2 * sy + k // 2][:, W * (k % 2) : W * (k % 2) + W]
-
-    for n, (ref, dst) in enumerate(((ham, xh), (dens, xd))):
+    ys = (y_low, y_high)
+    for n, (ref, dst, keep, turned) in enumerate(
+        ((ham, xh, h_edge, h_back), (dens, xd, d_edge, d_back))
+    ):
         put_strips(dst, ref)
         put_shared(dst)
         for side in range(2):
             m = ys[side]
-            line = line_blocks(m, n, None)
             put_y(
                 dst,
                 side,
-                line,
+                line_blocks(m, n, None),
                 lambda x, x2, m=m, n=n: m[13 if x == 0 else 14][:, W * n : W * n + W],
             )
         for side in range(2):
-            put_x(dst, side, line_blocks(xm[side], n, [corner(side, t, n + 1) for t in range(2)]))
+            x, go, _, back = edge(side)
+            for p in range(2):
+                tile = dst[p, x + 1, :, part(go)].T
+                dst[p, 5 * side, :, part(back)] = tile
+                turned[side, p] = tile
+                keep[side, p] = dst[p, x + 1]
     for x in range(4):
         for p in range(2):
             mask = both_rows(wide, x, p)
             lh = xh[p, x + 1, 64:192, :]
             ld = xd[p, x + 1, 64:192, :]
             for e in range(-1, 2):
-                cols = slice(256 * (e + 1), 256 * (e + 2))
-                a = dense_product(lh, xd, p, x, e) * mask[:, cols]
-                b = dense_product(ld, xh, p, x, e) * mask[:, cols]
-                a_rows[p, x, :, cols] = a.astype(BF)
-                xs[p, x + 1, 64:192, cols] = (a + b).astype(BF)
+                if 0 <= x + e < 4:
+                    cols = part(e + 1)
+                    a = dense_product(lh, xd, p, x, e) * mask[:, cols]
+                    b = dense_product(ld, xh, p, x, e) * mask[:, cols]
+                    a_rows[p, x, :, cols] = a.astype(BF)
+                    xs[p, x + 1, 64:192, cols] = (a + b).astype(BF)
     put_shared(xs)
-    firsts = {}
-    for sx in range(2):
-        hx, ex, go, back = (0, 1, 0, 2) if sx == 0 else (5, 4, 2, 0)
-        for sy in range(2):
-            hp, ep, base = (0, 1, 0) if sy == 0 else (3, 2, 128)
-
-            def at(m, k, f):
-                part = 256 * (f[0] - k[0] + 1)
-                rows = slice(base, base + 128) if k[1] is None else slice(W * k[1], W * k[1] + W)
-                start = part + (base if f[1] is None else W * f[1])
-                return m[sy, k[0], rows, start : start + (128 if f[1] is None else W)]
-
-            def through(k, m, f):
-                return jnp.dot(
-                    at(xh, k, m), at(xd, m, f), preferred_element_type=F32
-                ) + jnp.dot(at(xd, k, m), at(xh, m, f), preferred_element_type=F32)
-
-            a, b, c, d = (hx, hp), (hx, ep), (ex, hp), (ex, ep)
-            halo, brick = (hx, None), (ex, None)
-            xt, yt = xm[sx], ys[sy]
-            ca = cys[sy][sx, 1][:, W:]
-            keep_ba = xt[12][32 * sy : 32 * sy + 1, W:].astype(F32)
-            keep_bc = xt[12][32 * sy + 16 : 32 * sy + 17, W:].astype(F32)
-            keep_ca = yt[12][32 * sx : 32 * sx + 1, W:].astype(F32)
-            s_ba = corner(sx, sy, 4).astype(F32).T + through(b, brick, a) * keep_ba
-            s_ca = (
-                ca.astype(F32)
-                + corner(sx, sy, 3).astype(F32).T
-                + (through(c, b, a) + through(c, d, a)) * keep_ca
-            )
-            s_bc = (through(b, halo, c) + through(b, brick, c)) * keep_bc
-            firsts[sx, sy] = s_ba.astype(BF), s_ca.astype(BF), s_bc.astype(BF).T
-    for sy in range(2):
-        line = line_blocks(ys[sy], 2, None, firsts[0, sy][1], firsts[1, sy][1])
-        put_y(xs, sy, line, lambda x, x2, sy=sy: firsts[0 if x == 0 else 1, sy][2])
-    for sx in range(2):
-        put_x(
-            xs,
-            sx,
-            line_blocks(
-                xm[sx], 2, [corner(sx, t, 0) for t in range(2)], firsts[sx, 0][0], firsts[sx, 1][0]
-            ),
-        )
-    for x in range(4):
+    for side in range(2):
+        put_y(xs, side, line_blocks(ys[side], 2, None))
+        for p in range(2):
+            x = edge(side)[0]
+            a_edge[side, p] = a_rows[p, x, :, part(1)]
+    for x in (1, 2, 0, 3):
         for p in range(2):
             mask = both_rows(wide, x, p)
             la = a_rows[p, x]
             ld = xd[p, x + 1, 64:192, :]
             for e in range(-1, 2):
-                cols = slice(256 * (e + 1), 256 * (e + 2))
-                cubic = dense_product(la, xd, p, x, e) + dense_product(ld, xs, p, x, e)
-                linear = xs[p, x + 1, 64:192, cols].astype(F32)
-                total = ((3.0 * linear - 2.0 * cubic) * mask[:, cols]).astype(BF)
-                first = slice(192 * (e + 1), 192 * (e + 2))
-                out[x, 2 * p, :, first] = total[0:64, 0:192]
-                out[x, 2 * p + 1, :, first] = total[64:128, 64:256]
-
-
-def call(kernel, outs, scratch=(), inputs=pl.no_block_spec, limit=48):
+                if not 0 <= x + e < 4:
+                    continue
+                cols = part(e + 1)
+                cubic = dense_product(la, xd, p, x, e, True) + dense_product(ld, xs, p, x, e, True)
+                total = 3.0 * xs[p, x + 1, 64:192, cols].astype(F32) - 2.0 * cubic
+                if x in (1, 2):
+                    unpack_rows((total * mask[:, cols]).astype(BF), p, x - 1, e, rows)
+                elif e == 0:
+                    g_edge[x // 3, p] = total
+                else:
+                    done_edge[x // 3, p] = (total * mask[:, cols]).astype(BF)
+        if x == 2:
+            copy = pltpu.make_async_copy(rows, out.at[1:3], sems.at[0])
+            copy.start()
+    copy.wait()
+
+
+def last_kernel(
+    wide, y_low, y_high, cy_low, cy_high, x_low, x_high, c_low, h_edge, d_edge, h_back, d_back, a_edge, g_edge,
+    done_edge, given, out, hh, dh, sh, ss, sb, u, a_go, rows, sems,
+):
+    ys, cys, xm, cs = (y_low, y_high), (cy_low, cy_high), (x_low, x_high), (c_low, x_high.at[13:18])
+    both = [(sx, p) for sx in range(2) for p in range(2)]
+
+    def corner(sx, sy, k):
+        if k == 4:
+            return cs[sx][4][:, W * sy : W * sy + W]
+        return cs[sx][2 * sy + k // 2][:, W * (k % 2) : W * (k % 2) + W]
+
+    def dot(left, right):
+        return jnp.dot(left, right, preferred_element_type=F32)
+
+    def fill(dst, sx, n, corners, crossing):
+        msg, base = xm[sx], 4 * n if n < 2 else 9
+        for p in range(2):
+            u[sx, p, :, :] = jnp.zeros((256, 256), BF)
+            for i in range(4):
+                y = 2 * p - 1 + i
+                at = slice(W * i, W * i + W)
+                if y in (-1, 4):
+                    u[sx, p, at, at] = corners[p]
+                    continue
+                whole = i < 3 and not (n == 2 and y == 3)
+                u[sx, p, at, W * i : W * i + W * (2 if whole else 1)] = (
+                    msg[base + y] if whole else msg[base + y][:, :W]
+                )
+            places = crossing(u, p)
+            tile = u[sx, p]
+            dst[sx, p] = tile + tile.T * lower_blocks(places)
+
+    def crossing_of(sx, n):
+        def put(u, p):
+            if p == 1:
+                return ((1, 0), (2, 1), (3, 2))
+            u[sx, 0, 64:128, 0:64] = xm[sx][8][:, W * n : W * n + W]
+            return ((0, 1), (2, 1), (3, 2))
+
+        return put
+
+    for sx in range(2):
+        for n, halo in enumerate((hh, dh)):
+            fill(halo, sx, n, [corner(sx, t, n + 1) for t in range(2)], crossing_of(sx, n))
+    for sx, p in both:
+        x, go, _, back = edge(sx)
+        mask = both_rows(wide, x, p)[:, part(go)]
+
+        def to_halo(left, right, halo):
+            left = left[sx, p, 64:192, :]
+            return dot(left[:, part(go)], halo[sx, p]) + dot(
+                left[:, part(1)], right[sx, p, :, part(go)]
+            )
+
+        a = to_halo(h_edge, d_edge, dh) * mask
+        b = to_halo(d_edge, h_edge, hh) * mask
+        a_go[sx, p] = a.astype(BF)
+        ss[sx, p, 64:192, :] = (a + b).astype(BF)
+    z2 = jnp.zeros((W, 128), BF)
+    ab = {}
+    for sx, sy in both:
+        x, go, _, back = edge(sx)
+        two = slice(128 * sy, 128 * sy + 128)
+        hp, ep = (0, 1) if sy == 0 else (1, 0)
+
+        def four(row, halo, back_tile):
+            def cols(n):
+                return slice(256 * n + 128 * sy, 256 * n + 128 * sy + 128)
+
+            top = [halo[sx, sy, two, two], back_tile[sx, sy, two, two]]
+            low = [row[sx, sy, two, cols(go)], row[sx, sy, two, cols(1)]]
+            return jnp.concatenate(
+                [jnp.concatenate(top, axis=1), jnp.concatenate(low, axis=1)], axis=0
+            )
+
+        qh, qd = four(h_edge, hh, h_back), four(d_edge, dh, d_back)
+        q = dot(jnp.concatenate([qh, qd], axis=1), jnp.concatenate([qd, qh], axis=0))
+
+        def blk(i, j):
+            return q[W * i : W * i + W, W * j : W * j + W]
+
+        a, b, c = hp, ep, 2 + hp
+        xt, yt = xm[sx], ys[sy]
+        keep_ba = xt[12][32 * sy : 32 * sy + 1, W:].astype(F32)
+        keep_bc = xt[12][32 * sy + 16 : 32 * sy + 17, W:].astype(F32)
+        keep_ca = yt[12][32 * sx : 32 * sx + 1, W:].astype(F32)
+        ab[sx, sy] = (corner(sx, sy, 4).astype(F32) + keep_ba * blk(a, b)).astype(BF)
+        ca = cys[sy][1 + 3 * sx][:, W:].astype(F32) + corner(sx, sy, 3).astype(F32) + keep_ca * blk(c, a)
+        ca, cb = ca.astype(BF), (keep_bc * blk(c, b)).astype(BF)
+        here = slice(192 * sy, 192 * sy + W)
+        ss[sx, sy, here, :] = jnp.concatenate([ca, cb, z2] if sy == 0 else [z2, cb, ca], axis=1)
+    for sx in range(2):
+        ss[sx, 1, 0:64, :] = jnp.concatenate([ss[sx, 0, 128:192, 128:256], z2], axis=1)
+        ss[sx, 0, 192:256, :] = jnp.concatenate([z2, ss[sx, 1, 64:128, 0:128]], axis=1)
+
+        def put(u, p, sx=sx):
+            if p == 0:
+                u[sx, 0, 0:64, 64:128] = ab[sx, 0]
+                return ((1, 0), (2, 1), (3, 2))
+            u[sx, 1, 192:256, 128:192] = ab[sx, 1]
+            return ((1, 0), (2, 1), (2, 3))
+
+        fill(sh, sx, 2, [corner(sx, t, 0) for t in range(2)], put)
+        for p in range(2):
+            sb[sx, p] = ss[sx, p].T
+    copies = []
+    for sx, p in both:
+        x, go, _, back = edge(sx)
+        mask = both_rows(wide, x, p)
+        ld = d_edge[sx, p, 64:192, :]
+        outer = dot(a_go[sx, p], dh[sx, p]) + dot(ld[:, part(go)], sh[sx, p])
+        outer += dot(a_edge[sx, p], d_edge[sx, p, :, part(go)]) + dot(ld[:, part(1)], ss[sx, p])
+        outer = 3.0 * ss[sx, p, 64:192, :].astype(F32) - 2.0 * outer
+        same = dot(a_go[sx, p], d_back[sx, p]) + dot(ld[:, part(go)], sb[sx, p])
+        same = g_edge[sx, p] - 2.0 * same
+        unpack_rows((outer * mask[:, part(go)]).astype(BF), p, sx, go - 1, rows)
+        unpack_rows((same * mask[:, part(1)]).astype(BF), p, sx, 0, rows)
+        unpack_rows(done_edge[sx, p], p, sx, back - 1, rows)
+        if p == 1:
+            copies.append(pltpu.make_async_copy(rows.at[sx], out.at[x], sems.at[sx]))
+            copies[-1].start()
+    for copy in copies:
+        copy.wait()
+
+
+ANY = pl.BlockSpec(memory_space=pl.ANY)
+
+
+def call(kernel, outs, scratch, inputs, limit, spaces=None, aliases=None):
     def shape(s):
         return s if isinstance(s, jax.ShapeDtypeStruct) else jax.ShapeDtypeStruct(s, BF)
 
@@ -374,8 +476,9 @@
         kernel,
         out_shape=[shape(s) for s in outs],
         in_specs=inputs,
-        out_specs=[VMEM] * len(outs),
+        out_specs=spaces or [VMEM] * len(outs),
         scratch_shapes=[pltpu.VMEM(s, BF) if isinstance(s, tuple) else s for s in scratch],
+        input_output_aliases=aliases or {},
         compiler_params=pltpu.CompilerParams(vmem_limit_bytes=limit * 1024 * 1024),
     )
 
@@ -387,36 +490,55 @@
 
 def per_device(ham, dens, pattern, kept):
     dense = (2, 6, 256, 768)
-    corner, y_line, x_line = (2, 3, W, 128), (15, W, 128), (13, W, 128)
+    corner, y_line, x_line = (6, W, 128), (15, W, 128), (13, W, 128)
     mask = pltpu.VMEM(pattern.shape, pattern.dtype)
     flags = pltpu.VMEM((4, 4, 9 * W), F32)
     inputs = [pltpu.with_memory_space_constraint(v, pltpu.HBM) for v in (ham, dens, pattern, kept)]
-    cy_up, cy_down, ends, y_up, y_down, x_up, x_down, ham, dens, wide = call(
+    ends, cy_up, cy_down, y_up, y_down, x_up, x_down, ham, dens, wide = call(
         send_kernel,
-        [corner, corner, (2, 2, W, W), y_line, y_line, x_line, x_line, ham.shape, dens.shape]
+        [(2, 2, W, W), corner, corner, y_line, y_line, x_line, x_line, ham.shape, dens.shape]
         + [jax.ShapeDtypeStruct((4, 2, 4, 12 * W), F32)],
         [ham.shape, dens.shape, mask, mask, flags, flags]
         + [pltpu.SemaphoreType.DMA((2, 4)), pltpu.SemaphoreType.DMA((2,))],
-        [pl.BlockSpec(memory_space=pl.ANY)] * 4,
+        [ANY] * 4,
         16,
     )(*inputs)
     cy_low = shift(cy_up, "gy", 1)
     cy_high = shift(cy_down, "gy", -1)
-    x_high = shift(x_down, "gx", -1)
+    y_low = shift(y_up, "gy", 1)
+    y_high = shift(y_down, "gy", -1)
     x_low = shift(x_up, "gx", 1)
-    y_low = shift(y_up, "gy", 1)
-    y_down, y_low = lax.optimization_barrier((y_down, y_low))
-    y_high = shift(y_down, "gy", -1)
 
     def forward(n):
-        sums = [v[n, 2, :, :W] + ends[s, n] for s, v in enumerate((cy_low, cy_high))]
-        return jnp.concatenate([cy_low[n, :2], cy_high[n, :2], jnp.concatenate(sums, axis=1)[None]])
-
-    c_high = shift(forward(0), "gx", -1)
+        at = 3 * n
+        tiles = []
+        for v in (cy_low, cy_high):
+            tiles += [v[at], jnp.concatenate([v[at + 1, :, :W], v[at + 2, :, W:]], axis=1)]
+        sums = [v[at + 2, :, :W] + ends[s, n] for s, v in enumerate((cy_low, cy_high))]
+        return jnp.stack(tiles + [jnp.concatenate(sums, axis=1)])
+
+    x_high = shift(jnp.concatenate([x_down, forward(0)]), "gx", -1)
     c_low = shift(forward(1), "gx", 1)
-    return call(last_kernel, [ham.shape], [dense] * 3 + [(2, 4, 128, 768)])(
-        ham, dens, wide, y_low, y_high, x_low, x_high, cy_low, cy_high, c_low, c_high
-    )[0]
+    edges = [(2, 2, 256, 768)] * 2 + [(2, 2, 256, 256)] * 2 + [(2, 2, 128, 256)]
+    edges += [jax.ShapeDtypeStruct((2, 2, 128, 256), F32), (2, 2, 128, 256)]
+    out, *edges = call(
+        middle_kernel,
+        [ham.shape] + edges,
+        [dense] * 3 + [(2, 4, 128, 768), (2, 4, W, 9 * W), pltpu.SemaphoreType.DMA((1,))],
+        [VMEM] * 5,
+        32,
+        [ANY] + [VMEM] * 7,
+    )(ham, dens, wide, y_low, y_high)
+    tile, rows = (2, 2, 256, 256), (2, 4, W, 9 * W)
+    return call(
+        last_kernel,
+        [ham.shape],
+        [tile] * 6 + [(2, 2, 128, 256), rows, pltpu.SemaphoreType.DMA((2,))],
+        [VMEM] * 15 + [ANY],
+        32,
+        [ANY],
+        {15: 0},
+    )(wide, y_low, y_high, cy_low, cy_high, x_low, x_high, c_low, *edges, out)[0]
 
 
 def solution(mesh):

time: 31.3 us -> 27.8 us (0.89)
  waiting for transfers between devices: 9.38 us -> 4.79 us
  Pallas kernels: 11.5 us -> 11.9 us
    ppermute x8 -> x7, waiting for transfers between devices: 9.38 us -> 4.79 us  [shift(): lax.ppermute(value, axis, [(i, (i + step) % count) for i in range(count)])]
    pallas_call x2 -> x3, Pallas kernels: 11.5 us -> 11.9 us  [the longest x1 5.42 us: per_device(): call(middle_kernel, [ham.shape] + edges, [dense] * 3 + [(2, 4, 128, 768),...]
    ppermute x8 -> x7, starting transfers between devices: 9.94 us -> 10.2 us  [shift(): lax.ppermute(value, axis, [(i, (i + step) % count) for i in range(count)])]
  transfers between devices with their start and end apart: 8 -> 7, of which waited for: 3 -> 4; matrix products, arithmetic and copies ran while one was open for 1% -> 2% of each run, Pallas kernels for 0% -> 20%
where the time goes in v4:
time: 27.8 us; the launch traced here: 27.7 us
  Pallas kernels  11.9 us (43%)
  starting transfers between devices  10.2 us (37%)
  waiting for transfers between devices  4.79 us (17%)
  other arithmetic  0.46 us (2%)
    ppermute x7, starting transfers between devices, shift(): lax.ppermute(value, axis, [(i, (i + step) % count) for i in range(count)])  10.2 us
    pallas_call x1, Pallas kernels, per_device(): call(middle_kernel, [ham.shape] + edges, [dense] * 3 + [(2, 4, 128, 768),...  5.42 us
    ppermute x7, waiting for transfers between devices, shift(): lax.ppermute(value, axis, [(i, (i + step) % count) for i in range(count)])  4.79 us
    pallas_call x1, Pallas kernels, per_device(): call(send_kernel, [(2, 2, W, W), corner, corner, y_line, y_line, x_line,...  3.44 us
    pallas_call x1, Pallas kernels, per_device(): call(last_kernel, [ham.shape], [tile] * 6 + [(2, 2, 128, 256), rows, pltp...  3.08 us
  transfers between devices with their start and end apart: 7, of which 4 were waited for; matrix products, arithmetic and copies ran while one was open for 2% of the time, Pallas kernels for 20%

profile of v4, /device:TPU:0, one launch (start us, length us, event | category | flops | bytes accessed | tf_op | source)
XLA Modules:
  0.0 27.7 jit_solution(1753161525826624732)
XLA Ops:
  0.0 3.4 %shard_map.46 = (bf16[2,2,64,64]{3,2,1,0:T(8,128)(2,1)S(1)}, bf16[6,64,128]{2,1,0:T(8,128)(2,1)S(1)}, bf16[6,64,128]{2,1,0:T(8,128)(2,1)S(1)}, bf16[15,64,128]{2...) custom-call(bf16[4,4,64,576]{3,2,1,0:T(8,128)(2,1)} %ham.1, ...), custom_call_target="tpu_custom_call" | custom-call | tf_op jit(solution)/shard_map/pallas_call | solution.py:497
  3.4 0.5 %collective-permute-start.2 = (bf16[6,64,128]{2,1,0:T(8,128)(2,1)S(1)}, bf16[6,64,128]{2,1,0:T(8,128)(2,1)S(1)}, u32[]{:S(2)}, u32[]{:S(2)}) collective-permute-start(bf16[6,64,128]{2,1,0:T(8,128)(2,1)S(1)} %get-tuple-element.26), channel_id=1, source_target_pairs={{0,1},{1,2},{2,3},{3,0},{4,5},{5,6},{6,7},{7,4},{8,9},{9,10},{10,1... | collective-permute-start | bytes 294920 | tf_op jit(solution)/shard_map/ppermute | solution.py:488
  4.0 2.0 %collective-permute-start.3 = (bf16[6,64,128]{2,1,0:T(8,128)(2,1)S(1)}, bf16[6,64,128]{2,1,0:T(8,128)(2,1)S(1)}, u32[]{:S(2)}, u32[]{:S(2)}) collective-permute-start(bf16[6,64,128]{2,1,0:T(8,128)(2,1)S(1)} %get-tuple-element.27), channel_id=1, source_target_pairs={{0,3},{1,0},{2,1},{3,2},{4,7},{5,4},{6,5},{7,6},{8,11},{9,8},{10,9... | collective-permute-start | bytes 294920 | tf_op jit(solution)/shard_map/ppermute | solution.py:488
  5.9 2.3 %collective-permute-start.4 = (bf16[13,64,128]{2,1,0:T(8,128)(2,1)S(1)}, bf16[13,64,128]{2,1,0:T(8,128)(2,1)S(1)}, u32[]{:S(2)}, u32[]{:S(2)}) collective-permute-start(bf16[13,64,128]{2,1,0:T(8,128)(2,1)S(1)} %get-tuple-element.28), channel_id=1, source_target_pairs={{0,4},{4,8},{8,12},{12,16},{16,20},{20,24},{24,28},{28,0},{1,5},{5... | collective-permute-start | bytes 638984 | tf_op jit(solution)/shard_map/ppermute | solution.py:488
  8.2 0.0 collective-permute-start
  8.2 1.7 %collective-permute-start.1 = (bf16[15,64,128]{2,1,0:T(8,128)(2,1)S(1)}, bf16[15,64,128]{2,1,0:T(8,128)(2,1)S(1)}, u32[]{:S(2)}, u32[]{:S(2)}) collective-permute-start(bf16[15,64,128]{2,1,0:T(8,128)(2,1)S(1)} %get-tuple-element.25), channel_id=1, source_target_pairs={{0,3},{1,0},{2,1},{3,2},{4,7},{5,4},{6,5},{7,6},{8,11},{9,8},{10,9... | collective-permute-start | bytes 737288 | tf_op jit(solution)/shard_map/ppermute | solution.py:488
  10.0 0.0 collective-permute-done.2.cy_low
  10.0 0.1 slice_bitcast_fusion.5
  10.1 0.1 constant_dynamic-update-slice_fusion.3
  10.2 0.0 collective-permute-done.3.cy_high
  10.2 0.1 slice_bitcast_fusion.3
  10.3 0.1 constant_dynamic-update-slice_fusion.1
  10.4 0.1 constant_dynamic-update-slice_fusion
  10.5 3.7 %collective-permute-start.5 = (bf16[18,64,128]{2,1,0:T(8,128)(2,1)S(1)}, bf16[18,64,128]{2,1,0:T(8,128)(2,1)S(1)}, u32[]{:S(2)}, u32[]{:S(2)}) collective-permute-start(bf16[18,64,128]{2,1,0:T(8,128)(2,1)S(1)} %constant_dynamic-update-slice_fusion), channel_id=1, source_target_pairs={{0,28},{4,0},{8,4},{12,8},{16,12},{20,16},{24,20},{28,24},{1,29},{... | collective-permute-start | bytes 884744 | tf_op jit(solution)/shard_map/ppermute | solution.py:488
  14.1 0.1 constant_dynamic-update-slice_fusion.7
  14.2 0.1 constant_dynamic-update-slice_fusion.6
  14.3 0.1 collective-permute-start.6
  14.4 0.2 collective-permute-done.y_low
  14.6 0.9 %collective-permute-done.1.y_high = bf16[15,64,128]{2,1,0:T(8,128)(2,1)S(1)} collective-permute-done((bf16[15,64,128]{2,1,0:T(8,128)(2,1)S(1)}, bf16[15,64,128]{2,1,0:T(8,128)(2,1)S(1)}, u32[]{:S(2)}, u32[]{:S(2)}) %collective-permute-start.1) | collective-permute-done | bytes 245792 | tf_op jit(solution)/shard_map/ppermute | solution.py:488
  15.5 5.4 %shard_map.47 = (bf16[4,4,64,576]{3,2,1,0:T(8,128)(2,1)}, bf16[2,2,256,768]{3,2,1,0:T(8,128)(2,1)S(1)}, bf16[2,2,256,768]{3,2,1,0:T(8,128)(2,1)S(1)}, bf16[2,2,2...) custom-call(bf16[4,4,64,576]{3,2,1,0:T(8,128)(2,1)S(1)} %get-tuple-e, ...), custom_call_target="tpu_custom_call" | custom-call | tf_op jit(solution)/shard_map/pallas_call | solution.py:524
  20.9 0.8 %collective-permute-done.6.c_low = bf16[5,64,128]{2,1,0:T(8,128)(2,1)S(1)} collective-permute-done((bf16[5,64,128]{2,1,0:T(8,128)(2,1)S(1)}, bf16[5,64,128]{2,1,0:T(8,128)(2,1)S(1)}, u32[]{:S(2)}, u32[]{:S(2)}) %collective-permute-start.6) | collective-permute-done | bytes 81952 | tf_op jit(solution)/shard_map/ppermute | solution.py:488
  21.7 0.0 collective-permute-done.4.x_low
  21.7 2.9 %collective-permute-done.5.x_high = bf16[18,64,128]{2,1,0:T(8,128)(2,1)S(1)} collective-permute-done((bf16[18,64,128]{2,1,0:T(8,128)(2,1)S(1)}, bf16[18,64,128]{2,1,0:T(8,128)(2,1)S(1)}, u32[]{:S(2)}, u32[]{:S(2)}) %collective-permute-start.5) | collective-permute-done | bytes 294944 | tf_op jit(solution)/shard_map/ppermute | solution.py:488
  24.6 3.1 %shard_map.48 = bf16[4,4,64,576]{3,2,1,0:T(8,128)(2,1)} custom-call(f32[4,2,4,768]{3,2,1,0:T(4,128)S(1)} %get-tuple-element.23.wide, bf16[15,64,128]{2,1,0:T(8,128)(2,1)S(1)} %collective-permute-done.y_low, bf16[15,64,128]{2,1,0:T(8,128)(2,1)S(1)} %collective-permute-done.1.y_high, ...), custom_call_target="tpu_custom_call", output_to_operand_aliasing={{}: (15, {})} | custom-call | tf_op jit(solution)/shard_map/pallas_call | solution.py:533
  (4 shorter events, 0.0 us)
Async XLA Ops:
  3.4 6.5 %collective-permute-start.2 = (bf16[6,64,128]{2,1,0:T(8,128)(2,1)S(1)}, bf16[6,64,128]{2,1,0:T(8,128)(2,1)S(1)}, u32[]{:S(2)}, u32[]{:S(2)}) collective-permute-start(bf16[6,64,128]{2,1,0:T(8,128)(2,1)S(1)} %get-tuple-element.26), channel_id=1, source_target_pairs={{0,1},{1,2},{2,3},{3,0},{4,5},{5,6},{6,7},{7,4},{8,9},{9,10},{10,1... | collective-permute-start | bytes 294920 | tf_op jit(solution)/shard_map/ppermute | solution.py:488
  4.0 6.2 %collective-permute-start.3 = (bf16[6,64,128]{2,1,0:T(8,128)(2,1)S(1)}, bf16[6,64,128]{2,1,0:T(8,128)(2,1)S(1)}, u32[]{:S(2)}, u32[]{:S(2)}) collective-permute-start(bf16[6,64,128]{2,1,0:T(8,128)(2,1)S(1)} %get-tuple-element.27), channel_id=1, source_target_pairs={{0,3},{1,0},{2,1},{3,2},{4,7},{5,4},{6,5},{7,6},{8,11},{9,8},{10,9... | collective-permute-start | bytes 294920 | tf_op jit(solution)/shard_map/ppermute | solution.py:488
  5.9 15.8 %collective-permute-start.4 = (bf16[13,64,128]{2,1,0:T(8,128)(2,1)S(1)}, bf16[13,64,128]{2,1,0:T(8,128)(2,1)S(1)}, u32[]{:S(2)}, u32[]{:S(2)}) collective-permute-start(bf16[13,64,128]{2,1,0:T(8,128)(2,1)S(1)} %get-tuple-element.28), channel_id=1, source_target_pairs={{0,4},{4,8},{8,12},{12,16},{16,20},{20,24},{24,28},{28,0},{1,5},{5... | collective-permute-start | bytes 638984 | tf_op jit(solution)/shard_map/ppermute | solution.py:488
  8.2 6.4 %collective-permute-start = (bf16[15,64,128]{2,1,0:T(8,128)(2,1)S(1)}, bf16[15,64,128]{2,1,0:T(8,128)(2,1)S(1)}, u32[]{:S(2)}, u32[]{:S(2)}) collective-permute-start(bf16[15,64,128]{2,1,0:T(8,128)(2,1)S(1)} %get-tuple-element.24), channel_id=1, source_target_pairs={{0,1},{1,2},{2,3},{3,0},{4,5},{5,6},{6,7},{7,4},{8,9},{9,10},{10,1... | collective-permute-start | bytes 737288 | tf_op jit(solution)/shard_map/ppermute | solution.py:488
  8.2 7.3 %collective-permute-start.1 = (bf16[15,64,128]{2,1,0:T(8,128)(2,1)S(1)}, bf16[15,64,128]{2,1,0:T(8,128)(2,1)S(1)}, u32[]{:S(2)}, u32[]{:S(2)}) collective-permute-start(bf16[15,64,128]{2,1,0:T(8,128)(2,1)S(1)} %get-tuple-element.25), channel_id=1, source_target_pairs={{0,3},{1,0},{2,1},{3,2},{4,7},{5,4},{6,5},{7,6},{8,11},{9,8},{10,9... | collective-permute-start | bytes 737288 | tf_op jit(solution)/shard_map/ppermute | solution.py:488
  10.5 14.1 %collective-permute-start.5 = (bf16[18,64,128]{2,1,0:T(8,128)(2,1)S(1)}, bf16[18,64,128]{2,1,0:T(8,128)(2,1)S(1)}, u32[]{:S(2)}, u32[]{:S(2)}) collective-permute-start(bf16[18,64,128]{2,1,0:T(8,128)(2,1)S(1)} %constant_dynamic-update-slice_fusion), channel_id=1, source_target_pairs={{0,28},{4,0},{8,4},{12,8},{16,12},{20,16},{24,20},{28,24},{1,29},{... | collective-permute-start | bytes 884744 | tf_op jit(solution)/shard_map/ppermute | solution.py:488
  14.3 7.4 %collective-permute-start.6 = (bf16[5,64,128]{2,1,0:T(8,128)(2,1)S(1)}, bf16[5,64,128]{2,1,0:T(8,128)(2,1)S(1)}, u32[]{:S(2)}, u32[]{:S(2)}) collective-permute-start(bf16[5,64,128]{2,1,0:T(8,128)(2,1)S(1)} %constant_dynamic-update-slice_fusion.6), channel_id=1, source_target_pairs={{0,4},{4,8},{8,12},{12,16},{16,20},{20,24},{24,28},{28,0},{1,5},{5... | collective-permute-start | bytes 245768 | tf_op jit(solution)/shard_map/ppermute | solution.py:488

commit v5 on v4

--- a/solution.py
+++ b/solution.py
@@ -19,6 +19,12 @@
 def block(dense, x, y, x2, y2):
     p, i, r, c = spot(x, y, x2, y2)
     return dense[p, i, r : r + W, c : c + W]
+
+
+def triangles():
+    row = lax.broadcasted_iota(jnp.int32, (W, W), 0)
+    col = lax.broadcasted_iota(jnp.int32, (W, W), 1)
+    return [m.astype(F32).astype(BF) for m in (row <= col, row > col, row == col)]
 
 
 def strip_mask(mask_ref, x):
@@ -76,31 +82,35 @@
             dst[0, i, 192:256, c : c + 128] = zero
 
 
-def put_y(dst, side, along, across=None):
-    zero = jnp.zeros((W, W), BF)
+def put_y(dst, side, msg, n, masks, add):
     y, halo = (0, -1) if side == 0 else (3, 4)
+    same, after, before = line_tiles([line_cell(msg, n, i, 0, masks) for i in range(4)])
+
+    def along(x, x2):
+        c, d = x // 2, x2 // 2
+        tile = same[c] if c == d else after[0] if c < d else before[0]
+        return tile[W * (x % 2) : W * (x % 2) + W, W * (x2 % 2) : W * (x2 % 2) + W]
+
+    for x in range(4):
+        for x2 in range(max(0, x - 1), min(3, x + 1) + 1):
+            add[W * x : W * x + W, W * x2 : W * x2 + W] = block(dst, x, y, x2, halo)
+    inner = add[...].T
+    rest = jnp.zeros((W, 128), BF)
     for x in range(4):
         for d in (-1, 0, 1):
             x2 = x + d
-            inside = 0 <= x2 < 4
-            if not inside and across is None:
+            if 0 <= x2 < 4:
+                two = along(x, x2), inner[W * x : W * x + W, W * x2 : W * x2 + W]
+            elif n == 2:
                 continue
-            same = along(x, x2)
-            inner = block(dst, x2, y, x, halo).T if inside else across(x, x2)
-            rest = jnp.zeros((W, 128), BF)
-            parts = [same, inner, rest] if side == 0 else [rest, inner, same]
+            elif x == 0:
+                link = msg[6][:, W * n : W * n + W]
+                two = link, msg[10][:, W * n : W * n + W]
+            else:
+                two = msg[3 if n == 0 else 5][:, :W], msg[11][:, W * n : W * n + W]
+            parts = [*two, rest] if side == 0 else [rest, two[1], two[0]]
             c = 256 * (d + 1)
             dst[side, x + 1, 192 * side : 192 * side + W, c : c + 256] = jnp.concatenate(parts, axis=1)
-
-
-def lower_blocks(places):
-    row = lax.broadcasted_iota(jnp.int32, (256, 256), 0) // W
-    col = lax.broadcasted_iota(jnp.int32, (256, 256), 1) // W
-    hit = None
-    for i, j in places:
-        here = (row == i) & (col == j)
-        hit = here if hit is None else hit | here
-    return hit.astype(BF)
 
 
 def dense_product(left, right, p, x, e, brick=False):
@@ -130,28 +140,28 @@
 
 
 def send_kernel(
-    ham, dens, pattern, kept, ends, cy_up, cy_down, y_up, y_down, x_up, x_down, hm, dm, wide,
+    ham, dens, pattern, kept, ends_up, ends_down, cy_up, cy_down, y_up, y_down, x_up, x_down, hm, dm, wide,
     hb, db, pb, kb, live, keep, sems, mask_sems,
 ):
     masks = [
         pltpu.make_async_copy(pattern, pb, mask_sems.at[0]),
         pltpu.make_async_copy(kept, kb, mask_sems.at[1]),
     ]
-    copies = []
-    for x in (0, 3, 1, 2):
+    copies = {x: [] for x in (0, 3, 1, 2)}
+    for x in copies:
         for n, (ref, buf) in enumerate(((ham, hb), (dens, db))):
-            copies.append(pltpu.make_async_copy(ref.at[x], buf.at[x], sems.at[n, x]))
-    for copy in masks + copies:
+            copies[x].append(pltpu.make_async_copy(ref.at[x], buf.at[x], sems.at[n, x]))
+    for copy in masks + sum(copies.values(), []):
         copy.start()
     for copy in masks:
         copy.wait()
     for x in range(4):
         live[x] = strip_mask(pb, x)
         keep[x] = strip_mask(kb, x)
-        wide[x, 0], wide[x, 1] = window_mask(kb, x)
-    for copy in copies:
-        copy.wait()
-    for x in range(4):
+
+    def arrive(x):
+        for copy in copies[x]:
+            copy.wait()
         for y in range(4):
             mask = live[x, y : y + 1, :].astype(BF)
             hm[x, y] = hb[x, y] * mask
@@ -182,8 +192,8 @@
         return lax.dot_general(left, right, (((1,), (1,)), ((), ())), preferred_element_type=F32)
 
     def own(x, y):
-        total = rows(hm[x, y], dm[x, y])
-        return ((total + total.T) * flag(x, y, 0, 0)).astype(BF)
+        total = rows(hm[x, y], dm[x, y]) + rows(dm[x, y], hm[x, y])
+        return (total * flag(x, y, 0, 0)).astype(BF)
 
     def link(x, y, dx, dy):
         if dx == 1:
@@ -197,66 +207,121 @@
         total = rows(jnp.concatenate(left, axis=1), jnp.concatenate(right, axis=1))
         return (total * flag(x, y, dx, dy)).astype(BF)
 
-    def pair(one, two):
-        return jnp.concatenate([one, two], axis=1)
-
-    selfs = {(x, y): own(x, y) for x in range(4) for y in range(4) if x in (0, 3) or y in (0, 3)}
-    for y, out, dy in ((3, cy_up, 1), (0, cy_down, -1)):
+    def pair(one, two, swap=0):
+        return jnp.concatenate([two, one] if swap else [one, two], axis=1)
+
+    upper, lower, eye = triangles()
+    selfs = {}
+
+    def packed(x, y):
+        return get(hm, x, y, 0, 0) * upper + get(dm, x, y, 0, 0) * lower
+
+    def diagonal(value):
+        return jnp.sum((value * eye).astype(F32), axis=0, keepdims=True)
+
+    row = lax.broadcasted_iota(jnp.int32, (W, W), 0)
+    col = lax.broadcasted_iota(jnp.int32, (W, W), 1)
+    def put_line(out, cell, step, marks, first):
+        dx, dy = step
+        cells = [cell(i) for i in range(4)]
+        items = list(marks)
+        for i, (x, y) in enumerate(cells):
+            out[i] = pair(packed(x, y), get(hm, x, y, dx, dy), (first + i) % 2)
+            items.append(diagonal(get(dm, x, y, 0, 0)))
+        items += [diagonal(selfs[cells[i]]) for i in (2, 3)]
+        even = 1 - first % 2
+        for i in range(2):
+            one, two = cells[2 * i], cells[2 * i + 1]
+            out[4 + i] = pair(get(dm, *one, dx, dy), get(dm, *two, dx, dy), even)
+        x, y = cells[0]
+        out[6] = pair(get(hm, x, y, -dx, -dy), get(dm, x, y, -dx, -dy))
+        mixed = [selfs[cells[i]] * upper + selfs[cells[i + 2]] * lower for i in range(2)]
+        out[7] = pair(*mixed, 1 - even)
+        out[8] = pair(link(*cells[0], dx, dy), link(*cells[1], dx, dy), even)
+        rows = jnp.zeros((16, W), F32)
+        for k, item in enumerate(items):
+            rows = jnp.where(row[:16] == k, item, rows)
+        rows = jnp.concatenate([rows.astype(BF), jnp.zeros((48, W), BF)], axis=0)
+        out[9] = pair(link(*cells[2], dx, dy), rows, even)
+
+    arrive(0)
+    arrive(3)
+    for x, out, dx in ((0, x_down, -1), (3, x_up, 1)):
+        selfs.update({(x, y): own(x, y) for y in range(4)})
+        marks = [flag(x, 0, 0, -1), flag(x, 0, dx, -1), flag(x, 3, 0, 1), flag(x, 3, dx, 1)]
+        put_line(out, lambda i: (x, i), (0, 1), marks, 1)
+    arrive(1)
+    arrive(2)
+    for x in (1, 2):
+        selfs.update({(x, y): own(x, y) for y in (0, 3)})
+    ends_up[...] = jnp.zeros_like(ends_up)
+    ends_down[...] = jnp.zeros_like(ends_down)
+    for y, out, line, dy in ((3, cy_up, y_up, 1), (0, cy_down, y_down, -1)):
+        alongs = []
         for n, (x, dx) in enumerate(((0, -1), (3, 1))):
             across = through(x, y, ((x - dx, y),), 0, dy)
             along = through(x, y, ((x, y - dy),), dx, 0)
-            out[3 * n] = pair(selfs[x, y], get(hm, x, y, 0, 0))
-            out[3 * n + 1] = pair(get(dm, x, y, 0, 0), along)
-            out[3 * n + 2] = pair(across, along.T)
-            ends[0 if y == 0 else 1, n] = across.T
-
-    def line(out, cell, step, marks):
-        dx, dy = step
-        for i in range(4):
-            x, y = cell(i)
-            for n, ref in enumerate((hm, dm)):
-                out[4 * n + i] = pair(get(ref, x, y, 0, 0), get(ref, x, y, dx, dy))
-            if i < 3:
-                out[9 + i] = pair(selfs[x, y], link(x, y, dx, dy))
+            alongs.append(along)
+            low = diagonal(get(dm, x, y, 0, 0))
+            low = jnp.where(row == col + 1, low, jnp.where((row == 63) & (col == 0), low[:, 63:64], 0.0))
+            odd = 1 if y == 0 else 0
+            out[2 * n] = pair(selfs[x, y] * upper + low.astype(BF), across, odd)
+            out[2 * n + 1] = pair(packed(x, y), along.T, odd)
+            ends = ends_up if x == 3 else ends_down
+            if y == 0:
+                ends[0, :, W:] = across.T
             else:
-                rows = [jnp.broadcast_to(m, (16, W)).astype(BF) for m in marks]
-                out[12] = pair(selfs[x, y], jnp.concatenate(rows, axis=0))
-        x, y = cell(0)
-        out[8] = pair(get(hm, x, y, -dx, -dy), get(dm, x, y, -dx, -dy))
-
-    for x, out, dx in ((3, x_up, 1), (0, x_down, -1)):
-        marks = [flag(x, 0, 0, -1), flag(x, 0, dx, -1), flag(x, 3, 0, 1), flag(x, 3, dx, 1)]
-        line(out, lambda i: (x, i), (0, 1), marks)
+                ends[2, :, 0:W] = across.T
+        line[12] = pair(*alongs)
+
     for y, out, dy in ((3, y_up, 1), (0, y_down, -1)):
         marks = [flag(0, y, -1, 0), flag(0, y, -1, dy), flag(3, y, 1, 0), flag(3, y, 1, dy)]
-        line(out, lambda i: (i, y), (1, 0), marks)
+        put_line(out, lambda i: (i, y), (1, 0), marks, 0)
         for n, (x, dx) in enumerate(((0, -1), (3, 1))):
-            out[13 + n] = pair(get(hm, x, y, dx, dy), get(dm, x, y, dx, dy))
-
-
-def line_blocks(msg, n, corners, first=None, last=None):
-    base = 4 * n if n < 2 else 9
-
-    def right(i):
-        if i == 3 and last is not None:
-            return last
-        return msg[base + i][:, W:]
-
-    def left():
-        if first is not None:
-            return first
-        return msg[8][:, W * n : W * n + W]
-
-    def get(i, j):
-        if i == j:
-            return corners[0 if i < 0 else 1] if i in (-1, 4) else msg[base + i][:, :W]
-        if (i, j) == (0, -1):
-            return left()
-        if (i, j) == (-1, 0):
-            return left().T
-        return right(i) if j > i else right(j).T
-
-    return get
+            out[10 + n] = pair(get(hm, x, y, dx, dy), get(dm, x, y, dx, dy))
+    for x in range(4):
+        wide[x, 0], wide[x, 1] = window_mask(kb, x)
+
+
+def halves(odd):
+    row = lax.broadcasted_iota(jnp.int32, (W, 128), 0)
+    col = lax.broadcasted_iota(jnp.int32, (W, 128), 1) - W * odd
+    mine = (col >= 0) & (col < W)
+    masks = (mine & (row <= col), mine & (row > col), mine & (row == col), jnp.logical_not(mine))
+    return [m.astype(F32).astype(BF) for m in masks]
+
+
+def line_cell(msg, n, i, first, masks):
+    odd = (first + i) % 2
+    upper, lower, eye, other = masks[odd]
+    own = msg[i] if n < 2 else msg[7]
+    if n == 0:
+        link = own * other
+    else:
+        link = None if n == 2 and i == 3 else msg[4 + 4 * (n - 1) + i // 2] * other
+    if n == 1 or n == 2 and i >= 2:
+        add = own * lower
+        k = 4 + i if n == 1 else 6 + i
+        diag = msg[9][k : k + 1, W * (first % 2) : W * (first % 2) + W]
+        lay = add + jnp.concatenate([diag, diag], axis=1) * eye
+    else:
+        lay, add = own * upper, own * (upper - eye)
+    if odd or link is None:
+        return lay, add, link
+    return lay + link, add + link, None
+
+
+def line_tiles(rows):
+    zero = jnp.zeros((W, 128), BF)
+    same, after, before = [], [], []
+    for c in range(len(rows) // 2):
+        one, two = rows[2 * c], rows[2 * c + 1]
+        lay = jnp.concatenate([one[0], two[0]], axis=0)
+        same.append(lay + jnp.concatenate([one[1], two[1]], axis=0).T)
+        if 2 * c + 2 < len(rows):
+            after.append(jnp.concatenate([zero, two[2]], axis=0))
+            before.append(after[-1].T)
+    return same, after, before
 
 
 def edge(side):
@@ -275,22 +340,17 @@
 
 def middle_kernel(
     ham, dens, wide, y_low, y_high, out, h_edge, d_edge, h_back, d_back, a_edge, g_edge, done_edge,
-    xh, xd, xs, a_rows, rows, sems,
+    xh, xd, xs, a_rows, rows, add, sems,
 ):
     ys = (y_low, y_high)
+    masks = halves(0), halves(1)
     for n, (ref, dst, keep, turned) in enumerate(
         ((ham, xh, h_edge, h_back), (dens, xd, d_edge, d_back))
     ):
         put_strips(dst, ref)
         put_shared(dst)
         for side in range(2):
-            m = ys[side]
-            put_y(
-                dst,
-                side,
-                line_blocks(m, n, None),
-                lambda x, x2, m=m, n=n: m[13 if x == 0 else 14][:, W * n : W * n + W],
-            )
+            put_y(dst, side, ys[side], n, masks, add.at[2 * side + n])
         for side in range(2):
             x, go, _, back = edge(side)
             for p in range(2):
@@ -312,7 +372,7 @@
                     xs[p, x + 1, 64:192, cols] = (a + b).astype(BF)
     put_shared(xs)
     for side in range(2):
-        put_y(xs, side, line_blocks(ys[side], 2, None))
+        put_y(xs, side, ys[side], 2, masks, add.at[4 + side])
         for p in range(2):
             x = edge(side)[0]
             a_edge[side, p] = a_rows[p, x, :, part(1)]
@@ -340,57 +400,61 @@
 
 
 def last_kernel(
-    wide, y_low, y_high, cy_low, cy_high, x_low, x_high, c_low, h_edge, d_edge, h_back, d_back, a_edge, g_edge,
-    done_edge, given, out, hh, dh, sh, ss, sb, u, a_go, rows, sems,
+    wide, y_low, y_high, x_low, x_high, c_low, h_edge, d_edge, h_back, d_back, a_edge, g_edge,
+    done_edge, given, out, hh, dh, sh, ss, sb, a_go, rows, sems,
 ):
-    ys, cys, xm, cs = (y_low, y_high), (cy_low, cy_high), (x_low, x_high), (c_low, x_high.at[13:18])
+    ys, xm, cs = (y_low, y_high), (x_low, x_high), (c_low, x_high.at[10:14])
     both = [(sx, p) for sx in range(2) for p in range(2)]
 
-    def corner(sx, sy, k):
-        if k == 4:
-            return cs[sx][4][:, W * sy : W * sy + W]
-        return cs[sx][2 * sy + k // 2][:, W * (k % 2) : W * (k % 2) + W]
+    masks = halves(0), halves(1)
+
+    def corner_cell(sx, sy, n):
+        upper, lower, eye, _ = masks[sy]
+        one = cs[sx][2 * sy]
+        if n == 2:
+            return one * upper, one * (upper - eye), None
+        value = cs[sx][2 * sy + 1]
+        if n == 0:
+            return value * upper, value * (upper - eye), None
+        row = lax.broadcasted_iota(jnp.int32, (W, W), 0)
+        col = lax.broadcasted_iota(jnp.int32, (W, W), 1)
+        spread = one[:, W * sy : W * sy + W].astype(F32)
+        low = jnp.sum(jnp.where(row == col + 1, spread, 0.0), axis=0, keepdims=True)
+        low += jnp.where(col[0:1] == 63, spread[63:64, 0:1], 0.0)
+        below = value * lower
+        return below + jnp.concatenate([low, low], axis=1).astype(BF) * eye, below, None
+
+    def tile(ref, sx, p):
+        return ref[sx, 128 * p : 128 * p + 256, 128 * p : 128 * p + 256]
 
     def dot(left, right):
         return jnp.dot(left, right, preferred_element_type=F32)
 
-    def fill(dst, sx, n, corners, crossing):
-        msg, base = xm[sx], 4 * n if n < 2 else 9
-        for p in range(2):
-            u[sx, p, :, :] = jnp.zeros((256, 256), BF)
-            for i in range(4):
-                y = 2 * p - 1 + i
-                at = slice(W * i, W * i + W)
-                if y in (-1, 4):
-                    u[sx, p, at, at] = corners[p]
-                    continue
-                whole = i < 3 and not (n == 2 and y == 3)
-                u[sx, p, at, W * i : W * i + W * (2 if whole else 1)] = (
-                    msg[base + y] if whole else msg[base + y][:, :W]
-                )
-            places = crossing(u, p)
-            tile = u[sx, p]
-            dst[sx, p] = tile + tile.T * lower_blocks(places)
-
-    def crossing_of(sx, n):
-        def put(u, p):
-            if p == 1:
-                return ((1, 0), (2, 1), (3, 2))
-            u[sx, 0, 64:128, 0:64] = xm[sx][8][:, W * n : W * n + W]
-            return ((0, 1), (2, 1), (3, 2))
-
-        return put
+    def fill(dst, sx, n, crossing):
+        rows = [line_cell(xm[sx], n, i, 1, masks) for i in range(4)]
+        rows = [corner_cell(sx, 0, n), *rows, corner_cell(sx, 1, n)]
+        for place, value in crossing:
+            lay, add, rest = rows[place]
+            rows[place] = lay + value, add + value, rest
+        same, after, before = line_tiles(rows)
+        for c in range(3):
+            at, to = slice(128 * c, 128 * c + 128), slice(128 * c + 128, 128 * c + 256)
+            dst[sx, at, at] = same[c]
+            if c < 2:
+                dst[sx, at, to] = after[c]
+                dst[sx, to, at] = before[c]
 
     for sx in range(2):
-        for n, halo in enumerate((hh, dh)):
-            fill(halo, sx, n, [corner(sx, t, n + 1) for t in range(2)], crossing_of(sx, n))
+        cross = xm[sx][6]
+        fill(hh, sx, 0, [(1, cross * masks[1][3])])
+        fill(dh, sx, 1, [(1, jnp.concatenate([cross[:, W:], jnp.zeros((W, W), BF)], axis=1))])
     for sx, p in both:
         x, go, _, back = edge(sx)
         mask = both_rows(wide, x, p)[:, part(go)]
 
         def to_halo(left, right, halo):
             left = left[sx, p, 64:192, :]
-            return dot(left[:, part(go)], halo[sx, p]) + dot(
+            return dot(left[:, part(go)], tile(halo, sx, p)) + dot(
                 left[:, part(1)], right[sx, p, :, part(go)]
             )
 
@@ -409,7 +473,7 @@
             def cols(n):
                 return slice(256 * n + 128 * sy, 256 * n + 128 * sy + 128)
 
-            top = [halo[sx, sy, two, two], back_tile[sx, sy, two, two]]
+            top = [tile(halo, sx, sy)[two, two], back_tile[sx, sy, two, two]]
             low = [row[sx, sy, two, cols(go)], row[sx, sy, two, cols(1)]]
             return jnp.concatenate(
                 [jnp.concatenate(top, axis=1), jnp.concatenate(low, axis=1)], axis=0
@@ -423,11 +487,13 @@
 
         a, b, c = hp, ep, 2 + hp
         xt, yt = xm[sx], ys[sy]
-        keep_ba = xt[12][32 * sy : 32 * sy + 1, W:].astype(F32)
-        keep_bc = xt[12][32 * sy + 16 : 32 * sy + 17, W:].astype(F32)
-        keep_ca = yt[12][32 * sx : 32 * sx + 1, W:].astype(F32)
-        ab[sx, sy] = (corner(sx, sy, 4).astype(F32) + keep_ba * blk(a, b)).astype(BF)
-        ca = cys[sy][1 + 3 * sx][:, W:].astype(F32) + corner(sx, sy, 3).astype(F32) + keep_ca * blk(c, a)
+        keep_ba = xt[9][2 * sy : 2 * sy + 1, W:].astype(F32)
+        keep_bc = xt[9][2 * sy + 1 : 2 * sy + 2, W:].astype(F32)
+        keep_ca = yt[9][2 * sx : 2 * sx + 1, :W].astype(F32)
+        rest = slice(W * (1 - sy), W * (1 - sy) + W)
+        given_ab, given_ca = cs[sx][2 * sy][:, rest], cs[sx][2 * sy + 1][:, rest]
+        ab[sx, sy] = (given_ab.astype(F32) + keep_ba * blk(a, b)).astype(BF)
+        ca = yt[12][:, W * sx : W * sx + W].astype(F32) + given_ca.astype(F32) + keep_ca * blk(c, a)
         ca, cb = ca.astype(BF), (keep_bc * blk(c, b)).astype(BF)
         here = slice(192 * sy, 192 * sy + W)
         ss[sx, sy, here, :] = jnp.concatenate([ca, cb, z2] if sy == 0 else [z2, cb, ca], axis=1)
@@ -435,14 +501,12 @@
         ss[sx, 1, 0:64, :] = jnp.concatenate([ss[sx, 0, 128:192, 128:256], z2], axis=1)
         ss[sx, 0, 192:256, :] = jnp.concatenate([z2, ss[sx, 1, 64:128, 0:128]], axis=1)
 
-        def put(u, p, sx=sx):
-            if p == 0:
-                u[sx, 0, 0:64, 64:128] = ab[sx, 0]
-                return ((1, 0), (2, 1), (3, 2))
-            u[sx, 1, 192:256, 128:192] = ab[sx, 1]
-            return ((1, 0), (2, 1), (2, 3))
-
-        fill(sh, sx, 2, [corner(sx, t, 0) for t in range(2)], put)
+        none = jnp.zeros((W, W), BF)
+        crossing = [
+            (0, jnp.concatenate([none, ab[sx, 0]], axis=1)),
+            (5, jnp.concatenate([ab[sx, 1], none], axis=1)),
+        ]
+        fill(sh, sx, 2, crossing)
         for p in range(2):
             sb[sx, p] = ss[sx, p].T
     copies = []
@@ -450,7 +514,7 @@
         x, go, _, back = edge(sx)
         mask = both_rows(wide, x, p)
         ld = d_edge[sx, p, 64:192, :]
-        outer = dot(a_go[sx, p], dh[sx, p]) + dot(ld[:, part(go)], sh[sx, p])
+        outer = dot(a_go[sx, p], tile(dh, sx, p)) + dot(ld[:, part(go)], tile(sh, sx, p))
         outer += dot(a_edge[sx, p], d_edge[sx, p, :, part(go)]) + dot(ld[:, part(1)], ss[sx, p])
         outer = 3.0 * ss[sx, p, 64:192, :].astype(F32) - 2.0 * outer
         same = dot(a_go[sx, p], d_back[sx, p]) + dot(ld[:, part(go)], sb[sx, p])
@@ -490,13 +554,13 @@
 
 def per_device(ham, dens, pattern, kept):
     dense = (2, 6, 256, 768)
-    corner, y_line, x_line = (6, W, 128), (15, W, 128), (13, W, 128)
+    corner, y_line, x_line = (4, W, 128), (13, W, 128), (10, W, 128)
     mask = pltpu.VMEM(pattern.shape, pattern.dtype)
     flags = pltpu.VMEM((4, 4, 9 * W), F32)
     inputs = [pltpu.with_memory_space_constraint(v, pltpu.HBM) for v in (ham, dens, pattern, kept)]
-    ends, cy_up, cy_down, y_up, y_down, x_up, x_down, ham, dens, wide = call(
+    ends_up, ends_down, cy_up, cy_down, y_up, y_down, x_up, x_down, ham, dens, wide = call(
         send_kernel,
-        [(2, 2, W, W), corner, corner, y_line, y_line, x_line, x_line, ham.shape, dens.shape]
+        [corner] * 4 + [y_line, y_line, x_line, x_line, ham.shape, dens.shape]
         + [jax.ShapeDtypeStruct((4, 2, 4, 12 * W), F32)],
         [ham.shape, dens.shape, mask, mask, flags, flags]
         + [pltpu.SemaphoreType.DMA((2, 4)), pltpu.SemaphoreType.DMA((2,))],
@@ -509,36 +573,36 @@
     y_high = shift(y_down, "gy", -1)
     x_low = shift(x_up, "gx", 1)
 
-    def forward(n):
-        at = 3 * n
-        tiles = []
-        for v in (cy_low, cy_high):
-            tiles += [v[at], jnp.concatenate([v[at + 1, :, :W], v[at + 2, :, W:]], axis=1)]
-        sums = [v[at + 2, :, :W] + ends[s, n] for s, v in enumerate((cy_low, cy_high))]
-        return jnp.stack(tiles + [jnp.concatenate(sums, axis=1)])
-
-    x_high = shift(jnp.concatenate([x_down, forward(0)]), "gx", -1)
-    c_low = shift(forward(1), "gx", 1)
+    def forward(n, ends):
+        at = slice(2 * n, 2 * n + 2)
+        return jnp.concatenate([cy_low[at], cy_high[at]]) + ends
+
+    x_high = shift(jnp.concatenate([x_down, forward(0, ends_down)]), "gx", -1)
+    c_low = shift(forward(1, ends_up), "gx", 1)
     edges = [(2, 2, 256, 768)] * 2 + [(2, 2, 256, 256)] * 2 + [(2, 2, 128, 256)]
     edges += [jax.ShapeDtypeStruct((2, 2, 128, 256), F32), (2, 2, 128, 256)]
     out, *edges = call(
         middle_kernel,
         [ham.shape] + edges,
-        [dense] * 3 + [(2, 4, 128, 768), (2, 4, W, 9 * W), pltpu.SemaphoreType.DMA((1,))],
+        [dense] * 3 + [(2, 4, 128, 768), (2, 4, W, 9 * W)]
+        + [(6, 256, 256)]
+        + [pltpu.SemaphoreType.DMA((1,))],
         [VMEM] * 5,
         32,
         [ANY] + [VMEM] * 7,
     )(ham, dens, wide, y_low, y_high)
-    tile, rows = (2, 2, 256, 256), (2, 4, W, 9 * W)
+    six, tile, rows = (2, 384, 384), (2, 2, 256, 256), (2, 4, W, 9 * W)
     return call(
         last_kernel,
         [ham.shape],
-        [tile] * 6 + [(2, 2, 128, 256), rows, pltpu.SemaphoreType.DMA((2,))],
-        [VMEM] * 15 + [ANY],
+        [six] * 3
+        + [tile] * 2
+        + [(2, 2, 128, 256), rows, pltpu.SemaphoreType.DMA((2,))],
+        [VMEM] * 13 + [ANY],
         32,
         [ANY],
-        {15: 0},
-    )(wide, y_low, y_high, cy_low, cy_high, x_low, x_high, c_low, *edges, out)[0]
+        {13: 0},
+    )(wide, y_low, y_high, x_low, x_high, c_low, *edges, out)[0]
 
 
 def solution(mesh):

time: 27.8 us -> 24.6 us (0.88)
  waiting for transfers between devices: 4.79 us -> 3.45 us
  Pallas kernels: 11.9 us -> 11 us
  other arithmetic: 0.46 us -> 0.05 us
  starting transfers between devices: 10.2 us -> 9.85 us
    ppermute x7, waiting for transfers between devices: 4.79 us -> 3.45 us  [shift(): lax.ppermute(value, axis, [(i, (i + step) % count) for i in range(count)])]
    pallas_call x1, Pallas kernels: 5.42 us -> 4.94 us  [per_device(): call(middle_kernel, [ham.shape] + edges, [dense] * 3 + [(2, 4, 128, 768),...]
    pallas_call x2, Pallas kernels: 6.52 us -> 6.05 us  [the longest x1 3.5 us: per_device(): call(send_kernel, [corner] * 4 + [y_line, y_line, x_line, x_line, ham.sha...]
    ppermute x7, starting transfers between devices: 10.2 us -> 9.85 us  [shift(): lax.ppermute(value, axis, [(i, (i + step) % count) for i in range(count)])]
  transfers between devices with their start and end apart: 7 -> 7, of which waited for: 4 -> 4; matrix products, arithmetic and copies ran while one was open for 2% -> 0% of each run, Pallas kernels for 20% -> 20%
where the time goes in v5:
time: 24.6 us; the launch traced here: 24.4 us
  Pallas kernels  11 us (45%)
  starting transfers between devices  9.85 us (40%)
  waiting for transfers between devices  3.45 us (14%)
    ppermute x7, starting transfers between devices, shift(): lax.ppermute(value, axis, [(i, (i + step) % count) for i in range(count)])  9.85 us
    pallas_call x1, Pallas kernels, per_device(): call(middle_kernel, [ham.shape] + edges, [dense] * 3 + [(2, 4, 128, 768),...  4.94 us
    pallas_call x1, Pallas kernels, per_device(): call(send_kernel, [corner] * 4 + [y_line, y_line, x_line, x_line, ham.sha...  3.5 us
    ppermute x7, waiting for transfers between devices, shift(): lax.ppermute(value, axis, [(i, (i + step) % count) for i in range(count)])  3.45 us
    pallas_call x1, Pallas kernels, per_device(): call(last_kernel, [ham.shape], [six] * 3 + [tile] * 2 + [(2, 2, 128, 256)...  2.55 us
  transfers between devices with their start and end apart: 7, of which 4 were waited for; matrix products, arithmetic and copies ran while one was open for 0% of the time, Pallas kernels for 20%

profile of v5, /device:TPU:0, one launch (start us, length us, event | category | flops | bytes accessed | tf_op | source)
XLA Modules:
  0.0 24.4 jit_solution(2856070919880383482)
XLA Ops:
  0.0 3.5 %shard_map.46 = (bf16[4,64,128]{2,1,0:T(8,128)(2,1)S(1)}, bf16[4,64,128]{2,1,0:T(8,128)(2,1)S(1)}, bf16[4,64,128]{2,1,0:T(8,128)(2,1)S(1)}, bf16[4,64,128]{2,1,0...) custom-call(bf16[4,4,64,576]{3,2,1,0:T(8,128)(2,1)} %ham.1, ...), custom_call_target="tpu_custom_call" | custom-call | tf_op jit(solution)/shard_map/pallas_call | solution.py:561
  3.5 0.5 %collective-permute-start.3 = (bf16[4,64,128]{2,1,0:T(8,128)(2,1)S(1)}, bf16[4,64,128]{2,1,0:T(8,128)(2,1)S(1)}, u32[]{:S(2)}, u32[]{:S(2)}) collective-permute-start(bf16[4,64,128]{2,1,0:T(8,128)(2,1)S(1)} %get-tuple-element.29), channel_id=1, source_target_pairs={{0,1},{1,2},{2,3},{3,0},{4,5},{5,6},{6,7},{7,4},{8,9},{9,10},{10,1... | collective-permute-start | bytes 196616 | tf_op jit(solution)/shard_map/ppermute | solution.py:552
  4.0 2.0 %collective-permute-start.4 = (bf16[4,64,128]{2,1,0:T(8,128)(2,1)S(1)}, bf16[4,64,128]{2,1,0:T(8,128)(2,1)S(1)}, u32[]{:S(2)}, u32[]{:S(2)}) collective-permute-start(bf16[4,64,128]{2,1,0:T(8,128)(2,1)S(1)} %get-tuple-element.30), channel_id=1, source_target_pairs={{0,3},{1,0},{2,1},{3,2},{4,7},{5,4},{6,5},{7,6},{8,11},{9,8},{10,9... | collective-permute-start | bytes 196616 | tf_op jit(solution)/shard_map/ppermute | solution.py:552
  6.0 2.3 %collective-permute-start.2 = (bf16[10,64,128]{2,1,0:T(8,128)(2,1)S(1)}, bf16[10,64,128]{2,1,0:T(8,128)(2,1)S(1)}, u32[]{:S(2)}, u32[]{:S(2)}) collective-permute-start(bf16[10,64,128]{2,1,0:T(8,128)(2,1)S(1)} %get-tuple-element.27), channel_id=1, source_target_pairs={{0,4},{4,8},{8,12},{12,16},{16,20},{20,24},{24,28},{28,0},{1,5},{5... | collective-permute-start | bytes 491528 | tf_op jit(solution)/shard_map/ppermute | solution.py:552
  8.3 0.0 collective-permute-start
  8.3 1.7 %collective-permute-start.1 = (bf16[13,64,128]{2,1,0:T(8,128)(2,1)S(1)}, bf16[13,64,128]{2,1,0:T(8,128)(2,1)S(1)}, u32[]{:S(2)}, u32[]{:S(2)}) collective-permute-start(bf16[13,64,128]{2,1,0:T(8,128)(2,1)S(1)} %get-tuple-element.26), channel_id=1, source_target_pairs={{0,3},{1,0},{2,1},{3,2},{4,7},{5,4},{6,5},{7,6},{8,11},{9,8},{10,9... | collective-permute-start | bytes 638984 | tf_op jit(solution)/shard_map/ppermute | solution.py:552
  10.0 0.0 collective-permute-done.3
  10.0 0.0 collective-permute-done.4
  10.1 3.3 %collective-permute-start.5 = (bf16[14,64,128]{2,1,0:T(8,128)(2,1)S(1)}, bf16[14,64,128]{2,1,0:T(8,128)(2,1)S(1)}, u32[]{:S(2)}, u32[]{:S(2)}) collective-permute-start(bf16[14,64,128]{2,1,0:T(8,128)(2,1)S(1)} %pad_maximum_fusion), channel_id=1, source_target_pairs={{0,28},{4,0},{8,4},{12,8},{16,12},{20,16},{24,20},{28,24},{1,29},{... | collective-permute-start | bytes 688136 | tf_op jit(solution)/shard_map/ppermute | solution.py:552
  13.4 0.1 collective-permute-start.6
  13.5 0.5 %collective-permute-done.y_low = bf16[13,64,128]{2,1,0:T(8,128)(2,1)S(1)} collective-permute-done((bf16[13,64,128]{2,1,0:T(8,128)(2,1)S(1)}, bf16[13,64,128]{2,1,0:T(8,128)(2,1)S(1)}, u32[]{:S(2)}, u32[]{:S(2)}) %collective-permute-start) | collective-permute-done | bytes 213024 | tf_op jit(solution)/shard_map/ppermute | solution.py:552
  14.0 0.9 %collective-permute-done.1.y_high = bf16[13,64,128]{2,1,0:T(8,128)(2,1)S(1)} collective-permute-done((bf16[13,64,128]{2,1,0:T(8,128)(2,1)S(1)}, bf16[13,64,128]{2,1,0:T(8,128)(2,1)S(1)}, u32[]{:S(2)}, u32[]{:S(2)}) %collective-permute-start.1) | collective-permute-done | bytes 213024 | tf_op jit(solution)/shard_map/ppermute | solution.py:552
  14.8 4.9 %shard_map.47 = (bf16[4,4,64,576]{3,2,1,0:T(8,128)(2,1)}, bf16[2,2,256,768]{3,2,1,0:T(8,128)(2,1)S(1)}, bf16[2,2,256,768]{3,2,1,0:T(8,128)(2,1)S(1)}, bf16[2,2,2...) custom-call(bf16[4,4,64,576]{3,2,1,0:T(8,128)(2,1)S(1)} %get-tuple-e, ...), custom_call_target="tpu_custom_call" | custom-call | tf_op jit(solution)/shard_map/pallas_call | solution.py:584
  19.8 0.7 %collective-permute-done.6.c_low = bf16[4,64,128]{2,1,0:T(8,128)(2,1)S(1)} collective-permute-done((bf16[4,64,128]{2,1,0:T(8,128)(2,1)S(1)}, bf16[4,64,128]{2,1,0:T(8,128)(2,1)S(1)}, u32[]{:S(2)}, u32[]{:S(2)}) %collective-permute-start.6) | collective-permute-done | bytes 65568 | tf_op jit(solution)/shard_map/ppermute | solution.py:552
  20.5 0.0 collective-permute-done.2.x_low
  20.5 1.3 %collective-permute-done.5.x_high = bf16[14,64,128]{2,1,0:T(8,128)(2,1)S(1)} collective-permute-done((bf16[14,64,128]{2,1,0:T(8,128)(2,1)S(1)}, bf16[14,64,128]{2,1,0:T(8,128)(2,1)S(1)}, u32[]{:S(2)}, u32[]{:S(2)}) %collective-permute-start.5) | collective-permute-done | bytes 229408 | tf_op jit(solution)/shard_map/ppermute | solution.py:552
  21.9 2.6 %shard_map.48 = bf16[4,4,64,576]{3,2,1,0:T(8,128)(2,1)} custom-call(f32[4,2,4,768]{3,2,1,0:T(4,128)S(1)} %get-tuple-element.24.wide, bf16[13,64,128]{2,1,0:T(8,128)(2,1)S(1)} %collective-permute-done.y_low, bf16[13,64,128]{2,1,0:T(8,128)(2,1)S(1)} %collective-permute-done.1.y_high, ...), custom_call_target="tpu_custom_call", output_to_operand_aliasing={{}: (13, {})} | custom-call | tf_op jit(solution)/shard_map/pallas_call | solution.py:595
  (5 shorter events, 0.1 us)
Async XLA Ops:
  3.5 6.5 %collective-permute-start.3 = (bf16[4,64,128]{2,1,0:T(8,128)(2,1)S(1)}, bf16[4,64,128]{2,1,0:T(8,128)(2,1)S(1)}, u32[]{:S(2)}, u32[]{:S(2)}) collective-permute-start(bf16[4,64,128]{2,1,0:T(8,128)(2,1)S(1)} %get-tuple-element.29), channel_id=1, source_target_pairs={{0,1},{1,2},{2,3},{3,0},{4,5},{5,6},{6,7},{7,4},{8,9},{9,10},{10,1... | collective-permute-start | bytes 196616 | tf_op jit(solution)/shard_map/ppermute | solution.py:552
  4.0 6.0 %collective-permute-start.4 = (bf16[4,64,128]{2,1,0:T(8,128)(2,1)S(1)}, bf16[4,64,128]{2,1,0:T(8,128)(2,1)S(1)}, u32[]{:S(2)}, u32[]{:S(2)}) collective-permute-start(bf16[4,64,128]{2,1,0:T(8,128)(2,1)S(1)} %get-tuple-element.30), channel_id=1, source_target_pairs={{0,3},{1,0},{2,1},{3,2},{4,7},{5,4},{6,5},{7,6},{8,11},{9,8},{10,9... | collective-permute-start | bytes 196616 | tf_op jit(solution)/shard_map/ppermute | solution.py:552
  6.0 14.5 %collective-permute-start.2 = (bf16[10,64,128]{2,1,0:T(8,128)(2,1)S(1)}, bf16[10,64,128]{2,1,0:T(8,128)(2,1)S(1)}, u32[]{:S(2)}, u32[]{:S(2)}) collective-permute-start(bf16[10,64,128]{2,1,0:T(8,128)(2,1)S(1)} %get-tuple-element.27), channel_id=1, source_target_pairs={{0,4},{4,8},{8,12},{12,16},{16,20},{20,24},{24,28},{28,0},{1,5},{5... | collective-permute-start | bytes 491528 | tf_op jit(solution)/shard_map/ppermute | solution.py:552
  8.3 5.7 %collective-permute-start = (bf16[13,64,128]{2,1,0:T(8,128)(2,1)S(1)}, bf16[13,64,128]{2,1,0:T(8,128)(2,1)S(1)}, u32[]{:S(2)}, u32[]{:S(2)}) collective-permute-start(bf16[13,64,128]{2,1,0:T(8,128)(2,1)S(1)} %get-tuple-element.25), channel_id=1, source_target_pairs={{0,1},{1,2},{2,3},{3,0},{4,5},{5,6},{6,7},{7,4},{8,9},{9,10},{10,1... | collective-permute-start | bytes 638984 | tf_op jit(solution)/shard_map/ppermute | solution.py:552
  8.3 6.6 %collective-permute-start.1 = (bf16[13,64,128]{2,1,0:T(8,128)(2,1)S(1)}, bf16[13,64,128]{2,1,0:T(8,128)(2,1)S(1)}, u32[]{:S(2)}, u32[]{:S(2)}) collective-permute-start(bf16[13,64,128]{2,1,0:T(8,128)(2,1)S(1)} %get-tuple-element.26), channel_id=1, source_target_pairs={{0,3},{1,0},{2,1},{3,2},{4,7},{5,4},{6,5},{7,6},{8,11},{9,8},{10,9... | collective-permute-start | bytes 638984 | tf_op jit(solution)/shard_map/ppermute | solution.py:552
  10.1 11.8 %collective-permute-start.5 = (bf16[14,64,128]{2,1,0:T(8,128)(2,1)S(1)}, bf16[14,64,128]{2,1,0:T(8,128)(2,1)S(1)}, u32[]{:S(2)}, u32[]{:S(2)}) collective-permute-start(bf16[14,64,128]{2,1,0:T(8,128)(2,1)S(1)} %pad_maximum_fusion), channel_id=1, source_target_pairs={{0,28},{4,0},{8,4},{12,8},{16,12},{20,16},{24,20},{28,24},{1,29},{... | collective-permute-start | bytes 688136 | tf_op jit(solution)/shard_map/ppermute | solution.py:552
  13.4 7.1 %collective-permute-start.6 = (bf16[4,64,128]{2,1,0:T(8,128)(2,1)S(1)}, bf16[4,64,128]{2,1,0:T(8,128)(2,1)S(1)}, u32[]{:S(2)}, u32[]{:S(2)}) collective-permute-start(bf16[4,64,128]{2,1,0:T(8,128)(2,1)S(1)} %maximum_add_fusion.1), channel_id=1, source_target_pairs={{0,4},{4,8},{8,12},{12,16},{16,20},{20,24},{24,28},{28,0},{1,5},{5... | collective-permute-start | bytes 196616 | tf_op jit(solution)/shard_map/ppermute | solution.py:552

commit v6 on v5

--- a/solution.py
+++ b/solution.py
@@ -139,34 +139,7 @@
     return tiles
 
 
-def send_kernel(
-    ham, dens, pattern, kept, ends_up, ends_down, cy_up, cy_down, y_up, y_down, x_up, x_down, hm, dm, wide,
-    hb, db, pb, kb, live, keep, sems, mask_sems,
-):
-    masks = [
-        pltpu.make_async_copy(pattern, pb, mask_sems.at[0]),
-        pltpu.make_async_copy(kept, kb, mask_sems.at[1]),
-    ]
-    copies = {x: [] for x in (0, 3, 1, 2)}
-    for x in copies:
-        for n, (ref, buf) in enumerate(((ham, hb), (dens, db))):
-            copies[x].append(pltpu.make_async_copy(ref.at[x], buf.at[x], sems.at[n, x]))
-    for copy in masks + sum(copies.values(), []):
-        copy.start()
-    for copy in masks:
-        copy.wait()
-    for x in range(4):
-        live[x] = strip_mask(pb, x)
-        keep[x] = strip_mask(kb, x)
-
-    def arrive(x):
-        for copy in copies[x]:
-            copy.wait()
-        for y in range(4):
-            mask = live[x, y : y + 1, :].astype(BF)
-            hm[x, y] = hb[x, y] * mask
-            dm[x, y] = db[x, y] * mask
-
+def sender(hm, dm, keep):
     def lanes(dx, dy):
         k = 3 * (dx + 1) + dy + 1
         return slice(W * k, W * k + W)
@@ -244,6 +217,37 @@
         rows = jnp.concatenate([rows.astype(BF), jnp.zeros((48, W), BF)], axis=0)
         out[9] = pair(link(*cells[2], dx, dy), rows, even)
 
+    return get, flag, through, own, link, pair, packed, diagonal, put_line, selfs, upper, row, col
+
+
+def send_x_kernel(
+    ham, dens, pattern, kept, x_up, x_down, hm, dm, wide, keep, hb, db, pb, kb, live, sems, mask_sems,
+):
+    masks = [
+        pltpu.make_async_copy(pattern, pb, mask_sems.at[0]),
+        pltpu.make_async_copy(kept, kb, mask_sems.at[1]),
+    ]
+    copies = {x: [] for x in (0, 3, 1, 2)}
+    for x in copies:
+        for n, (ref, buf) in enumerate(((ham, hb), (dens, db))):
+            copies[x].append(pltpu.make_async_copy(ref.at[x], buf.at[x], sems.at[n, x]))
+    for copy in masks + sum(copies.values(), []):
+        copy.start()
+    for copy in masks:
+        copy.wait()
+    for x in range(4):
+        live[x] = strip_mask(pb, x)
+        keep[x] = strip_mask(kb, x)
+
+    def arrive(x):
+        for copy in copies[x]:
+            copy.wait()
+        for y in range(4):
+            mask = live[x, y : y + 1, :].astype(BF)
+            hm[x, y] = hb[x, y] * mask
+            dm[x, y] = db[x, y] * mask
+
+    _, flag, _, own, _, _, _, _, put_line, selfs, *_ = sender(hm, dm, keep)
     arrive(0)
     arrive(3)
     for x, out, dx in ((0, x_down, -1), (3, x_up, 1)):
@@ -252,8 +256,13 @@
         put_line(out, lambda i: (x, i), (0, 1), marks, 1)
     arrive(1)
     arrive(2)
-    for x in (1, 2):
-        selfs.update({(x, y): own(x, y) for y in (0, 3)})
+    for x in range(4):
+        wide[x, 0], wide[x, 1] = window_mask(kb, x)
+
+
+def send_y_kernel(hm, dm, keep, ends_up, ends_down, cy_up, cy_down, y_up, y_down):
+    get, flag, through, own, _, pair, packed, diagonal, put_line, selfs, upper, row, col = sender(hm, dm, keep)
+    selfs.update({(x, y): own(x, y) for x in range(4) for y in (0, 3)})
     ends_up[...] = jnp.zeros_like(ends_up)
     ends_down[...] = jnp.zeros_like(ends_down)
     for y, out, line, dy in ((3, cy_up, y_up, 1), (0, cy_down, y_down, -1)):
@@ -279,8 +288,6 @@
         put_line(out, lambda i: (i, y), (1, 0), marks, 0)
         for n, (x, dx) in enumerate(((0, -1), (3, 1))):
             out[10 + n] = pair(get(hm, x, y, dx, dy), get(dm, x, y, dx, dy))
-    for x in range(4):
-        wide[x, 0], wide[x, 1] = window_mask(kb, x)
 
 
 def halves(odd):
@@ -558,15 +565,18 @@
     mask = pltpu.VMEM(pattern.shape, pattern.dtype)
     flags = pltpu.VMEM((4, 4, 9 * W), F32)
     inputs = [pltpu.with_memory_space_constraint(v, pltpu.HBM) for v in (ham, dens, pattern, kept)]
-    ends_up, ends_down, cy_up, cy_down, y_up, y_down, x_up, x_down, ham, dens, wide = call(
-        send_kernel,
-        [corner] * 4 + [y_line, y_line, x_line, x_line, ham.shape, dens.shape]
-        + [jax.ShapeDtypeStruct((4, 2, 4, 12 * W), F32)],
-        [ham.shape, dens.shape, mask, mask, flags, flags]
+    keep = jax.ShapeDtypeStruct((4, 4, 9 * W), F32)
+    x_up, x_down, ham, dens, wide, keep = call(
+        send_x_kernel,
+        [x_line, x_line, ham.shape, dens.shape, jax.ShapeDtypeStruct((4, 2, 4, 12 * W), F32), keep],
+        [ham.shape, dens.shape, mask, mask, flags]
         + [pltpu.SemaphoreType.DMA((2, 4)), pltpu.SemaphoreType.DMA((2,))],
         [ANY] * 4,
         16,
     )(*inputs)
+    ends_up, ends_down, cy_up, cy_down, y_up, y_down = call(
+        send_y_kernel, [corner] * 4 + [y_line] * 2, [], [VMEM] * 3, 16
+    )(ham, dens, keep)
     cy_low = shift(cy_up, "gy", 1)
     cy_high = shift(cy_down, "gy", -1)
     y_low = shift(y_up, "gy", 1)

time: 24.6 us -> 24.1 us (0.980)
  the two profiles are of different devices: /device:TPU:0 before, /device:TPU:1 now
where the time goes in v6:
time: 24.1 us; the launch traced here: 23.9 us
  Pallas kernels  11.2 us (46%)
  starting transfers between devices  8.79 us (36%)
  waiting for transfers between devices  3.77 us (16%)
    ppermute x7, starting transfers between devices, shift(): lax.ppermute(value, axis, [(i, (i + step) % count) for i in range(count)])  8.79 us
    pallas_call x1, Pallas kernels, per_device(): call(middle_kernel, [ham.shape] + edges, [dense] * 3 + [(2, 4, 128, 768),...  4.94 us
    ppermute x7, waiting for transfers between devices, shift(): lax.ppermute(value, axis, [(i, (i + step) % count) for i in range(count)])  3.77 us
    pallas_call x1, Pallas kernels, per_device(): call(send_x_kernel, [x_line, x_line, ham.shape, dens.shape, jax.ShapeDtyp...  2.85 us
    pallas_call x1, Pallas kernels, per_device(): call(last_kernel, [ham.shape], [six] * 3 + [tile] * 2 + [(2, 2, 128, 256)...  2.56 us
    pallas_call x1, Pallas kernels, per_device(): call(send_y_kernel, [corner] * 4 + [y_line] * 2, [], [VMEM] * 3, 16)  0.88 us
  transfers between devices with their start and end apart: 7, of which 3 were waited for; matrix products, arithmetic and copies ran while one was open for 0% of the time, Pallas kernels for 21%

profile of v6, /device:TPU:1, one launch (start us, length us, event | category | flops | bytes accessed | tf_op | source)
XLA Modules:
  0.0 23.9 jit_solution(11992293052159698680)
XLA Ops:
  0.0 2.9 %shard_map.46 = (bf16[10,64,128]{2,1,0:T(8,128)(2,1)S(1)}, bf16[10,64,128]{2,1,0:T(8,128)(2,1)S(1)}, bf16[4,4,64,576]{3,2,1,0:T(8,128)(2,1)S(1)}, bf16[4,4,64,57...) custom-call(bf16[4,4,64,576]{3,2,1,0:T(8,128)(2,1)} %ham.1, ...), custom_call_target="tpu_custom_call" | custom-call | tf_op jit(solution)/shard_map/pallas_call | solution.py:569
  2.9 0.9 %shard_map.47 = (bf16[4,64,128]{2,1,0:T(8,128)(2,1)S(1)}, bf16[4,64,128]{2,1,0:T(8,128)(2,1)S(1)}, bf16[4,64,128]{2,1,0:T(8,128)(2,1)S(1)}, bf16[4,64,128]{2,1,0...) custom-call(bf16[4,4,64,576]{3,2,1,0:T(8,128)(2,1)S(1)} %get-tuple-element.26.hm.ham, ...), custom_call_target="tpu_custom_call" | custom-call | tf_op jit(solution)/shard_map/pallas_call | solution.py:577
  3.7 2.7 %collective-permute-start.3 = (bf16[4,64,128]{2,1,0:T(8,128)(2,1)S(1)}, bf16[4,64,128]{2,1,0:T(8,128)(2,1)S(1)}, u32[]{:S(2)}, u32[]{:S(2)}) collective-permute-start(bf16[4,64,128]{2,1,0:T(8,128)(2,1)S(1)} %get-tuple-element.33), channel_id=1, source_target_pairs={{0,1},{1,2},{2,3},{3,0},{4,5},{5,6},{6,7},{7,4},{8,9},{9,10},{10,1... | collective-permute-start | bytes 196616 | tf_op jit(solution)/shard_map/ppermute | solution.py:559
  6.4 1.2 %collective-permute-start.2 = (bf16[10,64,128]{2,1,0:T(8,128)(2,1)S(1)}, bf16[10,64,128]{2,1,0:T(8,128)(2,1)S(1)}, u32[]{:S(2)}, u32[]{:S(2)}) collective-permute-start(bf16[10,64,128]{2,1,0:T(8,128)(2,1)S(1)} %get-tuple-element.31), channel_id=1, source_target_pairs={{0,4},{4,8},{8,12},{12,16},{16,20},{20,24},{24,28},{28,0},{1,5},{5... | collective-permute-start | bytes 491528 | tf_op jit(solution)/shard_map/ppermute | solution.py:559
  7.6 0.0 collective-permute-start.4
  7.6 1.7 %collective-permute-start = (bf16[13,64,128]{2,1,0:T(8,128)(2,1)S(1)}, bf16[13,64,128]{2,1,0:T(8,128)(2,1)S(1)}, u32[]{:S(2)}, u32[]{:S(2)}) collective-permute-start(bf16[13,64,128]{2,1,0:T(8,128)(2,1)S(1)} %get-tuple-element.29), channel_id=1, source_target_pairs={{0,1},{1,2},{2,3},{3,0},{4,5},{5,6},{6,7},{7,4},{8,9},{9,10},{10,1... | collective-permute-start | bytes 638984 | tf_op jit(solution)/shard_map/ppermute | solution.py:559
  9.4 0.0 collective-permute-start.1
  9.4 0.0 collective-permute-done.3
  9.4 2.9 %collective-permute-done.4 = bf16[4,64,128]{2,1,0:T(8,128)(2,1)S(1)} collective-permute-done((bf16[4,64,128]{2,1,0:T(8,128)(2,1)S(1)}, bf16[4,64,128]{2,1,0:T(8,128)(2,1)S(1)}, u32[]{:S(2)}, u32[]{:S(2)}) %collective-permute-start.4) | collective-permute-done | bytes 65568 | tf_op jit(solution)/shard_map/ppermute | solution.py:559
  12.4 3.1 %collective-permute-start.5 = (bf16[14,64,128]{2,1,0:T(8,128)(2,1)S(1)}, bf16[14,64,128]{2,1,0:T(8,128)(2,1)S(1)}, u32[]{:S(2)}, u32[]{:S(2)}) collective-permute-start(bf16[14,64,128]{2,1,0:T(8,128)(2,1)S(1)} %pad_maximum_fusion), channel_id=1, source_target_pairs={{0,28},{4,0},{8,4},{12,8},{16,12},{20,16},{24,20},{28,24},{1,29},{... | collective-permute-start | bytes 688136 | tf_op jit(solution)/shard_map/ppermute | solution.py:559
  15.5 0.1 collective-permute-start.6
  15.6 0.0 collective-permute-done.y_low
  15.6 0.6 %collective-permute-done.1.y_high = bf16[13,64,128]{2,1,0:T(8,128)(2,1)S(1)} collective-permute-done((bf16[13,64,128]{2,1,0:T(8,128)(2,1)S(1)}, bf16[13,64,128]{2,1,0:T(8,128)(2,1)S(1)}, u32[]{:S(2)}, u32[]{:S(2)}) %collective-permute-start.1) | collective-permute-done | bytes 213024 | tf_op jit(solution)/shard_map/ppermute | solution.py:559
  16.2 4.9 %shard_map.48 = (bf16[4,4,64,576]{3,2,1,0:T(8,128)(2,1)}, bf16[2,2,256,768]{3,2,1,0:T(8,128)(2,1)S(1)}, bf16[2,2,256,768]{3,2,1,0:T(8,128)(2,1)S(1)}, bf16[2,2,2...) custom-call(bf16[4,4,64,576]{3,2,1,0:T(8,128)(2,1)S(1)} %get-tuple-e, ...), custom_call_target="tpu_custom_call" | custom-call | tf_op jit(solution)/shard_map/pallas_call | solution.py:594
  21.1 0.2 %collective-permute-done.6.c_low = bf16[4,64,128]{2,1,0:T(8,128)(2,1)S(1)} collective-permute-done((bf16[4,64,128]{2,1,0:T(8,128)(2,1)S(1)}, bf16[4,64,128]{2,1,0:T(8,128)(2,1)S(1)}, u32[]{:S(2)}, u32[]{:S(2)}) %collective-permute-start.6) | collective-permute-done | bytes 65568 | tf_op jit(solution)/shard_map/ppermute | solution.py:559
  21.4 0.0 collective-permute-done.2.x_low
  21.4 0.0 collective-permute-done.5.x_high
  21.4 2.6 %shard_map.49 = bf16[4,4,64,576]{3,2,1,0:T(8,128)(2,1)} custom-call(f32[4,2,4,768]{3,2,1,0:T(4,128)S(1)} %get-tuple-element.25.wide, bf16[13,64,128]{2,1,0:T(8,128)(2,1)S(1)} %collective-permute-done.y_low, bf16[13,64,128]{2,1,0:T(8,128)(2,1)S(1)} %collective-permute-done.1.y_high, ...), custom_call_target="tpu_custom_call", output_to_operand_aliasing={{}: (13, {})} | custom-call | tf_op jit(solution)/shard_map/pallas_call | solution.py:605
  (5 shorter events, 0.1 us)
Async XLA Ops:
  3.7 5.6 %collective-permute-start.3 = (bf16[4,64,128]{2,1,0:T(8,128)(2,1)S(1)}, bf16[4,64,128]{2,1,0:T(8,128)(2,1)S(1)}, u32[]{:S(2)}, u32[]{:S(2)}) collective-permute-start(bf16[4,64,128]{2,1,0:T(8,128)(2,1)S(1)} %get-tuple-element.33), channel_id=1, source_target_pairs={{0,1},{1,2},{2,3},{3,0},{4,5},{5,6},{6,7},{7,4},{8,9},{9,10},{10,1... | collective-permute-start | bytes 196616 | tf_op jit(solution)/shard_map/ppermute | solution.py:559
  6.4 15.0 %collective-permute-start.2 = (bf16[10,64,128]{2,1,0:T(8,128)(2,1)S(1)}, bf16[10,64,128]{2,1,0:T(8,128)(2,1)S(1)}, u32[]{:S(2)}, u32[]{:S(2)}) collective-permute-start(bf16[10,64,128]{2,1,0:T(8,128)(2,1)S(1)} %get-tuple-element.31), channel_id=1, source_target_pairs={{0,4},{4,8},{8,12},{12,16},{16,20},{20,24},{24,28},{28,0},{1,5},{5... | collective-permute-start | bytes 491528 | tf_op jit(solution)/shard_map/ppermute | solution.py:559
  7.6 4.7 %collective-permute-start.4 = (bf16[4,64,128]{2,1,0:T(8,128)(2,1)S(1)}, bf16[4,64,128]{2,1,0:T(8,128)(2,1)S(1)}, u32[]{:S(2)}, u32[]{:S(2)}) collective-permute-start(bf16[4,64,128]{2,1,0:T(8,128)(2,1)S(1)} %get-tuple-element.34), channel_id=1, source_target_pairs={{0,3},{1,0},{2,1},{3,2},{4,7},{5,4},{6,5},{7,6},{8,11},{9,8},{10,9... | collective-permute-start | bytes 196616 | tf_op jit(solution)/shard_map/ppermute | solution.py:559
  7.6 7.9 %collective-permute-start = (bf16[13,64,128]{2,1,0:T(8,128)(2,1)S(1)}, bf16[13,64,128]{2,1,0:T(8,128)(2,1)S(1)}, u32[]{:S(2)}, u32[]{:S(2)}) collective-permute-start(bf16[13,64,128]{2,1,0:T(8,128)(2,1)S(1)} %get-tuple-element.29), channel_id=1, source_target_pairs={{0,1},{1,2},{2,3},{3,0},{4,5},{5,6},{6,7},{7,4},{8,9},{9,10},{10,1... | collective-permute-start | bytes 638984 | tf_op jit(solution)/shard_map/ppermute | solution.py:559
  9.4 6.8 %collective-permute-start.1 = (bf16[13,64,128]{2,1,0:T(8,128)(2,1)S(1)}, bf16[13,64,128]{2,1,0:T(8,128)(2,1)S(1)}, u32[]{:S(2)}, u32[]{:S(2)}) collective-permute-start(bf16[13,64,128]{2,1,0:T(8,128)(2,1)S(1)} %get-tuple-element.30), channel_id=1, source_target_pairs={{0,3},{1,0},{2,1},{3,2},{4,7},{5,4},{6,5},{7,6},{8,11},{9,8},{10,9... | collective-permute-start | bytes 638984 | tf_op jit(solution)/shard_map/ppermute | solution.py:559
  12.4 9.0 %collective-permute-start.5 = (bf16[14,64,128]{2,1,0:T(8,128)(2,1)S(1)}, bf16[14,64,128]{2,1,0:T(8,128)(2,1)S(1)}, u32[]{:S(2)}, u32[]{:S(2)}) collective-permute-start(bf16[14,64,128]{2,1,0:T(8,128)(2,1)S(1)} %pad_maximum_fusion), channel_id=1, source_target_pairs={{0,28},{4,0},{8,4},{12,8},{16,12},{20,16},{24,20},{28,24},{1,29},{... | collective-permute-start | bytes 688136 | tf_op jit(solution)/shard_map/ppermute | solution.py:559
  15.5 5.9 %collective-permute-start.6 = (bf16[4,64,128]{2,1,0:T(8,128)(2,1)S(1)}, bf16[4,64,128]{2,1,0:T(8,128)(2,1)S(1)}, u32[]{:S(2)}, u32[]{:S(2)}) collective-permute-start(bf16[4,64,128]{2,1,0:T(8,128)(2,1)S(1)} %maximum_add_fusion.1), channel_id=1, source_target_pairs={{0,4},{4,8},{8,12},{12,16},{16,20},{20,24},{24,28},{28,0},{1,5},{5... | collective-permute-start | bytes 196616 | tf_op jit(solution)/shard_map/ppermute | solution.py:559

commit v7 on v6

--- a/solution.py
+++ b/solution.py
@@ -529,9 +529,9 @@
         unpack_rows((outer * mask[:, part(go)]).astype(BF), p, sx, go - 1, rows)
         unpack_rows((same * mask[:, part(1)]).astype(BF), p, sx, 0, rows)
         unpack_rows(done_edge[sx, p], p, sx, back - 1, rows)
-        if p == 1:
-            copies.append(pltpu.make_async_copy(rows.at[sx], out.at[x], sems.at[sx]))
-            copies[-1].start()
+        two = slice(2 * p, 2 * p + 2)
+        copies.append(pltpu.make_async_copy(rows.at[sx, two], out.at[x, two], sems.at[sx, p]))
+        copies[-1].start()
     for copy in copies:
         copy.wait()
 
@@ -607,7 +607,7 @@
         [ham.shape],
         [six] * 3
         + [tile] * 2
-        + [(2, 2, 128, 256), rows, pltpu.SemaphoreType.DMA((2,))],
+        + [(2, 2, 128, 256), rows, pltpu.SemaphoreType.DMA((2, 2))],
         [VMEM] * 13 + [ANY],
         32,
         [ANY],

time: 24.1 us -> 24 us (level)
  no operation moved by 1% of the time
where the time goes in v7:
time: 24 us; the launch traced here: 23.9 us
  Pallas kernels  11.2 us (47%)
  starting transfers between devices  8.79 us (37%)
  waiting for transfers between devices  3.77 us (16%)
    ppermute x7, starting transfers between devices, shift(): lax.ppermute(value, axis, [(i, (i + step) % count) for i in range(count)])  8.79 us
    pallas_call x1, Pallas kernels, per_device(): call(middle_kernel, [ham.shape] + edges, [dense] * 3 + [(2, 4, 128, 768),...  4.94 us
    ppermute x7, waiting for transfers between devices, shift(): lax.ppermute(value, axis, [(i, (i + step) % count) for i in range(count)])  3.77 us
    pallas_call x1, Pallas kernels, per_device(): call(send_x_kernel, [x_line, x_line, ham.shape, dens.shape, jax.ShapeDtyp...  2.85 us
    pallas_call x1, Pallas kernels, per_device(): call(last_kernel, [ham.shape], [six] * 3 + [tile] * 2 + [(2, 2, 128, 256)...  2.51 us
    pallas_call x1, Pallas kernels, per_device(): call(send_y_kernel, [corner] * 4 + [y_line] * 2, [], [VMEM] * 3, 16)  0.88 us
  transfers between devices with their start and end apart: 7, of which 3 were waited for; matrix products, arithmetic and copies ran while one was open for 0% of the time, Pallas kernels for 21%

profile of v7, /device:TPU:1, one launch (start us, length us, event | category | flops | bytes accessed | tf_op | source)
XLA Modules:
  0.0 23.9 jit_solution(10993545536405304048)
XLA Ops:
  0.0 2.9 %shard_map.46 = (bf16[10,64,128]{2,1,0:T(8,128)(2,1)S(1)}, bf16[10,64,128]{2,1,0:T(8,128)(2,1)S(1)}, bf16[4,4,64,576]{3,2,1,0:T(8,128)(2,1)S(1)}, bf16[4,4,64,57...) custom-call(bf16[4,4,64,576]{3,2,1,0:T(8,128)(2,1)} %ham.1, ...), custom_call_target="tpu_custom_call" | custom-call | tf_op jit(solution)/shard_map/pallas_call | solution.py:569
  2.9 0.9 %shard_map.47 = (bf16[4,64,128]{2,1,0:T(8,128)(2,1)S(1)}, bf16[4,64,128]{2,1,0:T(8,128)(2,1)S(1)}, bf16[4,64,128]{2,1,0:T(8,128)(2,1)S(1)}, bf16[4,64,128]{2,1,0...) custom-call(bf16[4,4,64,576]{3,2,1,0:T(8,128)(2,1)S(1)} %get-tuple-element.26.hm.ham, ...), custom_call_target="tpu_custom_call" | custom-call | tf_op jit(solution)/shard_map/pallas_call | solution.py:577
  3.7 2.7 %collective-permute-start.3 = (bf16[4,64,128]{2,1,0:T(8,128)(2,1)S(1)}, bf16[4,64,128]{2,1,0:T(8,128)(2,1)S(1)}, u32[]{:S(2)}, u32[]{:S(2)}) collective-permute-start(bf16[4,64,128]{2,1,0:T(8,128)(2,1)S(1)} %get-tuple-element.33), channel_id=1, source_target_pairs={{0,1},{1,2},{2,3},{3,0},{4,5},{5,6},{6,7},{7,4},{8,9},{9,10},{10,1... | collective-permute-start | bytes 196616 | tf_op jit(solution)/shard_map/ppermute | solution.py:559
  6.4 1.2 %collective-permute-start.2 = (bf16[10,64,128]{2,1,0:T(8,128)(2,1)S(1)}, bf16[10,64,128]{2,1,0:T(8,128)(2,1)S(1)}, u32[]{:S(2)}, u32[]{:S(2)}) collective-permute-start(bf16[10,64,128]{2,1,0:T(8,128)(2,1)S(1)} %get-tuple-element.31), channel_id=1, source_target_pairs={{0,4},{4,8},{8,12},{12,16},{16,20},{20,24},{24,28},{28,0},{1,5},{5... | collective-permute-start | bytes 491528 | tf_op jit(solution)/shard_map/ppermute | solution.py:559
  7.6 0.0 collective-permute-start.4
  7.6 1.7 %collective-permute-start = (bf16[13,64,128]{2,1,0:T(8,128)(2,1)S(1)}, bf16[13,64,128]{2,1,0:T(8,128)(2,1)S(1)}, u32[]{:S(2)}, u32[]{:S(2)}) collective-permute-start(bf16[13,64,128]{2,1,0:T(8,128)(2,1)S(1)} %get-tuple-element.29), channel_id=1, source_target_pairs={{0,1},{1,2},{2,3},{3,0},{4,5},{5,6},{6,7},{7,4},{8,9},{9,10},{10,1... | collective-permute-start | bytes 638984 | tf_op jit(solution)/shard_map/ppermute | solution.py:559
  9.4 0.0 collective-permute-start.1
  9.4 0.0 collective-permute-done.3
  9.4 2.9 %collective-permute-done.4 = bf16[4,64,128]{2,1,0:T(8,128)(2,1)S(1)} collective-permute-done((bf16[4,64,128]{2,1,0:T(8,128)(2,1)S(1)}, bf16[4,64,128]{2,1,0:T(8,128)(2,1)S(1)}, u32[]{:S(2)}, u32[]{:S(2)}) %collective-permute-start.4) | collective-permute-done | bytes 65568 | tf_op jit(solution)/shard_map/ppermute | solution.py:559
  12.4 3.1 %collective-permute-start.5 = (bf16[14,64,128]{2,1,0:T(8,128)(2,1)S(1)}, bf16[14,64,128]{2,1,0:T(8,128)(2,1)S(1)}, u32[]{:S(2)}, u32[]{:S(2)}) collective-permute-start(bf16[14,64,128]{2,1,0:T(8,128)(2,1)S(1)} %pad_maximum_fusion), channel_id=1, source_target_pairs={{0,28},{4,0},{8,4},{12,8},{16,12},{20,16},{24,20},{28,24},{1,29},{... | collective-permute-start | bytes 688136 | tf_op jit(solution)/shard_map/ppermute | solution.py:559
  15.5 0.1 collective-permute-start.6
  15.6 0.0 collective-permute-done.y_low
  15.6 0.6 %collective-permute-done.1.y_high = bf16[13,64,128]{2,1,0:T(8,128)(2,1)S(1)} collective-permute-done((bf16[13,64,128]{2,1,0:T(8,128)(2,1)S(1)}, bf16[13,64,128]{2,1,0:T(8,128)(2,1)S(1)}, u32[]{:S(2)}, u32[]{:S(2)}) %collective-permute-start.1) | collective-permute-done | bytes 213024 | tf_op jit(solution)/shard_map/ppermute | solution.py:559
  16.2 4.9 %shard_map.48 = (bf16[4,4,64,576]{3,2,1,0:T(8,128)(2,1)}, bf16[2,2,256,768]{3,2,1,0:T(8,128)(2,1)S(1)}, bf16[2,2,256,768]{3,2,1,0:T(8,128)(2,1)S(1)}, bf16[2,2,2...) custom-call(bf16[4,4,64,576]{3,2,1,0:T(8,128)(2,1)S(1)} %get-tuple-e, ...), custom_call_target="tpu_custom_call" | custom-call | tf_op jit(solution)/shard_map/pallas_call | solution.py:594
  21.1 0.2 %collective-permute-done.6.c_low = bf16[4,64,128]{2,1,0:T(8,128)(2,1)S(1)} collective-permute-done((bf16[4,64,128]{2,1,0:T(8,128)(2,1)S(1)}, bf16[4,64,128]{2,1,0:T(8,128)(2,1)S(1)}, u32[]{:S(2)}, u32[]{:S(2)}) %collective-permute-start.6) | collective-permute-done | bytes 65568 | tf_op jit(solution)/shard_map/ppermute | solution.py:559
  21.4 0.0 collective-permute-done.2.x_low
  21.4 0.0 collective-permute-done.5.x_high
  21.4 2.5 %shard_map.49 = bf16[4,4,64,576]{3,2,1,0:T(8,128)(2,1)} custom-call(f32[4,2,4,768]{3,2,1,0:T(4,128)S(1)} %get-tuple-element.25.wide, bf16[13,64,128]{2,1,0:T(8,128)(2,1)S(1)} %collective-permute-done.y_low, bf16[13,64,128]{2,1,0:T(8,128)(2,1)S(1)} %collective-permute-done.1.y_high, ...), custom_call_target="tpu_custom_call", output_to_operand_aliasing={{}: (13, {})} | custom-call | tf_op jit(solution)/shard_map/pallas_call | solution.py:605
  (5 shorter events, 0.1 us)
Async XLA Ops:
  3.7 5.6 %collective-permute-start.3 = (bf16[4,64,128]{2,1,0:T(8,128)(2,1)S(1)}, bf16[4,64,128]{2,1,0:T(8,128)(2,1)S(1)}, u32[]{:S(2)}, u32[]{:S(2)}) collective-permute-start(bf16[4,64,128]{2,1,0:T(8,128)(2,1)S(1)} %get-tuple-element.33), channel_id=1, source_target_pairs={{0,1},{1,2},{2,3},{3,0},{4,5},{5,6},{6,7},{7,4},{8,9},{9,10},{10,1... | collective-permute-start | bytes 196616 | tf_op jit(solution)/shard_map/ppermute | solution.py:559
  6.4 15.0 %collective-permute-start.2 = (bf16[10,64,128]{2,1,0:T(8,128)(2,1)S(1)}, bf16[10,64,128]{2,1,0:T(8,128)(2,1)S(1)}, u32[]{:S(2)}, u32[]{:S(2)}) collective-permute-start(bf16[10,64,128]{2,1,0:T(8,128)(2,1)S(1)} %get-tuple-element.31), channel_id=1, source_target_pairs={{0,4},{4,8},{8,12},{12,16},{16,20},{20,24},{24,28},{28,0},{1,5},{5... | collective-permute-start | bytes 491528 | tf_op jit(solution)/shard_map/ppermute | solution.py:559
  7.6 4.7 %collective-permute-start.4 = (bf16[4,64,128]{2,1,0:T(8,128)(2,1)S(1)}, bf16[4,64,128]{2,1,0:T(8,128)(2,1)S(1)}, u32[]{:S(2)}, u32[]{:S(2)}) collective-permute-start(bf16[4,64,128]{2,1,0:T(8,128)(2,1)S(1)} %get-tuple-element.34), channel_id=1, source_target_pairs={{0,3},{1,0},{2,1},{3,2},{4,7},{5,4},{6,5},{7,6},{8,11},{9,8},{10,9... | collective-permute-start | bytes 196616 | tf_op jit(solution)/shard_map/ppermute | solution.py:559
  7.6 7.9 %collective-permute-start = (bf16[13,64,128]{2,1,0:T(8,128)(2,1)S(1)}, bf16[13,64,128]{2,1,0:T(8,128)(2,1)S(1)}, u32[]{:S(2)}, u32[]{:S(2)}) collective-permute-start(bf16[13,64,128]{2,1,0:T(8,128)(2,1)S(1)} %get-tuple-element.29), channel_id=1, source_target_pairs={{0,1},{1,2},{2,3},{3,0},{4,5},{5,6},{6,7},{7,4},{8,9},{9,10},{10,1... | collective-permute-start | bytes 638984 | tf_op jit(solution)/shard_map/ppermute | solution.py:559
  9.4 6.8 %collective-permute-start.1 = (bf16[13,64,128]{2,1,0:T(8,128)(2,1)S(1)}, bf16[13,64,128]{2,1,0:T(8,128)(2,1)S(1)}, u32[]{:S(2)}, u32[]{:S(2)}) collective-permute-start(bf16[13,64,128]{2,1,0:T(8,128)(2,1)S(1)} %get-tuple-element.30), channel_id=1, source_target_pairs={{0,3},{1,0},{2,1},{3,2},{4,7},{5,4},{6,5},{7,6},{8,11},{9,8},{10,9... | collective-permute-start | bytes 638984 | tf_op jit(solution)/shard_map/ppermute | solution.py:559
  12.4 9.0 %collective-permute-start.5 = (bf16[14,64,128]{2,1,0:T(8,128)(2,1)S(1)}, bf16[14,64,128]{2,1,0:T(8,128)(2,1)S(1)}, u32[]{:S(2)}, u32[]{:S(2)}) collective-permute-start(bf16[14,64,128]{2,1,0:T(8,128)(2,1)S(1)} %pad_maximum_fusion), channel_id=1, source_target_pairs={{0,28},{4,0},{8,4},{12,8},{16,12},{20,16},{24,20},{28,24},{1,29},{... | collective-permute-start | bytes 688136 | tf_op jit(solution)/shard_map/ppermute | solution.py:559
  15.5 5.9 %collective-permute-start.6 = (bf16[4,64,128]{2,1,0:T(8,128)(2,1)S(1)}, bf16[4,64,128]{2,1,0:T(8,128)(2,1)S(1)}, u32[]{:S(2)}, u32[]{:S(2)}) collective-permute-start(bf16[4,64,128]{2,1,0:T(8,128)(2,1)S(1)} %maximum_add_fusion.1), channel_id=1, source_target_pairs={{0,4},{4,8},{8,12},{12,16},{16,20},{20,24},{24,28},{28,0},{1,5},{5... | collective-permute-start | bytes 196616 | tf_op jit(solution)/shard_map/ppermute | solution.py:559
